TPU v7x, 32 devices: a whole 2x2x4 slice. The times are simulated.
32 devices in a mesh: seq: 8 (over y, x, core), ch: 4 (over z).
Axes of the slice: x: 2, y: 2, z: 4, core: 2. Of those that a mesh axis runs over, the one named last changes fastest.
Arguments:
- grad_out: bfloat16 [1024, 8192], P('seq', 'ch'), may hold values from -6 to 6
- out_weight: bfloat16 [8192, 8192], P('ch'), may hold values from -0.0625 to 0.0625
- query_gate: bfloat16 [1024, 8192], P('seq', 'ch'), may hold values from -6 to 6
- key_branch: bfloat16 [1024, 8192], P('seq', 'ch'), may hold values from -6 to 6
- value_branch: bfloat16 [1024, 8192], P('seq', 'ch'), may hold values from -6 to 6
- filter_taps: bfloat16 [1024, 8192], P('seq', 'ch'), may hold values from -4 to 4
Outputs:
- key_grad: bfloat16 [1024, 8192], P('seq', 'ch')
- value_grad: bfloat16 [1024, 8192], P('seq', 'ch')
- filter_grad: float32 [1024, 8192], P('seq', 'ch')
All inputs are finite; a program needn't handle non-finite values.
Results may differ from a plain program's by a relative error of at most 0.017.
Values may be sent and summed in bfloat16 or wider, within the bound.
No kernel may reach another device: no remote copies, remote signals or barrier semaphores. Data moves between devices by JAX's collectives and lax.ppermute only.
A program may use at most 192 MiB of HBM per device.

v0:
```python
import math

import jax
import jax.numpy as jnp
from jax import lax
from jax.sharding import PartitionSpec as P


def build_tables(seg_len):
    twice_length = 2 * seg_len
    freq_index = jnp.arange(twice_length, dtype=jnp.int32)
    row_index = jnp.arange(seg_len, dtype=jnp.int32)
    angle_unit = 2.0 * math.pi / twice_length
    fwd_phase = (freq_index[:, None] * row_index[None, :] % twice_length).astype(
        jnp.float32
    ) * angle_unit
    back_phase = (freq_index[None, :] * (seg_len - row_index[:, None]) % twice_length).astype(
        jnp.float32
    ) * angle_unit
    window_pos = (freq_index + seg_len) % twice_length
    window_phase = (freq_index[None, :] * window_pos[:, None] % twice_length).astype(
        jnp.float32
    ) * angle_unit
    parity = jnp.where(freq_index % 2 == 0, 1.0, -1.0).astype(jnp.float32)[:, None]
    return (
        jnp.cos(fwd_phase).astype(jnp.bfloat16),
        jnp.sin(fwd_phase).astype(jnp.bfloat16),
        jnp.cos(back_phase).astype(jnp.bfloat16),
        jnp.sin(back_phase).astype(jnp.bfloat16),
        jnp.cos(window_phase).astype(jnp.bfloat16),
        jnp.sin(window_phase).astype(jnp.bfloat16),
        parity,
    )


def spectra(block_list, cosine_forward, sine_forward):
    cosine_piece = jnp.einsum(
        "qk,rkb->rqb", cosine_forward, block_list, preferred_element_type=jnp.float32
    )
    sine_piece = jnp.einsum(
        "qk,rkb->rqb", sine_forward, block_list, preferred_element_type=jnp.float32
    )
    return (cosine_piece, sine_piece)


def shards(grad_out, out_weight, query_gate, key_branch, value_branch, filter_taps):
    seg_len = query_gate.shape[0]
    channels = query_gate.shape[1]
    twice_length = 2 * seg_len
    segments = lax.axis_size("seq")
    my_index = lax.axis_index("seq")
    factor = 1.0 / math.sqrt(seg_len * segments)
    grad_mix = lax.dot_general(
        lax.all_gather(grad_out, "ch", axis=1, tiled=True),
        out_weight,
        (((1,), (1,)), ((), ())),
        preferred_element_type=jnp.float32,
    )
    gated_grad = (grad_mix * query_gate.astype(jnp.float32)).astype(jnp.bfloat16)
    conv_input = (key_branch.astype(jnp.float32) * value_branch.astype(jnp.float32)).astype(
        jnp.bfloat16
    )
    tables = build_tables(seg_len)
    (
        cosine_forward,
        sine_forward,
        cosine_backward,
        sine_backward,
        cosine_window,
        sine_window,
        parity,
    ) = tables
    all_taps = lax.all_gather(filter_taps, "seq", axis=0, tiled=True)
    tap_cos, tap_sin = spectra(
        all_taps.reshape(segments, seg_len, channels), cosine_forward, sine_forward
    )
    kern_cos = jnp.concatenate([jnp.zeros_like(tap_cos[:1]), tap_cos[:-1]], 0) + parity * tap_cos
    kern_sin = jnp.concatenate([jnp.zeros_like(tap_sin[:1]), tap_sin[:-1]], 0) + parity * tap_sin
    own_cos, own_sin = spectra(conv_input[None], cosine_forward, sine_forward)
    own_cos = own_cos[0]
    own_sin = own_sin[0]
    zero_spec = jnp.zeros((twice_length, channels), jnp.float32)
    initial = (zero_spec, zero_spec, jnp.zeros(((segments + 1) * seg_len, channels), jnp.float32))
    piece_data = lax.all_gather(gated_grad, "seq", axis=0, tiled=True)
    block_count = piece_data.shape[0] // seg_len
    seg_ids = jnp.arange(block_count, dtype=jnp.int32)
    block_list = piece_data.reshape(block_count, seg_len, channels)
    grad_cos, grad_sin = spectra(block_list, cosine_forward, sine_forward)
    lag_steps = seg_ids - my_index
    inside = seg_ids < segments
    live_mask = ((lag_steps >= 0) & inside).astype(jnp.float32)[:, None, None]
    lag_clip = jnp.clip(lag_steps, 0, segments - 1)
    lag_kcos = jnp.take(kern_cos, lag_clip, axis=0)
    lag_ksin = jnp.take(kern_sin, lag_clip, axis=0)
    running_real = jnp.sum(live_mask * (grad_cos * lag_kcos + grad_sin * lag_ksin), axis=0)
    running_imaginary = jnp.sum(live_mask * (grad_sin * lag_kcos - grad_cos * lag_ksin), axis=0)
    product_real = (own_cos * grad_cos + own_sin * grad_sin).astype(jnp.bfloat16)
    product_imaginary = (own_sin * grad_cos - own_cos * grad_sin).astype(jnp.bfloat16)
    windows = jnp.einsum(
        "an,hny->hay", cosine_window, product_real, preferred_element_type=jnp.float32
    ) - jnp.einsum(
        "an,hny->hay", sine_window, product_imaginary, preferred_element_type=jnp.float32
    )
    windows = windows * (live_mask / twice_length)

    def place(item_index, buffer):
        offset = lag_clip[item_index] * seg_len
        current = lax.dynamic_slice_in_dim(buffer, offset, twice_length, 0)
        return lax.dynamic_update_slice_in_dim(buffer, current + windows[item_index], offset, 0)

    buffer = lax.fori_loop(0, block_list.shape[0], place, initial[2])
    convolution_gradient = (
        jnp.dot(
            cosine_backward, running_real.astype(jnp.bfloat16), preferred_element_type=jnp.float32
        )
        - jnp.dot(
            sine_backward,
            running_imaginary.astype(jnp.bfloat16),
            preferred_element_type=jnp.float32,
        )
    ) / twice_length
    own_rows = lax.psum_scatter(
        buffer[seg_len:].astype(jnp.bfloat16), "seq", scatter_dimension=0, tiled=True
    ).astype(jnp.float32)
    filter_grad = own_rows * factor
    key_grad = (convolution_gradient * value_branch.astype(jnp.float32)).astype(jnp.bfloat16)
    value_grad = (convolution_gradient * key_branch.astype(jnp.float32)).astype(jnp.bfloat16)
    return (key_grad, value_grad, filter_grad)


def solution(mesh):
    return jax.shard_map(
        shards,
        mesh=mesh,
        in_specs=(
            P("seq", "ch"),
            P("ch", None),
            P("seq", "ch"),
            P("seq", "ch"),
            P("seq", "ch"),
            P("seq", "ch"),
        ),
        out_specs=(P("seq", "ch"), P("seq", "ch"), P("seq", "ch")),
        check_vma=False,
    )
```

profile of v0, /device:TPU:0, one launch (start us, length us, event | category | flops | bytes accessed | tf_op | source)
XLA Modules:
  0.0 464.2 jit_solution(15966368828542519154)
XLA Ops:
  8.7 49.5 %all-gather.4.cloned.1.call-done = bf16[128,8192]{1,0:T(8,128)(2,1)} async-done(((bf16[128,2048]{1,0:T(8,128)(2,1)}), bf16[128,8192]{1,0:T(8,128)(2,1)}) %all-gather.4.cloned.1.call-update) | async-done | bytes 2097168 | tf_op jit(solution)/shard_map/all_gather | solution.py:54
  58.2 17.4 %fusion.22 = bf16[128,2048]{1,0:T(8,128)(2,1)} fusion(bf16[128,8192]{1,0:T(8,128)(2,1)} %all-gather.4.cloned.1.call-done, bf16[2048,8192]{1,0:T(8,128)(2,1)} %param.11, bf16[128,2048]{1,0:T(8,128)(2,1)} %param.12), kind=kOutput, calls=%fused_computation.40 | convolution fusion | flops 4295753728 | bytes 36700160 | tf_op jit(solution)/shard_map/dot_general | solution.py:53
  79.5 16.1 %all-gather.8.cloned.1.call-done = bf16[1024,2048]{1,0:T(8,128)(2,1)} async-done(((bf16[128,2048]{1,0:T(8,128)(2,1)}), bf16[1024,2048]{1,0:T(8,128)(2,1)}) %all-gather.8.cloned.1.call-update) | async-done | bytes 4194320 | tf_op jit(solution)/shard_map/all_gather | solution.py:73
  95.6 11.0 %convolution_bitcast_fusion.1 = f32[8,256,2048]{2,1,0:T(8,128)} fusion(bf16[8,128,2048]{2,1,0:T(8,128)(2,1)} %bitcast.103), kind=kOutput, calls=%fused_computation.34 | convolution fusion | flops 1074233344 | bytes 20971520 | tf_op jit(solution)/shard_map/qk,rkb->rqb/dot_general | solution.py:37
  106.6 13.2 %slice.17 = f32[7,256,2048]{2,1,0:T(8,128)} slice(f32[8,256,2048]{2,1,0:T(8,128)} %convolution_bitcast_fusion.1), slice={[0:7], [0:256], [0:2048]} | slice | bytes 29360128 | tf_op jit(solution)/shard_map/slice | solution.py:77
  119.8 11.0 %convolution_bitcast_fusion = f32[8,256,2048]{2,1,0:T(8,128)} fusion(bf16[8,128,2048]{2,1,0:T(8,128)(2,1)} %bitcast.104), kind=kOutput, calls=%fused_computation.33 | convolution fusion | flops 1074233344 | bytes 20971520 | tf_op jit(solution)/shard_map/qk,rkb->rqb/dot_general | solution.py:40
  130.8 13.2 %slice.18 = f32[7,256,2048]{2,1,0:T(8,128)} slice(f32[8,256,2048]{2,1,0:T(8,128)} %convolution_bitcast_fusion), slice={[0:7], [0:256], [0:2048]} | slice | bytes 29360128 | tf_op jit(solution)/shard_map/slice | solution.py:78
  143.9 32.3 %multiply_add_fusion.1 = (f32[8,256,2048]{2,1,0:T(8,128)}, f32[8,256,2048]{2,1,0:T(8,128)}) fusion(f32[8,256,2048]{2,1,0:T(8,128)} %convolution_bitcast_fusion.1, f32[7,256,2048]{2,1,0:T(8,128)} %slice.17, f32[256]{0:T(256)S(1)} %compare_select_fusion.3, f32[8,256,2048]{2,1,0:T(8,128)} %convolution_bitcast_fusion, f32[7,256,2048]{2,1,0:T(8,128)} %slice.18), kind=kLoop, calls=%fused_computation.25 | loop fusion | flops 16777216 | bytes 96470016 | tf_op jit(solution)/shard_map/add | solution.py:77
  176.2 13.8 %gather_fusion = f32[8,256,2048]{2,1,0:T(8,128)} fusion(f32[8,256,2048]{2,1,0:T(8,128)} %get-tuple-element.108, s32[1024]{0:T(1024)S(1)} %pad_clamp_fusion), kind=kCustom, calls=%fused_computation.clone | custom fusion | bytes 33554464 | tf_op jit(solution)/shard_map/jit(_take)/gather | solution.py:93
  190.0 16.4 %copy.18 = f32[8,256,2048]{1,2,0:T(8,128)} copy(f32[8,256,2048]{2,1,0:T(8,128)} %gather_fusion) | data formatting | bytes 33554432 | tf_op jit(solution)/shard_map/jit(_take)/gather | solution.py:93
  206.4 13.8 %gather_fusion.1 = f32[8,256,2048]{2,1,0:T(8,128)} fusion(f32[8,256,2048]{2,1,0:T(8,128)} %get-tuple-element.109, s32[1024]{0:T(1024)S(1)} %pad_clamp_fusion), kind=kCustom, calls=%fused_computation.1.clone | custom fusion | bytes 33554464 | tf_op jit(solution)/shard_map/jit(_take)/gather | solution.py:94
  220.2 16.4 %copy.20 = f32[8,256,2048]{1,2,0:T(8,128)} copy(f32[8,256,2048]{2,1,0:T(8,128)} %gather_fusion.1) | data formatting | bytes 33554432 | tf_op jit(solution)/shard_map/jit(_take)/gather | solution.py:94
  236.6 10.9 %fusion.59 = f32[8,2048,256]{2,1,0:T(8,128)} fusion(bf16[8,128,2048]{2,1,0:T(8,128)(2,1)} %bitcast.101), kind=kOutput, calls=%fused_computation.90 | convolution fusion | flops 1074233344 | bytes 20971520 | tf_op jit(solution)/shard_map/qk,rkb->rqb/dot_general | solution.py:37
  247.5 25.4 %fusion.6 = (bf16[256,2048]{0,1:T(8,128)(2,1)}, bf16[256,2048]{0,1:T(8,128)(2,1)}, f32[8,2048,256]{2,1,0:T(8,128)}) fusion(f32[8,2048,256]{2,1,0:T(8,128)} %fusion.59, f32[8,256,2048]{1,2,0:T(8,128)} %copy.20, f32[8,256,2048]{1,2,0:T(8,128)} %copy.18, f32[8]{0:T(128)S(1)} %get-tuple-element.114, pred[8]{0:T(512)(128)(4,1)S(1)} %get-tuple-element.113, ...), kind=kOutput, calls=%fused_computation.14 | convolution fusion | flops 1123516416 | bytes 73400360 | tf_op jit(solution)/shard_map/qk,rkb->rqb/dot_general | solution.py:40
  273.0 19.7 %fusion.11 = f32[8,2048,256]{2,1,0:T(8,128)} fusion(f32[8,2048,256]{2,1,0:T(8,128)} %get-tuple-element.110, f32[8,2048,256]{2,1,0:T(8,128)} %fusion.59, f32[256,2048]{0,1:T(8,128)S(1)} %convolution_bitcast_fusion.2, f32[256,2048]{0,1:T(8,128)} %convolution_bitcast_fusion.3, s32[256]{0:T(256)S(1)} %and_select_fusion), kind=kOutput, calls=%fused_computation.26 | convolution fusion | flops 2165243904 | bytes 54526976 | tf_op jit(solution)/shard_map/an,hny->hay/dot_general | solution.py:101
  292.7 25.1 %multiply_bitcast_fusion = f32[8,256,2048]{1,2,0:T(8,128)} fusion(f32[8,2048,256]{2,1,0:T(8,128)} %fusion.11, f32[8]{0:T(128)S(1)} %broadcast_select_fusion, f32[8,2048,256]{2,1,0:T(8,128)} %get-tuple-element.110, f32[8,2048,256]{2,1,0:T(8,128)} %fusion.59, f32[256,2048]{0,1:T(8,128)S(1)} %convolution_bitcast_fusion.2, ...), kind=kOutput, calls=%fused_computation.23 | convolution fusion | flops 2173632512 | bytes 71304224 | tf_op jit(solution)/shard_map/an,hny->hay/dot_general | solution.py:99
  317.8 4.8 %broadcast_in_dim.30 = f32[1152,2048]{1,0:T(8,128)} broadcast(f32[]{:T(128)} %constant.124.clone.1), dimensions={} | broadcast | bytes 9437188 | tf_op jit(solution)/shard_map/broadcast_in_dim | solution.py:83
  322.6 75.3 %while.13 = (s32[]{:T(128)}, f32[1152,2048]{1,0:T(8,128)}, s32[8]{0:T(128)S(1)}, f32[8,256,2048]{1,2,0:T(8,128)}, s32[]{:T(128)}, /*index=5*/s32[1]{0:T(128)}, s32[]{:T(128)}, s32[]{:T(128)}) while((s32[]{:T(128)}, f32[1152,2048]{1,0:T(8,128)}, s32[8]{0:T(128)S(1)}, f32[8,256,2048]{1,2,0:T(8,128)}, s32[]{:T(128)}, /*index=5*/s32[1]{0:T(128)}, ...), condition=%wide.region_3.5_spmd, body=%wide.region_2.4_spmd.sunk | while | flops 524294 | bytes 14680215 | solution.py:111
  323.8 3.0 constant_dynamic-slice_fusion.2
  328.8 3.2 fusion.115
  333.2 3.0 constant_dynamic-slice_fusion.2
  338.2 3.2 fusion.115
  347.6 3.2 fusion.115
  352.1 3.0 constant_dynamic-slice_fusion.2
  357.1 3.2 fusion.115
  366.5 3.2 fusion.115
  375.9 3.2 fusion.115
  385.4 3.2 fusion.115
  394.7 3.2 fusion.115
  397.9 6.0 %slice.21 = bf16[1024,2048]{1,0:T(8,128)(2,1)} slice(f32[1152,2048]{1,0:T(8,128)} %get-tuple-element.83), slice={[128:1152], [0:2048]} | slice | bytes 8388608 | tf_op jit(solution)/shard_map/slice | solution.py:123
  406.1 3.2 fusion.24
  409.3 46.2 %reduce-scatter.2.cloned.1.call-done = bf16[128,2048]{1,0:T(8,128)(2,1)} async-done(((bf16[1024,2048]{1,0:T(8,128)(2,1)}), bf16[128,2048]{1,0:T(8,128)(2,1)}) %reduce-scatter.2.cloned.1.call-update) | async-done | bytes 524304 | tf_op jit(solution)/shard_map/reduce_scatter | solution.py:122
  (53 shorter events, 44.9 us)
Async XLA Ops:
  7.2 51.1 %all-gather.4.cloned.1.call-start = ((), (), s32[]{:S(2)}) async-start(), calls=%async_computation.1 | async-start | bytes 2621440 | tf_op jit(solution)/shard_map/all_gather | solution.py:54
  7.9 87.7 %all-gather.8.cloned.1.call-start = ((), (), s32[]{:S(2)}) async-start(), calls=%async_computation.3 | async-start | bytes 4718592 | tf_op jit(solution)/shard_map/all_gather | solution.py:73
  8.6 67.6 %copy-start.1 = (bf16[128,2048]{1,0:T(8,128)(2,1)S(1)}, bf16[128,2048]{1,0:T(8,128)(2,1)}, u32[]{:S(2)}) copy-start(bf16[128,2048]{1,0:T(8,128)(2,1)} %param.13) | copy-start | bytes 1572868
  8.7 67.6 %copy-start.3 = (bf16[128,2048]{1,0:T(8,128)(2,1)S(1)}, bf16[128,2048]{1,0:T(8,128)(2,1)}, u32[]{:S(2)}) copy-start(bf16[128,2048]{1,0:T(8,128)(2,1)} %param.14) | copy-start | bytes 1572868
  8.7 227.9 %all-gather.6.cloned.1.call-start = ((), (), s32[]{:S(2)}) async-start(), calls=%async_computation.2 | async-start | bytes 4718592 | tf_op jit(solution)/shard_map/all_gather | solution.py:84
  75.6 379.9 %reduce-scatter.2.cloned.1.call-start = ((), (), s32[]{:S(2)}) async-start(), calls=%async_computation.4 | async-start | bytes 4718592 | tf_op jit(solution)/shard_map/reduce_scatter | solution.py:122
  236.6 10.9 %copy-start = (bf16[1024,2048]{1,0:T(8,128)(2,1)S(1)}, bf16[1024,2048]{1,0:T(8,128)(2,1)}, u32[]{:S(2)}) copy-start(bf16[1024,2048]{1,0:T(8,128)(2,1)} %all-gather.6.cloned.1.call-done) | copy-start | bytes 12582916
  292.7 29.9 %copy-start.5 = (s32[8]{0:T(128)S(1)}, s32[8]{0:T(128)}, u32[]{:S(2)}) copy-start(s32[8]{0:T(128)} %get-tuple-element.142) | copy-start | bytes 100
  322.6 83.5 %copy-start.2 = (bf16[128,2048]{1,0:T(8,128)(2,1)S(1)}, bf16[128,2048]{1,0:T(8,128)(2,1)}, u32[]{:S(2)}) copy-start(bf16[128,2048]{1,0:T(8,128)(2,1)} %param.13) | copy-start | bytes 1572868
  322.6 83.6 %copy-start.4 = (bf16[128,2048]{1,0:T(8,128)(2,1)S(1)}, bf16[128,2048]{1,0:T(8,128)(2,1)}, u32[]{:S(2)}) copy-start(bf16[128,2048]{1,0:T(8,128)(2,1)} %param.14) | copy-start | bytes 1572868
Sparse Core Ops, SparseCore 0:
  9.6 48.6 all-gather.3
  60.1 35.4 all-gather.7
  98.1 36.7 all-gather.5
  404.1 51.4 reduce-scatter.1
where the time goes:
time: 466 us; the launch traced here: 464 us
  local copies, waits for them, and re-layouts  142 us (30%)
  matrix products  129 us (28%)
  waiting for transfers between devices  113 us (24%)
  other arithmetic  60.5 us (13%)
  between operations  13.9 us (3%)
  loops' own time  5.33 us (1%)
    all_gather x1, waiting for transfers between devices, shards(): lax.all_gather(grad_out, 'ch', axis=1, tiled=True)  49.5 us
    reduce_scatter x1, waiting for transfers between devices, shards(): lax.psum_scatter(buffer[seg_len:].astype(jnp.bfloat16), 'seq', scatter_di...  46.2 us
    dynamic_slice x16, local copies, waits for them, and re-layouts, place(): windows[item_index]  39.8 us
    dot_general x3, matrix products, spectra(): jnp.einsum('qk,rkb->rqb', sine_forward, block_list, preferred_element_typ...  37.4 us
    add x1, other arithmetic, shards(): jnp.concatenate([jnp.zeros_like(tap_cos[:1]), tap_cos[:-1]], 0)  32.3 us
    gather x2, local copies, waits for them, and re-layouts, shards(): lag_ksin = jnp.take(kern_sin, lag_clip, axis=0)  30.2 us
    gather x2, local copies, waits for them, and re-layouts, shards(): lag_kcos = jnp.take(kern_cos, lag_clip, axis=0)  30.2 us
    dynamic_update_slice x8, other arithmetic, place(): lax.dynamic_update_slice_in_dim(buffer, current + windows[item_index], of...  25.6 us
  transfers between devices with their start and end apart: 4, of which 3 were waited for; matrix products, arithmetic and copies ran while one was open for 36% of the time, Pallas kernels for 0%

commit v1 on v0

--- a/solution.py
+++ b/solution.py
@@ -1,9 +1,17 @@
+import functools
 import math
 
 import jax
 import jax.numpy as jnp
+import ml_dtypes
+import numpy as np
 from jax import lax
+from jax.experimental import pallas as pl
+from jax.experimental.pallas import tpu as pltpu
 from jax.sharding import PartitionSpec as P
+
+LANES = 128
+CHUNKS = 2
 
 
 def build_tables(seg_len):
@@ -128,9 +136,352 @@
     return (key_grad, value_grad, filter_grad)
 
 
+def half_tables(rows):
+    size = 2 * rows
+    freq = np.arange(rows)
+    pos = np.arange(rows)
+    angle = 2.0 * np.pi * (np.outer(freq, pos) % size) / size
+    sine = np.sin(angle)
+    sine[0] = (-1.0) ** pos
+    forward = np.concatenate([np.cos(angle), sine], 0)
+    angle = 2.0 * np.pi * (np.outer(rows - pos, freq) % size) / size
+    cos_back = 2.0 * np.cos(angle)
+    sin_back = -2.0 * np.sin(angle)
+    cos_back[:, 0] = 1.0
+    sin_back[:, 0] = (-1.0) ** (rows - pos)
+    back = np.concatenate([cos_back, sin_back], 1) / size
+    return forward.astype(ml_dtypes.bfloat16), back.astype(ml_dtypes.bfloat16)
+
+
+def whole(shape):
+    return pl.BlockSpec(shape, lambda *_: (0,) * len(shape))
+
+
+def params(mib=48):
+    return pltpu.CompilerParams(vmem_limit_bytes=mib * 2**20)
+
+
+def pack_kernel(ids, key, value, taps, *outs):
+    step = pl.program_id(0)
+    conv_input = (key[...].astype(jnp.float32) * value[...].astype(jnp.float32)).astype(jnp.bfloat16)
+    for k, out in enumerate(outs):
+
+        @pl.when(step == k)
+        def _():
+            out[0] = taps[...]
+            out[1] = conv_input
+
+
+def pack(ids, key, value, taps, n):
+    rows, channels = key.shape
+    width = channels // n
+    column = pl.BlockSpec((rows, width), lambda k, ids: (0, ids[0] ^ k))
+    return pl.pallas_call(
+        pack_kernel,
+        grid_spec=pltpu.PrefetchScalarGridSpec(
+            num_scalar_prefetch=1,
+            grid=(n,),
+            in_specs=[column] * 3,
+            out_specs=[whole((2, rows, width))] * n,
+        ),
+        out_shape=[jax.ShapeDtypeStruct((2, rows, width), jnp.bfloat16)] * n,
+        compiler_params=params(),
+        name="pack_taps_input",
+    )(ids, key, value, taps)
+
+
+def contract(x, w):
+    return lax.dot_general(x, w, (((1,), (1,)), ((), ())), preferred_element_type=jnp.float32)
+
+
+def choose(ids, pair):
+    if len(pair) == 1:
+        return pair[0][...]
+    return jnp.where(ids[2] == 1, pair[0][...], pair[1][...])
+
+
+def mix_kernel(parts, per_part, has_total, ids, *refs):
+    xs = refs[: parts * per_part]
+    w, *rest = refs[parts * per_part :]
+    total, out = rest if has_total else (None, rest[0])
+    rows = xs[0].shape[0]
+    for c in range(parts):
+        block = contract(choose(ids, xs[c * per_part : (c + 1) * per_part]), w[...])
+        if has_total:
+            block += total[c * rows : (c + 1) * rows]
+        out[c * rows : (c + 1) * rows] = block
+
+
+def mix(ids, where, parts, weight, total, n):
+    channels = weight.shape[0]
+    depth = parts[0][0].shape[1]
+    rows = sum(p[0].shape[0] for p in parts)
+    width = channels // n
+    flat = [x for p in parts for x in p]
+    column = pl.BlockSpec((rows, width), lambda k, ids: (0, k))
+    return pl.pallas_call(
+        functools.partial(mix_kernel, len(parts), len(parts[0]), total is not None),
+        grid_spec=pltpu.PrefetchScalarGridSpec(
+            num_scalar_prefetch=1,
+            grid=(n,),
+            in_specs=[whole(x.shape) for x in flat]
+            + [pl.BlockSpec((width, depth), lambda k, ids: (k, ids[where]))]
+            + ([column] if total is not None else []),
+            out_specs=column,
+        ),
+        out_shape=jax.ShapeDtypeStruct((rows, channels), jnp.float32),
+        compiler_params=params(),
+        name="mix",
+    )(ids, *flat, weight, *([total] if total is not None else []))
+
+
+def gate_kernel(per_part, ids, *refs):
+    xs = refs[:per_part]
+    w, total, gate, *outs = refs[per_part:]
+    step = pl.program_id(0)
+    mixed = total[...] + contract(choose(ids, xs), w[...])
+    gated = (mixed * gate[...].astype(jnp.float32)).astype(jnp.bfloat16)
+    for k, out in enumerate(outs):
+
+        @pl.when(step == k)
+        def _():
+            out[...] = gated
+
+
+def mix_gate(ids, where, pair, weight, total, gate, chunk, n):
+    channels = weight.shape[0]
+    rows, depth = pair[0].shape
+    width = channels // n
+    column = pl.BlockSpec((rows, width), lambda k, ids: (chunk, ids[0] ^ k))
+    return pl.pallas_call(
+        functools.partial(gate_kernel, len(pair)),
+        grid_spec=pltpu.PrefetchScalarGridSpec(
+            num_scalar_prefetch=1,
+            grid=(n,),
+            in_specs=[whole(x.shape) for x in pair]
+            + [pl.BlockSpec((width, depth), lambda k, ids: (ids[0] ^ k, ids[where])), column, column],
+            out_specs=[whole((rows, width))] * n,
+        ),
+        out_shape=[jax.ShapeDtypeStruct((rows, width), jnp.bfloat16)] * n,
+        compiler_params=params(),
+        name="mix_gate",
+    )(ids, *pair, weight, total, gate)
+
+
+def tap_kernel(n, ids, forward, *refs):
+    pieces = refs[:n]
+    out, data, spec = refs[n:]
+    rows = pieces[0].shape[1]
+    seg = forward.shape[1]
+    for k in range(n):
+        at = pl.multiple_of((ids[0] ^ k) * rows, rows)
+        data[:, pl.ds(at, rows)] = pieces[k][...]
+    row = lax.broadcasted_iota(jnp.int32, (2 * seg, data.shape[2]), 0)
+    sign = jnp.where(row % 2 == 0, 1.0, -1.0)
+    for x in range(2):
+        for r in range(n * rows // seg):
+            now = jnp.dot(forward[...], data[x, r * seg : (r + 1) * seg], preferred_element_type=jnp.float32)
+            kern = sign * now
+            if r:
+                kern += spec[...]
+            spec[...] = now
+            out[x, r] = kern.astype(jnp.bfloat16)
+
+
+def tap_kernels(ids, forward, pieces):
+    n = len(pieces)
+    _, rows, width = pieces[0].shape
+    seg = forward.shape[1]
+    shape = (2, n * rows // seg, 2 * seg, width)
+    return pl.pallas_call(
+        functools.partial(tap_kernel, n),
+        grid_spec=pltpu.PrefetchScalarGridSpec(
+            num_scalar_prefetch=1,
+            grid=(1,),
+            in_specs=[whole(forward.shape)] + [whole(p.shape) for p in pieces],
+            out_specs=whole(shape),
+            scratch_shapes=[
+                pltpu.VMEM((2, n * rows, width), jnp.bfloat16),
+                pltpu.VMEM((2 * seg, width), jnp.float32),
+            ],
+        ),
+        out_shape=jax.ShapeDtypeStruct(shape, jnp.bfloat16),
+        compiler_params=params(),
+        name="kernels",
+    )(ids, forward, *pieces)
+
+
+def correlate_kernel(n, parts, ids, forward, back, kern, *refs):
+    pieces = refs[: n * parts]
+    outs = refs[n * parts : n * parts + n]
+    data, spec, acc, result = refs[n * parts + n :]
+    part_rows = pieces[0].shape[0]
+    rows = part_rows * parts
+    seg = forward.shape[1]
+    segs = n * rows // seg
+    width = data.shape[1]
+    for k in range(n):
+        for c in range(parts):
+            at = pl.multiple_of((ids[0] ^ k) * rows + c * part_rows, part_rows)
+            data[pl.ds(at, part_rows)] = pieces[k * parts + c][...]
+    for i in range(segs):
+        spec[i] = jnp.dot(forward[...], data[i * seg : (i + 1) * seg], preferred_element_type=jnp.float32)
+
+    tile = 16
+
+    def products(x, row, lane, first):
+        here = (pl.ds(row, tile), pl.ds(lane, LANES))
+        there = (pl.ds(row + seg, tile), pl.ds(lane, LANES))
+        g_real = [spec[(i, *here)] for i in range(segs)]
+        g_imag = [spec[(i, *there)] for i in range(segs)]
+        k_real = [kern[(x, r, *here)].astype(jnp.float32) for r in range(segs)]
+        k_imag = [kern[(x, r, *there)].astype(jnp.float32) for r in range(segs)]
+        if first:
+            edge = lax.broadcasted_iota(jnp.int32, (tile, LANES), 0) == 0
+        for j in range(segs):
+            both = sum(g_real[i] * k_real[i - j] for i in range(j, segs))
+            other = sum(g_imag[i] * k_imag[i - j] for i in range(j, segs))
+            cross = sum(g_imag[i] * k_real[i - j] - g_real[i] * k_imag[i - j] for i in range(j, segs))
+            if first:
+                real = both + jnp.where(edge, 0.0, other)
+                cross = jnp.where(edge, other, cross)
+            else:
+                real = both + other
+            acc[(j, *here)] = real.astype(jnp.bfloat16)
+            acc[(j, *there)] = cross.astype(jnp.bfloat16)
+
+    for x in range(2):
+        for lane in range(0, width, LANES):
+            products(x, 0, lane, True)
+
+            @pl.loop(1, seg // tile)
+            def _(t):
+                products(x, pl.multiple_of(t * tile, tile), lane, False)
+
+        for j in range(segs):
+            value = jnp.dot(back[...], acc[j], preferred_element_type=jnp.float32).astype(jnp.bfloat16)
+            for h in range(seg // rows):
+                result[j * (seg // rows) + h, x] = value[h * rows : (h + 1) * rows]
+    for k in range(n):
+        outs[k][...] = result[ids[0] ^ k]
+
+
+def correlate(ids, forward, back, kern, pieces):
+    n, parts = len(pieces), len(pieces[0])
+    flat = [p for group in pieces for p in group]
+    part_rows, width = flat[0].shape
+    rows = part_rows * parts
+    seg = forward.shape[1]
+    segs = n * rows // seg
+    out = (2, rows, width)
+    return pl.pallas_call(
+        functools.partial(correlate_kernel, n, parts),
+        grid_spec=pltpu.PrefetchScalarGridSpec(
+            num_scalar_prefetch=1,
+            grid=(1,),
+            in_specs=[whole(a.shape) for a in (forward, back, kern, *flat)],
+            out_specs=[whole(out)] * n,
+            scratch_shapes=[
+                pltpu.VMEM((n * rows, width), jnp.bfloat16),
+                pltpu.VMEM((segs, 2 * seg, width), jnp.float32),
+                pltpu.VMEM((segs, 2 * seg, width), jnp.bfloat16),
+                pltpu.VMEM((n, *out), jnp.bfloat16),
+            ],
+        ),
+        out_shape=[jax.ShapeDtypeStruct(out, jnp.bfloat16)] * n,
+        compiler_params=params(),
+        name="correlate",
+    )(ids, forward, back, kern, *flat)
+
+
+def finish_kernel(n, factor, ids, key, value, *refs):
+    pieces = refs[:n]
+    key_grad, value_grad, filter_grad = refs[n:]
+    step = pl.program_id(0)
+    for k in range(n):
+
+        @pl.when(step == k)
+        def _():
+            conv_grad = pieces[k][0].astype(jnp.float32)
+            key_grad[...] = (conv_grad * value[...].astype(jnp.float32)).astype(jnp.bfloat16)
+            value_grad[...] = (conv_grad * key[...].astype(jnp.float32)).astype(jnp.bfloat16)
+            filter_grad[...] = pieces[k][1].astype(jnp.float32) * factor
+
+
+def finish(ids, key, value, pieces, factor):
+    n = len(pieces)
+    rows, channels = key.shape
+    column = pl.BlockSpec((rows, channels // n), lambda k, ids: (0, ids[0] ^ k))
+    return pl.pallas_call(
+        functools.partial(finish_kernel, n, factor),
+        grid_spec=pltpu.PrefetchScalarGridSpec(
+            num_scalar_prefetch=1,
+            grid=(n,),
+            in_specs=[column] * 2 + [whole(p.shape) for p in pieces],
+            out_specs=[column] * 3,
+        ),
+        out_shape=[
+            jax.ShapeDtypeStruct(key.shape, jnp.bfloat16),
+            jax.ShapeDtypeStruct(key.shape, jnp.bfloat16),
+            jax.ShapeDtypeStruct(key.shape, jnp.float32),
+        ],
+        compiler_params=params(),
+        name="finish",
+    )(ids, key, value, *pieces)
+
+
+def exchange(pieces, n):
+    return [
+        piece if k == 0 else lax.ppermute(piece, "seq", [(i, i ^ k) for i in range(n)])
+        for k, piece in enumerate(pieces)
+    ]
+
+
+def fast_shards(grad_out, out_weight, query_gate, key_branch, value_branch, filter_taps):
+    n = lax.axis_size("seq")
+    planes = lax.axis_size("ch")
+    me = lax.axis_index("seq")
+    plane = lax.axis_index("ch")
+    rows = grad_out.shape[0]
+    factor = 1.0 / math.sqrt(rows * n)
+    forward, back = half_tables(2 * rows)
+    low = plane < planes // 2
+    ids = jnp.stack(
+        [
+            me,
+            plane,
+            jnp.where((plane == 0) | (plane == planes - 1), 1, 0),
+            plane ^ 1,
+            jnp.where(low, 2, 1),
+            jnp.where(low, 3, 0),
+        ]
+    ).astype(jnp.int32)
+
+    outer = [(i, i ^ 1) for i in range(planes)]
+    inner = [(1, 2), (2, 1), (0, 0), (3, 3)]
+    size = rows // CHUNKS
+    own = [grad_out[c * size : (c + 1) * size] for c in range(CHUNKS)]
+    outer_0 = [lax.ppermute(x, "ch", outer) for x in own]
+    inner_0 = [lax.ppermute(x, "ch", inner) for x in own]
+    outer_1 = [lax.ppermute(x, "ch", outer) for x in inner_0]
+    inner_1 = [lax.ppermute(x, "ch", inner) for x in outer_0]
+    outer_2 = [lax.ppermute(x, "ch", outer) for x in inner_1]
+
+    taps_input = exchange(pack(ids, key_branch, value_branch, filter_taps, n), n)
+    total = mix(ids, 1, [(grad_out,)], out_weight, None, n)
+    kern = tap_kernels(ids, forward, taps_input)
+    total = mix(ids, 3, [(x,) for x in outer_0], out_weight, total, n)
+    total = mix(ids, 4, list(zip(outer_1, inner_0)), out_weight, total, n)
+    gated = [
+        exchange(mix_gate(ids, 5, (outer_2[c], inner_1[c]), out_weight, total, query_gate, c, n), n)
+        for c in range(CHUNKS)
+    ]
+    results = exchange(correlate(ids, forward, back, kern, list(zip(*gated))), n)
+    return finish(ids, key_branch, value_branch, results, factor)
+
+
 def solution(mesh):
-    return jax.shard_map(
-        shards,
+    specs = dict(
         mesh=mesh,
         in_specs=(
             P("seq", "ch"),
@@ -143,3 +494,11 @@
         out_specs=(P("seq", "ch"), P("seq", "ch"), P("seq", "ch")),
         check_vma=False,
     )
+    n, planes = mesh.shape["seq"], mesh.shape["ch"]
+
+    def step(*arrays):
+        whole_tiles = arrays[1].shape[0] // planes % (n * LANES) == 0
+        fits = whole_tiles and planes == 4 and n & (n - 1) == 0
+        return jax.shard_map(fast_shards if fits else shards, **specs)(*arrays)
+
+    return step

time: 466 us -> 132 us (0.28)
  local copies, waits for them, and re-layouts: 142 us -> 5.35 us
  matrix products: 129 us -> 0 us
  waiting for transfers between devices: 113 us -> 26.8 us
  other arithmetic: 60.5 us -> 0 us
  Pallas kernels: 0 us -> 54.9 us
  starting transfers between devices: 0.16 us -> 43.4 us
  between operations: 13.9 us -> 0.9 us
  loops' own time: 5.33 us -> 0 us
    dot_general x11 -> x0, matrix products: 129 us -> none  [the longest x3 37.4 us: spectra(): jnp.einsum('qk,rkb->rqb', sine_forward, block_list, preferred_element_typ...]
    all_gather x3 -> x0, waiting for transfers between devices: 65.6 us -> none  [the longest x1 49.5 us: shards(): lax.all_gather(grad_out, 'ch', axis=1, tiled=True)]
    gather x4 -> x0, local copies, waits for them, and re-layouts: 60.4 us -> none  [the longest x2 30.2 us: shards(): lag_ksin = jnp.take(kern_sin, lag_clip, axis=0)]
    pallas_call x0 -> x9, Pallas kernels: none -> 54.9 us  [the longest x3 27.4 us: mix(): pl.pallas_call(functools.partial(mix_kernel, len(parts), len(parts[0]), t...]
    reduce_scatter x1 -> x0, waiting for transfers between devices: 46.2 us -> none  [shards(): lax.psum_scatter(buffer[seg_len:].astype(jnp.bfloat16), 'seq', scatter_di...]
    dynamic_slice x24 -> x0, local copies, waits for them, and re-layouts: 44.4 us -> none  [the longest x16 39.8 us: place(): windows[item_index]]
    ppermute x0 -> x38, starting transfers between devices: none -> 43.4 us  [the longest x28 25.3 us: exchange(): lax.ppermute(piece, 'seq', [(i, i ^ k) for i in range(n)])]
    add x1 -> x0, other arithmetic: 32.3 us -> none  [shards(): jnp.concatenate([jnp.zeros_like(tap_cos[:1]), tap_cos[:-1]], 0)]
  transfers between devices with their start and end apart: 4 -> 38, of which waited for: 3 -> 12; matrix products, arithmetic and copies ran while one was open for 36% -> 0% of each run, Pallas kernels for 0% -> 36%
where the time goes in v1:
time: 132 us; the launch traced here: 131 us
  Pallas kernels  54.9 us (42%)
  starting transfers between devices  43.4 us (33%)
  waiting for transfers between devices  26.8 us (20%)
  local copies, waits for them, and re-layouts  5.35 us (4%)
    pallas_call x3, Pallas kernels, mix(): pl.pallas_call(functools.partial(mix_kernel, len(parts), len(parts[0]), t...  27.4 us
    ppermute x28, starting transfers between devices, exchange(): lax.ppermute(piece, 'seq', [(i, i ^ k) for i in range(n)])  25.3 us
    pallas_call x2, Pallas kernels, mix_gate(): pl.pallas_call(functools.partial(gate_kernel, len(pair)), grid_spec=pltpu...  16.6 us
    ppermute x28, waiting for transfers between devices, exchange(): lax.ppermute(piece, 'seq', [(i, i ^ k) for i in range(n)])  13.1 us
    ppermute x2, starting transfers between devices, fast_shards(): outer_2 = [lax.ppermute(x, 'ch', outer) for x in inner_1]  6.7 us
    ppermute x2, waiting for transfers between devices, fast_shards(): outer_0 = [lax.ppermute(x, 'ch', outer) for x in own]  5.7 us
    ppermute x2, starting transfers between devices, fast_shards(): outer_1 = [lax.ppermute(x, 'ch', outer) for x in inner_0]  5.57 us
    unnamed x18, local copies, waits for them, and re-layouts  4.2 us
  transfers between devices with their start and end apart: 38, of which 12 were waited for; matrix products, arithmetic and copies ran while one was open for 0% of the time, Pallas kernels for 36%

profile of v1, /device:TPU:0, one launch (start us, length us, event | category | flops | bytes accessed | tf_op | source)
XLA Modules:
  0.0 131.4 jit_solution(6144945743861527372)
XLA Ops:
  0.6 1.1 fusion
  1.7 3.1 %collective-permute-start.14 = (bf16[64,2048]{1,0:T(8,128)(2,1)S(1)}, bf16[64,2048]{1,0:T(8,128)(2,1)S(1)}, u32[]{:S(2)}, u32[]{:S(2)}) collective-permute-start(bf16[64,2048]{1,0:T(8,128)(2,1)S(1)} %get-tuple-element.67), channel_id=1, source_target_pairs={{0,1},{1,0},{2,3},{3,2},{4,5},{5,4},{6,7},{7,6},{8,9},{9,8},{10,11... | collective-permute-start | bytes 786440 | tf_op jit(solution)/shard_map/ppermute | solution.py:464
  6.2 5.7 %collective-permute-done.14.refs_1_ = bf16[64,2048]{1,0:T(8,128)(2,1)S(1)} collective-permute-done((bf16[64,2048]{1,0:T(8,128)(2,1)S(1)}, bf16[64,2048]{1,0:T(8,128)(2,1)S(1)}, u32[]{:S(2)}, u32[]{:S(2)}) %collective-permute-start.14) | collective-permute-done | bytes 262176 | tf_op jit(solution)/shard_map/ppermute | solution.py:464
  12.7 1.0 copy-done.2
  15.8 1.5 %pack_taps_input.1 = (bf16[2,128,256]{2,1,0:T(8,128)(2,1)S(1)}, bf16[2,128,256]{2,1,0:T(8,128)(2,1)S(1)}, bf16[2,128,256]{2,1,0:T(8,128)(2,1)S(1)}, bf16[2,128,2...) custom-call(s32[6]{0:T(128)S(1)} %stack.27.ids, ...), custom_call_target="tpu_custom_call" | custom-call | tf_op jit(solution)/shard_map/pack_taps_input/pallas_call | solution.py:179
  18.8 2.0 %collective-permute-start.1 = (bf16[2,128,256]{2,1,0:T(8,128)(2,1)S(1)}, bf16[2,128,256]{2,1,0:T(8,128)(2,1)S(1)}, u32[]{:S(2)}, u32[]{:S(2)}) collective-permute-start(bf16[2,128,256]{2,1,0:T(8,128)(2,1)S(1)} %get-tuple-element.37), channel_id=1, source_target_pairs={{0,8},{4,12},{8,0},{12,4},{16,24},{20,28},{24,16},{28,20},{1,9},{5... | collective-permute-start | bytes 393224 | tf_op jit(solution)/shard_map/ppermute | solution.py:435
  20.7 5.5 %collective-permute-start.11 = (bf16[64,2048]{1,0:T(8,128)(2,1)S(1)}, bf16[64,2048]{1,0:T(8,128)(2,1)S(1)}, u32[]{:S(2)}, u32[]{:S(2)}) collective-permute-start(bf16[64,2048]{1,0:T(8,128)(2,1)S(1)} %collective-permute-done.10.refs_1_), channel_id=1, source_target_pairs={{0,1},{1,0},{2,3},{3,2},{4,5},{5,4},{6,7},{7,6},{8,9},{9,8},{10,11... | collective-permute-start | bytes 786440 | tf_op jit(solution)/shard_map/ppermute | solution.py:466
  26.3 2.0 %collective-permute-start.16 = (bf16[64,2048]{1,0:T(8,128)(2,1)S(1)}, bf16[64,2048]{1,0:T(8,128)(2,1)S(1)}, u32[]{:S(2)}, u32[]{:S(2)}) collective-permute-start(bf16[64,2048]{1,0:T(8,128)(2,1)S(1)} %collective-permute-done.15.refs_1_), channel_id=1, source_target_pairs={{0,1},{1,0},{2,3},{3,2},{4,5},{5,4},{6,7},{7,6},{8,9},{9,8},{10,11... | collective-permute-start | bytes 786440 | tf_op jit(solution)/shard_map/ppermute | solution.py:468
  28.3 4.7 %collective-permute-start.9 = (bf16[64,2048]{1,0:T(8,128)(2,1)S(1)}, bf16[64,2048]{1,0:T(8,128)(2,1)S(1)}, u32[]{:S(2)}, u32[]{:S(2)}) collective-permute-start(bf16[64,2048]{1,0:T(8,128)(2,1)S(1)} %collective-permute-done.8.refs_1_), channel_id=1, source_target_pairs={{0,1},{1,0},{2,3},{3,2},{4,5},{5,4},{6,7},{7,6},{8,9},{9,8},{10,11... | collective-permute-start | bytes 786440 | tf_op jit(solution)/shard_map/ppermute | solution.py:468
  33.6 1.5 %collective-permute-start.3 = (bf16[2,128,256]{2,1,0:T(8,128)(2,1)S(1)}, bf16[2,128,256]{2,1,0:T(8,128)(2,1)S(1)}, u32[]{:S(2)}, u32[]{:S(2)}) collective-permute-start(bf16[2,128,256]{2,1,0:T(8,128)(2,1)S(1)} %get-tuple-element.39), channel_id=1, source_target_pairs={{0,16},{4,20},{8,24},{12,28},{16,0},{20,4},{24,8},{28,12},{1,17},{... | collective-permute-start | bytes 393224 | tf_op jit(solution)/shard_map/ppermute | solution.py:435
  35.1 3.9 %collective-permute-done.13.refs_2_ = bf16[64,2048]{1,0:T(8,128)(2,1)S(1)} collective-permute-done((bf16[64,2048]{1,0:T(8,128)(2,1)S(1)}, bf16[64,2048]{1,0:T(8,128)(2,1)S(1)}, u32[]{:S(2)}, u32[]{:S(2)}) %collective-permute-start.13) | collective-permute-done | bytes 262176 | tf_op jit(solution)/shard_map/ppermute | solution.py:466
  39.0 1.5 %collective-permute-start.5 = (bf16[2,128,256]{2,1,0:T(8,128)(2,1)S(1)}, bf16[2,128,256]{2,1,0:T(8,128)(2,1)S(1)}, u32[]{:S(2)}, u32[]{:S(2)}) collective-permute-start(bf16[2,128,256]{2,1,0:T(8,128)(2,1)S(1)} %get-tuple-element.41), channel_id=1, source_target_pairs={{0,24},{4,28},{8,16},{12,20},{16,8},{20,12},{24,0},{28,4},{1,25},{... | collective-permute-start | bytes 393224 | tf_op jit(solution)/shard_map/ppermute | solution.py:435
  40.5 4.1 %collective-permute-done.16.refs_0_ = bf16[64,2048]{1,0:T(8,128)(2,1)S(1)} collective-permute-done((bf16[64,2048]{1,0:T(8,128)(2,1)S(1)}, bf16[64,2048]{1,0:T(8,128)(2,1)S(1)}, u32[]{:S(2)}, u32[]{:S(2)}) %collective-permute-start.16) | collective-permute-done | bytes 262176 | tf_op jit(solution)/shard_map/ppermute | solution.py:468
  45.7 8.2 %mix.3.refs_3_ = f32[128,2048]{1,0:T(8,128)S(1)} custom-call(s32[6]{0:T(128)S(1)} %stack.27.ids, bf16[128,2048]{1,0:T(8,128)(2,1)S(1)} %copy-done.1, bf16[2048,8192]{1,0:T(8,128)(2,1)} %refs_2_.5), custom_call_target="tpu_custom_call" | custom-call | tf_op jit(solution)/shard_map/mix/pallas_call | solution.py:222
  53.9 9.6 %mix.4.refs_5_ = f32[128,2048]{1,0:T(8,128)S(1)} custom-call(s32[6]{0:T(128)S(1)} %stack.27.ids, bf16[64,2048]{1,0:T(8,128)(2,1)S(1)} %collective-permute-done.7.refs_0_, bf16[64,2048]{1,0:T(8,128)(2,1)S(1)} %collective-permute-done.14.refs_1_, bf16[2048,8192]{1,0:T(8,128)(2,1)} %refs_2_.5, f32[128,2048]{1,0:T(8,128)S(1)} %mix.3.refs_3_), custom_call_target="tpu_custom_call" | custom-call | tf_op jit(solution)/shard_map/mix/pallas_call | solution.py:222
  63.5 9.6 %mix.5.refs_3_ = f32[128,2048]{1,0:T(8,128)S(1)} custom-call(s32[6]{0:T(128)S(1)} %stack.27.ids, bf16[64,2048]{1,0:T(8,128)(2,1)S(1)} %collective-permute-done.11.refs_0_, bf16[64,2048]{1,0:T(8,128)(2,1)S(1)} %collective-permute-done.10.refs_1_, bf16[64,2048]{1,0:T(8,128)(2,1)S(1)} %collective-permute-done.13.refs_2_, ...), custom_call_target="tpu_custom_call" | custom-call | tf_op jit(solution)/shard_map/mix/pallas_call | solution.py:222
  73.1 8.3 %mix_gate.3 = (bf16[64,256]{1,0:T(8,128)(2,1)S(1)}, bf16[64,256]{1,0:T(8,128)(2,1)S(1)}, bf16[64,256]{1,0:T(8,128)(2,1)S(1)}, bf16[64,256]{1,0:T(8,128)(2,1)S(1)...) custom-call(s32[6]{0:T(128)S(1)} %stack.27.ids, ...), custom_call_target="tpu_custom_call" | custom-call | tf_op jit(solution)/shard_map/mix_gate/pallas_call | solution.py:256
  81.5 1.7 %collective-permute-start.18 = (bf16[64,256]{1,0:T(8,128)(2,1)S(1)}, bf16[64,256]{1,0:T(8,128)(2,1)S(1)}, u32[]{:S(2)}, u32[]{:S(2)}) collective-permute-start(bf16[64,256]{1,0:T(8,128)(2,1)S(1)} %get-tuple-element.46), channel_id=1, source_target_pairs={{0,4},{4,0},{8,12},{12,8},{16,20},{20,16},{24,28},{28,24},{1,5},{5... | collective-permute-start | bytes 98312 | tf_op jit(solution)/shard_map/ppermute | solution.py:435
  83.1 1.5 %collective-permute-start.20 = (bf16[64,256]{1,0:T(8,128)(2,1)S(1)}, bf16[64,256]{1,0:T(8,128)(2,1)S(1)}, u32[]{:S(2)}, u32[]{:S(2)}) collective-permute-start(bf16[64,256]{1,0:T(8,128)(2,1)S(1)} %get-tuple-element.48), channel_id=1, source_target_pairs={{0,8},{4,12},{8,0},{12,4},{16,24},{20,28},{24,16},{28,20},{1,9},{5... | collective-permute-start | bytes 98312 | tf_op jit(solution)/shard_map/ppermute | solution.py:435
  85.2 8.3 %mix_gate.2 = (bf16[64,256]{1,0:T(8,128)(2,1)S(1)}, bf16[64,256]{1,0:T(8,128)(2,1)S(1)}, bf16[64,256]{1,0:T(8,128)(2,1)S(1)}, bf16[64,256]{1,0:T(8,128)(2,1)S(1)...) custom-call(s32[6]{0:T(128)S(1)} %stack.27.ids, ...), custom_call_target="tpu_custom_call" | custom-call | tf_op jit(solution)/shard_map/mix_gate/pallas_call | solution.py:256
  93.5 1.5 %collective-permute-start.26 = (bf16[64,256]{1,0:T(8,128)(2,1)S(1)}, bf16[64,256]{1,0:T(8,128)(2,1)S(1)}, u32[]{:S(2)}, u32[]{:S(2)}) collective-permute-start(bf16[64,256]{1,0:T(8,128)(2,1)S(1)} %get-tuple-element.54), channel_id=1, source_target_pairs={{0,20},{4,16},{8,28},{12,24},{16,4},{20,0},{24,12},{28,8},{1,21},{... | collective-permute-start | bytes 98312 | tf_op jit(solution)/shard_map/ppermute | solution.py:435
  95.0 1.4 %collective-permute-start.28 = (bf16[64,256]{1,0:T(8,128)(2,1)S(1)}, bf16[64,256]{1,0:T(8,128)(2,1)S(1)}, u32[]{:S(2)}, u32[]{:S(2)}) collective-permute-start(bf16[64,256]{1,0:T(8,128)(2,1)S(1)} %get-tuple-element.56), channel_id=1, source_target_pairs={{0,24},{4,28},{8,16},{12,20},{16,8},{20,12},{24,0},{28,4},{1,25},{... | collective-permute-start | bytes 98312 | tf_op jit(solution)/shard_map/ppermute | solution.py:435
  98.1 1.5 %collective-permute-start.19 = (bf16[64,256]{1,0:T(8,128)(2,1)S(1)}, bf16[64,256]{1,0:T(8,128)(2,1)S(1)}, u32[]{:S(2)}, u32[]{:S(2)}) collective-permute-start(bf16[64,256]{1,0:T(8,128)(2,1)S(1)} %get-tuple-element.47), channel_id=1, source_target_pairs={{0,8},{4,12},{8,0},{12,4},{16,24},{20,28},{24,16},{28,20},{1,9},{5... | collective-permute-start | bytes 98312 | tf_op jit(solution)/shard_map/ppermute | solution.py:435
  101.0 1.2 collective-permute-start.25
  103.2 1.8 %collective-permute-start.29 = (bf16[64,256]{1,0:T(8,128)(2,1)S(1)}, bf16[64,256]{1,0:T(8,128)(2,1)S(1)}, u32[]{:S(2)}, u32[]{:S(2)}) collective-permute-start(bf16[64,256]{1,0:T(8,128)(2,1)S(1)} %get-tuple-element.57), channel_id=1, source_target_pairs={{0,28},{4,24},{8,20},{12,16},{16,12},{20,8},{24,4},{28,0},{1,29},{... | collective-permute-start | bytes 98312 | tf_op jit(solution)/shard_map/ppermute | solution.py:435
  105.0 1.3 %kernels.1.kern = bf16[2,4,512,256]{3,2,1,0:T(8,128)(2,1)S(1)} custom-call(s32[6]{0:T(128)S(1)} %stack.27.ids, bf16[512,256]{1,0:T(8,128)(2,1)S(1)} %copy-done.6, bf16[2,128,256]{2,1,0:T(8,128)(2,1)S(1)} %get-tuple-element.35.refs_0_, bf16[2,128,256]{2,1,0:T(8,128)(2,1)S(1)} %collective-permute-done.refs_1_, ...), custom_call_target="tpu_custom_call" | custom-call | tf_op jit(solution)/shard_map/kernels/pallas_call | solution.py:296
  107.6 4.1 %correlate.1 = (bf16[2,128,256]{2,1,0:T(8,128)(2,1)S(1)}, bf16[2,128,256]{2,1,0:T(8,128)(2,1)S(1)}, bf16[2,128,256]{2,1,0:T(8,128)(2,1)S(1)}, bf16[2,128,256]{2,...) custom-call(s32[6]{0:T(128)S(1)} %stack.27.ids, ...), custom_call_target="tpu_custom_call" | custom-call | tf_op jit(solution)/shard_map/correlate/pallas_call | solution.py:377
  113.6 1.2 collective-permute-start.34
  115.4 1.9 %collective-permute-start.36 = (bf16[2,128,256]{2,1,0:T(8,128)(2,1)S(1)}, bf16[2,128,256]{2,1,0:T(8,128)(2,1)S(1)}, u32[]{:S(2)}, u32[]{:S(2)}) collective-permute-start(bf16[2,128,256]{2,1,0:T(8,128)(2,1)S(1)} %get-tuple-element.65), channel_id=1, source_target_pairs={{0,24},{4,28},{8,16},{12,20},{16,8},{20,12},{24,0},{28,4},{1,25},{... | collective-permute-start | bytes 393224 | tf_op jit(solution)/shard_map/ppermute | solution.py:435
  118.6 1.3 collective-permute-done.33.refs_3_
  119.9 7.5 %collective-permute-done.35.refs_5_ = bf16[2,128,256]{2,1,0:T(8,128)(2,1)S(1)} collective-permute-done((bf16[2,128,256]{2,1,0:T(8,128)(2,1)S(1)}, bf16[2,128,256]{2,1,0:T(8,128)(2,1)S(1)}, u32[]{:S(2)}, u32[]{:S(2)}) %collective-permute-start.35) | collective-permute-done | bytes 131104 | tf_op jit(solution)/shard_map/ppermute | solution.py:435
  127.4 4.0 %finish.1 = (bf16[128,2048]{1,0:T(8,128)(2,1)}, bf16[128,2048]{1,0:T(8,128)(2,1)}, f32[128,2048]{1,0:T(8,128)}) custom-call(s32[6]{0:T(128)S(1)} %stack.27.ids, bf16[128,2048]{1,0:T(8,128)(2,1)S(1)} %copy-done.3, bf16[128,2048]{1,0:T(8,128)(2,1)S(1)} %copy-done.5, bf16[2,128,256]{2,1,0:T(8,128)(2,1)S(1)} %get-tuple-element.59.refs_0_, ...), custom_call_target="tpu_custom_call" | custom-call | tf_op jit(solution)/shard_map/finish/pallas_call | solution.py:415
  (73 shorter events, 17.0 us)
Async XLA Ops:
  1.7 10.2 %collective-permute-start.14 = (bf16[64,2048]{1,0:T(8,128)(2,1)S(1)}, bf16[64,2048]{1,0:T(8,128)(2,1)S(1)}, u32[]{:S(2)}, u32[]{:S(2)}) collective-permute-start(bf16[64,2048]{1,0:T(8,128)(2,1)S(1)} %get-tuple-element.67), channel_id=1, source_target_pairs={{0,1},{1,0},{2,3},{3,2},{4,5},{5,4},{6,7},{7,6},{8,9},{9,8},{10,11... | collective-permute-start | bytes 786440 | tf_op jit(solution)/shard_map/ppermute | solution.py:464
  4.8 12.7 %collective-permute-start.7 = (bf16[64,2048]{1,0:T(8,128)(2,1)S(1)}, bf16[64,2048]{1,0:T(8,128)(2,1)S(1)}, u32[]{:S(2)}, u32[]{:S(2)}) collective-permute-start(bf16[64,2048]{1,0:T(8,128)(2,1)S(1)} %get-tuple-element.68), channel_id=1, source_target_pairs={{0,1},{1,0},{2,3},{3,2},{4,5},{5,4},{6,7},{7,6},{8,9},{9,8},{10,11... | collective-permute-start | bytes 786440 | tf_op jit(solution)/shard_map/ppermute | solution.py:464
  4.9 15.9 %collective-permute-start.10 = (bf16[64,2048]{1,0:T(8,128)(2,1)S(1)}, bf16[64,2048]{1,0:T(8,128)(2,1)S(1)}, u32[]{:S(2)}, u32[]{:S(2)}) collective-permute-start(bf16[64,2048]{1,0:T(8,128)(2,1)S(1)} %get-tuple-element.68), channel_id=1, source_target_pairs={{1,2},{2,1},{0,0},{3,3},{5,6},{6,5},{4,4},{7,7},{9,10},{10,9},{8,8... | collective-permute-start | bytes 786440 | tf_op jit(solution)/shard_map/ppermute | solution.py:465
  5.5 20.7 %collective-permute-start.12 = (bf16[64,2048]{1,0:T(8,128)(2,1)S(1)}, bf16[64,2048]{1,0:T(8,128)(2,1)S(1)}, u32[]{:S(2)}, u32[]{:S(2)}) collective-permute-start(bf16[64,2048]{1,0:T(8,128)(2,1)S(1)} %get-tuple-element.67), channel_id=1, source_target_pairs={{1,2},{2,1},{0,0},{3,3},{5,6},{6,5},{4,4},{7,7},{9,10},{10,9},{8,8... | collective-permute-start | bytes 786440 | tf_op jit(solution)/shard_map/ppermute | solution.py:465
  11.9 14.4 %collective-permute-start.15 = (bf16[64,2048]{1,0:T(8,128)(2,1)S(1)}, bf16[64,2048]{1,0:T(8,128)(2,1)S(1)}, u32[]{:S(2)}, u32[]{:S(2)}) collective-permute-start(bf16[64,2048]{1,0:T(8,128)(2,1)S(1)} %collective-permute-done.14.refs_1_), channel_id=1, source_target_pairs={{1,2},{2,1},{0,0},{3,3},{5,6},{6,5},{4,4},{7,7},{9,10},{10,9},{8,8... | collective-permute-start | bytes 786440 | tf_op jit(solution)/shard_map/ppermute | solution.py:467
  17.4 10.8 %collective-permute-start.8 = (bf16[64,2048]{1,0:T(8,128)(2,1)S(1)}, bf16[64,2048]{1,0:T(8,128)(2,1)S(1)}, u32[]{:S(2)}, u32[]{:S(2)}) collective-permute-start(bf16[64,2048]{1,0:T(8,128)(2,1)S(1)} %collective-permute-done.7.refs_0_), channel_id=1, source_target_pairs={{1,2},{2,1},{0,0},{3,3},{5,6},{6,5},{4,4},{7,7},{9,10},{10,9},{8,8... | collective-permute-start | bytes 786440 | tf_op jit(solution)/shard_map/ppermute | solution.py:467
  18.8 9.5 %collective-permute-start.1 = (bf16[2,128,256]{2,1,0:T(8,128)(2,1)S(1)}, bf16[2,128,256]{2,1,0:T(8,128)(2,1)S(1)}, u32[]{:S(2)}, u32[]{:S(2)}) collective-permute-start(bf16[2,128,256]{2,1,0:T(8,128)(2,1)S(1)} %get-tuple-element.37), channel_id=1, source_target_pairs={{0,8},{4,12},{8,0},{12,4},{16,24},{20,28},{24,16},{28,20},{1,9},{5... | collective-permute-start | bytes 393224 | tf_op jit(solution)/shard_map/ppermute | solution.py:435
  20.7 14.3 %collective-permute-start.11 = (bf16[64,2048]{1,0:T(8,128)(2,1)S(1)}, bf16[64,2048]{1,0:T(8,128)(2,1)S(1)}, u32[]{:S(2)}, u32[]{:S(2)}) collective-permute-start(bf16[64,2048]{1,0:T(8,128)(2,1)S(1)} %collective-permute-done.10.refs_1_), channel_id=1, source_target_pairs={{0,1},{1,0},{2,3},{3,2},{4,5},{5,4},{6,7},{7,6},{8,9},{9,8},{10,11... | collective-permute-start | bytes 786440 | tf_op jit(solution)/shard_map/ppermute | solution.py:466
  26.3 12.7 %collective-permute-start.13 = (bf16[64,2048]{1,0:T(8,128)(2,1)S(1)}, bf16[64,2048]{1,0:T(8,128)(2,1)S(1)}, u32[]{:S(2)}, u32[]{:S(2)}) collective-permute-start(bf16[64,2048]{1,0:T(8,128)(2,1)S(1)} %collective-permute-done.12.refs_3_), channel_id=1, source_target_pairs={{0,1},{1,0},{2,3},{3,2},{4,5},{5,4},{6,7},{7,6},{8,9},{9,8},{10,11... | collective-permute-start | bytes 786440 | tf_op jit(solution)/shard_map/ppermute | solution.py:466
  26.3 18.3 %collective-permute-start.16 = (bf16[64,2048]{1,0:T(8,128)(2,1)S(1)}, bf16[64,2048]{1,0:T(8,128)(2,1)S(1)}, u32[]{:S(2)}, u32[]{:S(2)}) collective-permute-start(bf16[64,2048]{1,0:T(8,128)(2,1)S(1)} %collective-permute-done.15.refs_1_), channel_id=1, source_target_pairs={{0,1},{1,0},{2,3},{3,2},{4,5},{5,4},{6,7},{7,6},{8,9},{9,8},{10,11... | collective-permute-start | bytes 786440 | tf_op jit(solution)/shard_map/ppermute | solution.py:468
  28.3 5.3 %collective-permute-start.2 = (bf16[2,128,256]{2,1,0:T(8,128)(2,1)S(1)}, bf16[2,128,256]{2,1,0:T(8,128)(2,1)S(1)}, u32[]{:S(2)}, u32[]{:S(2)}) collective-permute-start(bf16[2,128,256]{2,1,0:T(8,128)(2,1)S(1)} %get-tuple-element.38), channel_id=1, source_target_pairs={{0,12},{4,8},{8,4},{12,0},{16,28},{20,24},{24,20},{28,16},{1,13},{... | collective-permute-start | bytes 393224 | tf_op jit(solution)/shard_map/ppermute | solution.py:435
  28.3 56.3 %collective-permute-start.9 = (bf16[64,2048]{1,0:T(8,128)(2,1)S(1)}, bf16[64,2048]{1,0:T(8,128)(2,1)S(1)}, u32[]{:S(2)}, u32[]{:S(2)}) collective-permute-start(bf16[64,2048]{1,0:T(8,128)(2,1)S(1)} %collective-permute-done.8.refs_1_), channel_id=1, source_target_pairs={{0,1},{1,0},{2,3},{3,2},{4,5},{5,4},{6,7},{7,6},{8,9},{9,8},{10,11... | collective-permute-start | bytes 786440 | tf_op jit(solution)/shard_map/ppermute | solution.py:468
  33.6 47.9 %collective-permute-start.3 = (bf16[2,128,256]{2,1,0:T(8,128)(2,1)S(1)}, bf16[2,128,256]{2,1,0:T(8,128)(2,1)S(1)}, u32[]{:S(2)}, u32[]{:S(2)}) collective-permute-start(bf16[2,128,256]{2,1,0:T(8,128)(2,1)S(1)} %get-tuple-element.39), channel_id=1, source_target_pairs={{0,16},{4,20},{8,24},{12,28},{16,0},{20,4},{24,8},{28,12},{1,17},{... | collective-permute-start | bytes 393224 | tf_op jit(solution)/shard_map/ppermute | solution.py:435
  35.1 48.1 %collective-permute-start.4 = (bf16[2,128,256]{2,1,0:T(8,128)(2,1)S(1)}, bf16[2,128,256]{2,1,0:T(8,128)(2,1)S(1)}, u32[]{:S(2)}, u32[]{:S(2)}) collective-permute-start(bf16[2,128,256]{2,1,0:T(8,128)(2,1)S(1)} %get-tuple-element.40), channel_id=1, source_target_pairs={{0,20},{4,16},{8,28},{12,24},{16,4},{20,0},{24,12},{28,8},{1,21},{... | collective-permute-start | bytes 393224 | tf_op jit(solution)/shard_map/ppermute | solution.py:435
  39.0 45.6 %collective-permute-start.5 = (bf16[2,128,256]{2,1,0:T(8,128)(2,1)S(1)}, bf16[2,128,256]{2,1,0:T(8,128)(2,1)S(1)}, u32[]{:S(2)}, u32[]{:S(2)}) collective-permute-start(bf16[2,128,256]{2,1,0:T(8,128)(2,1)S(1)} %get-tuple-element.41), channel_id=1, source_target_pairs={{0,24},{4,28},{8,16},{12,20},{16,8},{20,12},{24,0},{28,4},{1,25},{... | collective-permute-start | bytes 393224 | tf_op jit(solution)/shard_map/ppermute | solution.py:435
  44.6 48.9 %collective-permute-start.6 = (bf16[2,128,256]{2,1,0:T(8,128)(2,1)S(1)}, bf16[2,128,256]{2,1,0:T(8,128)(2,1)S(1)}, u32[]{:S(2)}, u32[]{:S(2)}) collective-permute-start(bf16[2,128,256]{2,1,0:T(8,128)(2,1)S(1)} %get-tuple-element.42), channel_id=1, source_target_pairs={{0,28},{4,24},{8,20},{12,16},{16,12},{20,8},{24,4},{28,0},{1,29},{... | collective-permute-start | bytes 393224 | tf_op jit(solution)/shard_map/ppermute | solution.py:435
  81.5 13.6 %collective-permute-start.18 = (bf16[64,256]{1,0:T(8,128)(2,1)S(1)}, bf16[64,256]{1,0:T(8,128)(2,1)S(1)}, u32[]{:S(2)}, u32[]{:S(2)}) collective-permute-start(bf16[64,256]{1,0:T(8,128)(2,1)S(1)} %get-tuple-element.46), channel_id=1, source_target_pairs={{0,4},{4,0},{8,12},{12,8},{16,20},{20,16},{24,28},{28,24},{1,5},{5... | collective-permute-start | bytes 98312 | tf_op jit(solution)/shard_map/ppermute | solution.py:435
  83.1 13.4 %collective-permute-start.20 = (bf16[64,256]{1,0:T(8,128)(2,1)S(1)}, bf16[64,256]{1,0:T(8,128)(2,1)S(1)}, u32[]{:S(2)}, u32[]{:S(2)}) collective-permute-start(bf16[64,256]{1,0:T(8,128)(2,1)S(1)} %get-tuple-element.48), channel_id=1, source_target_pairs={{0,8},{4,12},{8,0},{12,4},{16,24},{20,28},{24,16},{28,20},{1,9},{5... | collective-permute-start | bytes 98312 | tf_op jit(solution)/shard_map/ppermute | solution.py:435
  84.6 12.9 %collective-permute-start.22 = (bf16[64,256]{1,0:T(8,128)(2,1)S(1)}, bf16[64,256]{1,0:T(8,128)(2,1)S(1)}, u32[]{:S(2)}, u32[]{:S(2)}) collective-permute-start(bf16[64,256]{1,0:T(8,128)(2,1)S(1)} %get-tuple-element.50), channel_id=1, source_target_pairs={{0,12},{4,8},{8,4},{12,0},{16,28},{20,24},{24,20},{28,16},{1,13},{... | collective-permute-start | bytes 98312 | tf_op jit(solution)/shard_map/ppermute | solution.py:435
  84.6 13.5 %collective-permute-start.24 = (bf16[64,256]{1,0:T(8,128)(2,1)S(1)}, bf16[64,256]{1,0:T(8,128)(2,1)S(1)}, u32[]{:S(2)}, u32[]{:S(2)}) collective-permute-start(bf16[64,256]{1,0:T(8,128)(2,1)S(1)} %get-tuple-element.52), channel_id=1, source_target_pairs={{0,16},{4,20},{8,24},{12,28},{16,0},{20,4},{24,8},{28,12},{1,17},{... | collective-permute-start | bytes 98312 | tf_op jit(solution)/shard_map/ppermute | solution.py:435
  93.5 6.1 %collective-permute-start.26 = (bf16[64,256]{1,0:T(8,128)(2,1)S(1)}, bf16[64,256]{1,0:T(8,128)(2,1)S(1)}, u32[]{:S(2)}, u32[]{:S(2)}) collective-permute-start(bf16[64,256]{1,0:T(8,128)(2,1)S(1)} %get-tuple-element.54), channel_id=1, source_target_pairs={{0,20},{4,16},{8,28},{12,24},{16,4},{20,0},{24,12},{28,8},{1,21},{... | collective-permute-start | bytes 98312 | tf_op jit(solution)/shard_map/ppermute | solution.py:435
  98.1 5.1 %collective-permute-start.19 = (bf16[64,256]{1,0:T(8,128)(2,1)S(1)}, bf16[64,256]{1,0:T(8,128)(2,1)S(1)}, u32[]{:S(2)}, u32[]{:S(2)}) collective-permute-start(bf16[64,256]{1,0:T(8,128)(2,1)S(1)} %get-tuple-element.47), channel_id=1, source_target_pairs={{0,8},{4,12},{8,0},{12,4},{16,24},{20,28},{24,16},{28,20},{1,9},{5... | collective-permute-start | bytes 98312 | tf_op jit(solution)/shard_map/ppermute | solution.py:435
  99.6 6.7 %collective-permute-start.21 = (bf16[64,256]{1,0:T(8,128)(2,1)S(1)}, bf16[64,256]{1,0:T(8,128)(2,1)S(1)}, u32[]{:S(2)}, u32[]{:S(2)}) collective-permute-start(bf16[64,256]{1,0:T(8,128)(2,1)S(1)} %get-tuple-element.49), channel_id=1, source_target_pairs={{0,12},{4,8},{8,4},{12,0},{16,28},{20,24},{24,20},{28,16},{1,13},{... | collective-permute-start | bytes 98312 | tf_op jit(solution)/shard_map/ppermute | solution.py:435
  99.9 6.5 %collective-permute-start.23 = (bf16[64,256]{1,0:T(8,128)(2,1)S(1)}, bf16[64,256]{1,0:T(8,128)(2,1)S(1)}, u32[]{:S(2)}, u32[]{:S(2)}) collective-permute-start(bf16[64,256]{1,0:T(8,128)(2,1)S(1)} %get-tuple-element.51), channel_id=1, source_target_pairs={{0,16},{4,20},{8,24},{12,28},{16,0},{20,4},{24,8},{28,12},{1,17},{... | collective-permute-start | bytes 98312 | tf_op jit(solution)/shard_map/ppermute | solution.py:435
  101.0 5.3 %collective-permute-start.25 = (bf16[64,256]{1,0:T(8,128)(2,1)S(1)}, bf16[64,256]{1,0:T(8,128)(2,1)S(1)}, u32[]{:S(2)}, u32[]{:S(2)}) collective-permute-start(bf16[64,256]{1,0:T(8,128)(2,1)S(1)} %get-tuple-element.53), channel_id=1, source_target_pairs={{0,20},{4,16},{8,28},{12,24},{16,4},{20,0},{24,12},{28,8},{1,21},{... | collective-permute-start | bytes 98312 | tf_op jit(solution)/shard_map/ppermute | solution.py:435
  102.3 4.8 %collective-permute-start.27 = (bf16[64,256]{1,0:T(8,128)(2,1)S(1)}, bf16[64,256]{1,0:T(8,128)(2,1)S(1)}, u32[]{:S(2)}, u32[]{:S(2)}) collective-permute-start(bf16[64,256]{1,0:T(8,128)(2,1)S(1)} %get-tuple-element.55), channel_id=1, source_target_pairs={{0,24},{4,28},{8,16},{12,20},{16,8},{20,12},{24,0},{28,4},{1,25},{... | collective-permute-start | bytes 98312 | tf_op jit(solution)/shard_map/ppermute | solution.py:435
  111.8 6.3 %collective-permute-start.32 = (bf16[2,128,256]{2,1,0:T(8,128)(2,1)S(1)}, bf16[2,128,256]{2,1,0:T(8,128)(2,1)S(1)}, u32[]{:S(2)}, u32[]{:S(2)}) collective-permute-start(bf16[2,128,256]{2,1,0:T(8,128)(2,1)S(1)} %get-tuple-element.61), channel_id=1, source_target_pairs={{0,8},{4,12},{8,0},{12,4},{16,24},{20,28},{24,16},{28,20},{1,9},{5... | collective-permute-start | bytes 393224 | tf_op jit(solution)/shard_map/ppermute | solution.py:435
  112.8 7.1 %collective-permute-start.33 = (bf16[2,128,256]{2,1,0:T(8,128)(2,1)S(1)}, bf16[2,128,256]{2,1,0:T(8,128)(2,1)S(1)}, u32[]{:S(2)}, u32[]{:S(2)}) collective-permute-start(bf16[2,128,256]{2,1,0:T(8,128)(2,1)S(1)} %get-tuple-element.62), channel_id=1, source_target_pairs={{0,12},{4,8},{8,4},{12,0},{16,28},{20,24},{24,20},{28,16},{1,13},{... | collective-permute-start | bytes 393224 | tf_op jit(solution)/shard_map/ppermute | solution.py:435
  113.6 6.3 %collective-permute-start.34 = (bf16[2,128,256]{2,1,0:T(8,128)(2,1)S(1)}, bf16[2,128,256]{2,1,0:T(8,128)(2,1)S(1)}, u32[]{:S(2)}, u32[]{:S(2)}) collective-permute-start(bf16[2,128,256]{2,1,0:T(8,128)(2,1)S(1)} %get-tuple-element.63), channel_id=1, source_target_pairs={{0,16},{4,20},{8,24},{12,28},{16,0},{20,4},{24,8},{28,12},{1,17},{... | collective-permute-start | bytes 393224 | tf_op jit(solution)/shard_map/ppermute | solution.py:435
  114.8 12.6 %collective-permute-start.35 = (bf16[2,128,256]{2,1,0:T(8,128)(2,1)S(1)}, bf16[2,128,256]{2,1,0:T(8,128)(2,1)S(1)}, u32[]{:S(2)}, u32[]{:S(2)}) collective-permute-start(bf16[2,128,256]{2,1,0:T(8,128)(2,1)S(1)} %get-tuple-element.64), channel_id=1, source_target_pairs={{0,20},{4,16},{8,28},{12,24},{16,4},{20,0},{24,12},{28,8},{1,21},{... | collective-permute-start | bytes 393224 | tf_op jit(solution)/shard_map/ppermute | solution.py:435
  115.4 12.0 %collective-permute-start.36 = (bf16[2,128,256]{2,1,0:T(8,128)(2,1)S(1)}, bf16[2,128,256]{2,1,0:T(8,128)(2,1)S(1)}, u32[]{:S(2)}, u32[]{:S(2)}) collective-permute-start(bf16[2,128,256]{2,1,0:T(8,128)(2,1)S(1)} %get-tuple-element.65), channel_id=1, source_target_pairs={{0,24},{4,28},{8,16},{12,20},{16,8},{20,12},{24,0},{28,4},{1,25},{... | collective-permute-start | bytes 393224 | tf_op jit(solution)/shard_map/ppermute | solution.py:435
  118.2 9.2 %collective-permute-start.37 = (bf16[2,128,256]{2,1,0:T(8,128)(2,1)S(1)}, bf16[2,128,256]{2,1,0:T(8,128)(2,1)S(1)}, u32[]{:S(2)}, u32[]{:S(2)}) collective-permute-start(bf16[2,128,256]{2,1,0:T(8,128)(2,1)S(1)} %get-tuple-element.66), channel_id=1, source_target_pairs={{0,28},{4,24},{8,20},{12,16},{16,12},{20,8},{24,4},{28,0},{1,29},{... | collective-permute-start | bytes 393224 | tf_op jit(solution)/shard_map/ppermute | solution.py:435
  (15 other events, 222.0 us)

commit v2 on v0

--- a/solution.py
+++ b/solution.py
@@ -1,9 +1,17 @@
+import functools
 import math
 
 import jax
 import jax.numpy as jnp
+import ml_dtypes
+import numpy as np
 from jax import lax
+from jax.experimental import pallas as pl
+from jax.experimental.pallas import tpu as pltpu
 from jax.sharding import PartitionSpec as P
+
+LANES = 128
+CHUNKS = 2
 
 
 def build_tables(seg_len):
@@ -128,9 +136,483 @@
     return (key_grad, value_grad, filter_grad)
 
 
+def half_tables(rows):
+    size = 2 * rows
+    freq = np.arange(rows)
+    pos = np.arange(rows)
+    angle = 2.0 * np.pi * (np.outer(freq, pos) % size) / size
+    sine = np.sin(angle)
+    sine[0] = (-1.0) ** pos
+    forward = np.concatenate([np.cos(angle), sine], 0)
+    angle = 2.0 * np.pi * (np.outer(rows - pos, freq) % size) / size
+    cos_back = 2.0 * np.cos(angle)
+    sin_back = -2.0 * np.sin(angle)
+    cos_back[:, 0] = 1.0
+    sin_back[:, 0] = (-1.0) ** (rows - pos)
+    back = np.concatenate([cos_back, sin_back], 1) / size
+    return forward.astype(ml_dtypes.bfloat16), back.astype(ml_dtypes.bfloat16)
+
+
+CHIP, CORE, OUTER, BLOCKS = 0, 1, 2, 3
+ANY = pl.BlockSpec(memory_space=pl.ANY)
+VMEM = pl.BlockSpec(memory_space=pltpu.VMEM)
+
+
+def call(kernel, ids, args, in_specs, outs, out_specs, name, scratch=(), flops=0, moved=0, limit=16):
+    return pl.pallas_call(
+        kernel,
+        grid_spec=pltpu.PrefetchScalarGridSpec(
+            num_scalar_prefetch=1,
+            grid=(1,),
+            in_specs=in_specs,
+            out_specs=out_specs,
+            scratch_shapes=scratch,
+        ),
+        out_shape=outs,
+        compiler_params=pltpu.CompilerParams(vmem_limit_bytes=limit * 2**20),
+        cost_estimate=pl.CostEstimate(flops=flops, bytes_accessed=moved, transcendentals=0),
+        name=name,
+    )(ids, *args)
+
+
+def whole(x):
+    return pl.BlockSpec(x.shape, lambda *_: (0,) * len(x.shape))
+
+
+def array(shape, dtype=jnp.bfloat16):
+    return jax.ShapeDtypeStruct(shape, dtype)
+
+
+def place(ids, k, core, width):
+    return pl.multiple_of(((ids[CHIP] ^ k) * 2 + core) * width, width)
+
+
+def load_kernel(chips, ids, weight, grad, held, second, sem):
+    width = held.shape[1]
+    copies = []
+    for b in range(4):
+        depth = held.shape[2] // 4
+        at = pl.multiple_of(ids[BLOCKS + b] * depth, depth)
+        for k in range(chips):
+            rows = pl.ds(place(ids, k, ids[CORE], width), width)
+            copies.append(
+                pltpu.make_async_copy(
+                    weight.at[rows, pl.ds(at, depth)],
+                    held.at[k, :, pl.ds(b * depth, depth)],
+                    sem.at[b * chips + k],
+                )
+            )
+    half = second.shape[0]
+    copies.append(pltpu.make_async_copy(grad.at[pl.ds(half, half)], second, sem.at[4 * chips]))
+    for copy in copies:
+        copy.start()
+    for copy in copies:
+        copy.wait()
+
+
+def load(ids, weight, grad, chips):
+    width = weight.shape[0] // (2 * chips)
+    held = (chips, width, weight.shape[1])
+    second = (grad.shape[0] // 2, grad.shape[1])
+    return call(
+        functools.partial(load_kernel, chips),
+        ids,
+        (weight, grad),
+        [ANY, ANY],
+        [pltpu.VMEM(held, weight.dtype), array(second)],
+        [VMEM, ANY],
+        "load_weight",
+        [pltpu.SemaphoreType.DMA((4 * chips + 1,))],
+        moved=2 * math.prod(held),
+    )
+
+
+def pack_kernel(chips, ids, gate, key, value, taps, out):
+    width = out.shape[3]
+    for k in range(chips):
+        here = (slice(None), pl.ds(place(ids, k, 1 - ids[CORE], width), width))
+        out[0, k] = gate[here]
+        out[1, k] = taps[here]
+        out[2, k] = (key[here].astype(jnp.float32) * value[here].astype(jnp.float32)).astype(jnp.bfloat16)
+
+
+def pack(ids, gate, key, value, taps, chips):
+    rows, channels = key.shape
+    out = (3, chips, rows, channels // (2 * chips))
+    return call(
+        functools.partial(pack_kernel, chips),
+        ids,
+        (gate, key, value, taps),
+        [whole(key)] * 4,
+        array(out),
+        whole(array(out)),
+        "pack_core",
+        moved=8 * key.size,
+    )
+
+
+def merge_kernel(chips, ids, gate, key, value, taps, other, gates, *outs):
+    width = other.shape[3]
+    mine, theirs = ids[CORE], 1 - ids[CORE]
+    for k, out in enumerate(outs):
+        here = (slice(None), pl.ds(place(ids, k, mine, width), width))
+        gates[k, 0] = gate[here]
+        gates[k, 1] = other[0, k]
+        out[0, mine] = taps[here]
+        out[0, theirs] = other[1, k]
+        out[1, mine] = (key[here].astype(jnp.float32) * value[here].astype(jnp.float32)).astype(jnp.bfloat16)
+        out[1, theirs] = other[2, k]
+
+
+def merge(ids, gate, key, value, taps, other, chips):
+    rows, channels = key.shape
+    width = channels // (2 * chips)
+    piece = array((2, 2, rows, width))
+    gates = array((chips, 2, rows, width))
+    out = call(
+        functools.partial(merge_kernel, chips),
+        ids,
+        (gate, key, value, taps, other),
+        [whole(key)] * 4 + [whole(other)],
+        [gates] + [piece] * chips,
+        [whole(gates)] + [whole(piece)] * chips,
+        "merge_cores",
+        moved=12 * key.size,
+    )
+    return out[0], out[1:]
+
+
+def contract(x, w):
+    return lax.dot_general(x, w, (((1,), (1,)), ((), ())), preferred_element_type=jnp.float32)
+
+
+def fetch(ids, groups, x, sem):
+    rows = groups[0][0].shape[0]
+    for i, group in enumerate(groups):
+        to = x.at[pl.ds(i * rows, rows)]
+        for j, ref in enumerate(group):
+            copy = pltpu.make_async_copy(ref, to, sem.at[i])
+            if len(group) == 1:
+                copy.start()
+            else:
+                pl.when(ids[OUTER] == 1 - j)(copy.start)
+    for i, group in enumerate(groups):
+        pltpu.make_async_copy(group[0], x.at[pl.ds(i * rows, rows)], sem.at[i]).wait()
+
+
+def grouped(refs, sizes):
+    refs = list(refs)
+    return [[refs.pop(0) for _ in range(s)] for s in sizes]
+
+
+def mix_kernel(block, sizes, has_total, ids, *refs):
+    count = sum(sizes)
+    groups = grouped(refs[:count], sizes)
+    held, *rest = refs[count:]
+    total, out, x, sem = rest if has_total else (None, *rest)
+    depth = x.shape[1]
+    fetch(ids, groups, x, sem)
+
+    @pl.loop(0, held.shape[0])
+    def _(k):
+        value = contract(x[...], held[k, :, block * depth : (block + 1) * depth])
+        out[k] = value + total[k] if has_total else value
+
+
+def mix(ids, block, groups, held, total):
+    chips, width, _ = held.shape
+    sizes = [len(g) for g in groups]
+    flat = [x for g in groups for x in g]
+    rows = sum(g[0].shape[0] for g in groups)
+    depth = flat[0].shape[1]
+    out = (chips, rows, width)
+    return call(
+        functools.partial(mix_kernel, block, sizes, total is not None),
+        ids,
+        (*flat, held) + ((total,) if total is not None else ()),
+        [ANY] * len(flat) + [VMEM] + ([VMEM] if total is not None else []),
+        pltpu.VMEM(out, jnp.float32),
+        VMEM,
+        "mix",
+        [pltpu.VMEM((rows, depth), jnp.bfloat16), pltpu.SemaphoreType.DMA((len(groups),))],
+        flops=2 * rows * depth * chips * width,
+    )
+
+
+def gate_kernel(chunk, parts, sizes, ids, *refs):
+    count = sum(sizes)
+    groups = grouped(refs[:count], sizes)
+    held, total, gates, *outs, x, sem = refs[count:]
+    depth = x.shape[1]
+    rows = x.shape[0] // 2
+    own_rows = rows * parts
+    fetch(ids, groups, x, sem)
+    for k, out in enumerate(outs):
+        value = contract(x[...], held[k, :, 3 * depth : 4 * depth])
+        for h, core in enumerate((ids[CORE], 1 - ids[CORE])):
+            at = 2 * rows * chunk + h * rows
+            mixed = total[k, at : at + rows] + value[h * rows : (h + 1) * rows]
+            gate = gates[k, h, chunk * rows : (chunk + 1) * rows].astype(jnp.float32)
+            out[core] = (mixed * gate).astype(jnp.bfloat16)
+
+
+def mix_gate(ids, chunk, parts, groups, held, total, gates):
+    chips, width, _ = held.shape
+    sizes = [len(g) for g in groups]
+    flat = [x for g in groups for x in g]
+    rows, depth = flat[0].shape
+    piece = array((2, rows, width))
+    return call(
+        functools.partial(gate_kernel, chunk, parts, sizes),
+        ids,
+        (*flat, held, total, gates),
+        [ANY] * len(flat) + [VMEM, VMEM, whole(gates)],
+        [piece] * chips,
+        [whole(piece)] * chips,
+        "mix_gate",
+        [pltpu.VMEM((2 * rows, depth), jnp.bfloat16), pltpu.SemaphoreType.DMA((len(groups),))],
+        flops=4 * rows * depth * chips * width,
+    )
+
+
+def tap_kernel(ids, forward, *refs):
+    *pieces, out, spec = refs
+    segs = len(pieces)
+    seg = forward.shape[1]
+    width = pieces[0].shape[3]
+    row = lax.broadcasted_iota(jnp.int32, (2 * seg, width), 0)
+    sign = jnp.where(row % 2 == 0, 1.0, -1.0)
+    for x in range(2):
+        for k, piece in enumerate(pieces):
+            block = piece[x].reshape(seg, width)
+            spec[ids[CHIP] ^ k] = jnp.dot(forward[...], block, preferred_element_type=jnp.float32)
+        for r in range(segs):
+            kern = sign * spec[r]
+            if r:
+                kern += spec[r - 1]
+            out[x, r] = kern.astype(jnp.bfloat16)
+
+
+def tap_kernels(ids, forward, pieces):
+    segs = len(pieces)
+    width = pieces[0].shape[3]
+    shape = (2, segs, *forward.shape[:1], width)
+    return call(
+        tap_kernel,
+        ids,
+        (forward, *pieces),
+        [whole(forward)] + [whole(p) for p in pieces],
+        pltpu.VMEM(shape, jnp.bfloat16),
+        VMEM,
+        "kernels",
+        [pltpu.VMEM(shape[1:], jnp.float32)],
+        flops=2 * math.prod(shape) * forward.shape[1],
+    )
+
+
+def correlate_kernel(parts, ids, forward, back, kern, *refs):
+    segs = kern.shape[1]
+    n = 2 * segs
+    pieces = refs[: segs * parts]
+    outs = refs[segs * parts : segs * parts + n]
+    data, spec, acc, result = refs[segs * parts + n :]
+    part = pieces[0].shape[1]
+    rows = part * parts
+    seg = 2 * rows
+    width = data.shape[2]
+    for k in range(segs):
+        for c in range(parts):
+            for core in range(2):
+                at = core * rows + c * part
+                data[ids[CHIP] ^ k, at : at + part] = pieces[k * parts + c][core]
+    for i in range(segs):
+        spec[i] = jnp.dot(forward[...], data[i], preferred_element_type=jnp.float32)
+
+    tile = 16
+
+    def products(x, row, lane, first):
+        here = (pl.ds(row, tile), pl.ds(lane, LANES))
+        there = (pl.ds(row + seg, tile), pl.ds(lane, LANES))
+        g_real = [spec[(i, *here)] for i in range(segs)]
+        g_imag = [spec[(i, *there)] for i in range(segs)]
+        k_real = [kern[(x, r, *here)].astype(jnp.float32) for r in range(segs)]
+        k_imag = [kern[(x, r, *there)].astype(jnp.float32) for r in range(segs)]
+        if first:
+            edge = lax.broadcasted_iota(jnp.int32, (tile, LANES), 0) == 0
+        for j in range(segs):
+            both = sum(g_real[i] * k_real[i - j] for i in range(j, segs))
+            other = sum(g_imag[i] * k_imag[i - j] for i in range(j, segs))
+            cross = sum(g_imag[i] * k_real[i - j] - g_real[i] * k_imag[i - j] for i in range(j, segs))
+            if first:
+                real = both + jnp.where(edge, 0.0, other)
+                cross = jnp.where(edge, other, cross)
+            else:
+                real = both + other
+            acc[(j, *here)] = real.astype(jnp.bfloat16)
+            acc[(j, *there)] = cross.astype(jnp.bfloat16)
+
+    for x in range(2):
+        for lane in range(0, width, LANES):
+            products(x, 0, lane, True)
+
+            @pl.loop(1, seg // tile)
+            def _(t):
+                products(x, pl.multiple_of(t * tile, tile), lane, False)
+
+        for j in range(segs):
+            value = jnp.dot(back[...], acc[j], preferred_element_type=jnp.float32).astype(jnp.bfloat16)
+            for core in range(2):
+                result[2 * j + core, x] = value[core * rows : (core + 1) * rows]
+    me = 2 * ids[CHIP] + ids[CORE]
+    for k in range(n):
+        outs[k][...] = result[me ^ k]
+
+
+def correlate(ids, forward, back, kern, pieces):
+    segs, parts = len(pieces), len(pieces[0])
+    flat = [p for group in pieces for p in group]
+    width = flat[0].shape[2]
+    rows = flat[0].shape[1] * parts
+    seg = 2 * rows
+    n = 2 * segs
+    out = array((2, rows, width))
+    return call(
+        functools.partial(correlate_kernel, parts),
+        ids,
+        (forward, back, kern, *flat),
+        [whole(forward), whole(back), VMEM] + [whole(p) for p in flat],
+        [out] * n,
+        [whole(out)] * n,
+        "correlate",
+        [
+            pltpu.VMEM((segs, seg, width), jnp.bfloat16),
+            pltpu.VMEM((segs, 2 * seg, width), jnp.float32),
+            pltpu.VMEM((segs, 2 * seg, width), jnp.bfloat16),
+            pltpu.VMEM((n, *out.shape), jnp.bfloat16),
+        ],
+        flops=2 * segs * seg * seg * 2 * width * 3,
+    )
+
+
+def finish_kernel(factor, ids, key, value, *refs):
+    n = len(refs) - 11
+    pieces = refs[:n]
+    outs = refs[n : n + 3]
+    key_v, value_v, piece_v, key_o, value_o, filter_o, in_sem, out_sem = refs[n + 3 :]
+    width = piece_v.shape[3]
+    me = 2 * ids[CHIP] + ids[CORE]
+    loads = [pltpu.make_async_copy(p, piece_v.at[k], in_sem.at[k]) for k, p in enumerate(pieces)]
+    loads += [pltpu.make_async_copy(key, key_v, in_sem.at[n]), pltpu.make_async_copy(value, value_v, in_sem.at[n + 1])]
+    for copy in loads[::-1]:
+        copy.start()
+    for copy in loads[n:]:
+        copy.wait()
+    stores = []
+    for k in range(n):
+        here = (slice(None), pl.ds(pl.multiple_of((me ^ k) * width, width), width))
+        loads[k].wait()
+        conv_grad = piece_v[k, 0].astype(jnp.float32)
+        key_o[here] = (conv_grad * value_v[here].astype(jnp.float32)).astype(jnp.bfloat16)
+        value_o[here] = (conv_grad * key_v[here].astype(jnp.float32)).astype(jnp.bfloat16)
+        filter_o[here] = piece_v[k, 1].astype(jnp.float32) * factor
+        for o, (src, dst) in enumerate(zip((key_o, value_o, filter_o), outs)):
+            stores.append(pltpu.make_async_copy(src.at[here], dst.at[here], out_sem.at[o, k]))
+            stores[-1].start()
+    for copy in stores:
+        copy.wait()
+
+
+def finish(ids, key, value, pieces, factor):
+    n = len(pieces)
+    outs = [array(key.shape), array(key.shape), array(key.shape, jnp.float32)]
+    return call(
+        functools.partial(finish_kernel, factor),
+        ids,
+        (key, value, *pieces),
+        [ANY] * (2 + n),
+        outs,
+        [ANY] * 3,
+        "finish",
+        [
+            pltpu.VMEM(key.shape, key.dtype),
+            pltpu.VMEM(key.shape, key.dtype),
+            pltpu.VMEM((n, *pieces[0].shape), pieces[0].dtype),
+            *[pltpu.VMEM(o.shape, o.dtype) for o in outs],
+            pltpu.SemaphoreType.DMA((n + 2,)),
+            pltpu.SemaphoreType.DMA((3, n)),
+        ],
+        moved=12 * key.size,
+    )
+
+
+def swap(x, k, n):
+    return lax.ppermute(x, "seq", [(i, i ^ k) for i in range(n)]) if k else x
+
+
+def fast_shards(grad_out, out_weight, query_gate, key_branch, value_branch, filter_taps):
+    n = lax.axis_size("seq")
+    planes = lax.axis_size("ch")
+    me = lax.axis_index("seq")
+    plane = lax.axis_index("ch")
+    rows = grad_out.shape[0]
+    chips = n // 2
+    factor = 1.0 / math.sqrt(rows * n)
+    forward, back = half_tables(2 * rows)
+    low = plane < planes // 2
+    ids = jnp.stack(
+        [
+            me // 2,
+            me % 2,
+            jnp.where((plane == 0) | (plane == planes - 1), 1, 0),
+            plane,
+            plane ^ 1,
+            jnp.where(low, 2, 1),
+            jnp.where(low, 3, 0),
+        ]
+    ).astype(jnp.int32)
+
+    outer = [(i, i ^ 1) for i in range(planes)]
+    inner = []
+    for s in range(n):
+        inner += [(s * planes + 1, s * planes + 2), (s * planes + 2, s * planes + 1)]
+        inner += [(s * planes + z, (s ^ 1) * planes + z) for z in (0, planes - 1)]
+
+    def send_outer(x):
+        return lax.ppermute(x, "ch", outer)
+
+    def send_inner(x):
+        return lax.ppermute(x, ("seq", "ch"), inner)
+
+    def both(*candidates):
+        return [list(candidates), [swap(x, 1, n) for x in candidates]]
+
+    held, second = load(ids, out_weight, grad_out, chips)
+    own = [grad_out[: rows // CHUNKS], second]
+    outer_0 = [send_outer(x) for x in own]
+    inner_0 = [send_inner(x) for x in own]
+    outer_1 = [send_outer(x) for x in inner_0]
+    inner_1 = [send_inner(x) for x in outer_0]
+    outer_2 = [send_outer(x) for x in inner_1]
+
+    other = swap(pack(ids, query_gate, key_branch, value_branch, filter_taps, chips), 1, n)
+    gates, taps_input = merge(ids, query_gate, key_branch, value_branch, filter_taps, other, chips)
+    taps_input = [swap(x, 2 * k, n) for k, x in enumerate(taps_input)]
+
+    total = mix(ids, 0, [g for x in own for g in both(x)], held, None)
+    total = mix(ids, 1, [g for x in outer_0 for g in both(x)], held, total)
+    total = mix(ids, 2, [g for x in zip(outer_1, inner_0) for g in both(*x)], held, total)
+    kern = tap_kernels(ids, forward, taps_input)
+    gated = []
+    for c, x in enumerate(zip(outer_2, inner_1)):
+        pieces = mix_gate(ids, c, CHUNKS, both(*x), held, total, gates)
+        gated.append([swap(p, 2 * k, n) for k, p in enumerate(pieces)])
+    results = correlate(ids, forward, back, kern, list(zip(*gated)))
+    results = [swap(x, k, n) for k, x in enumerate(results)]
+    return finish(ids, key_branch, value_branch, results, factor)
+
+
 def solution(mesh):
-    return jax.shard_map(
-        shards,
+    specs = dict(
         mesh=mesh,
         in_specs=(
             P("seq", "ch"),
@@ -143,3 +625,11 @@
         out_specs=(P("seq", "ch"), P("seq", "ch"), P("seq", "ch")),
         check_vma=False,
     )
+    n, planes = mesh.shape["seq"], mesh.shape["ch"]
+
+    def step(*arrays):
+        whole_tiles = arrays[1].shape[0] // planes % (n * LANES) == 0
+        fits = whole_tiles and planes == 4 and n & (n - 1) == 0
+        return jax.shard_map(fast_shards if fits else shards, **specs)(*arrays)
+
+    return step

time: 466 us -> 102 us (0.22)
  local copies, waits for them, and re-layouts: 142 us -> 1.18 us
  matrix products: 129 us -> 0 us
  waiting for transfers between devices: 113 us -> 42.8 us
  other arithmetic: 60.5 us -> 0 us
  Pallas kernels: 0 us -> 29.6 us
  starting transfers between devices: 0.16 us -> 27.4 us
  between operations: 13.9 us -> 0.88 us
  loops' own time: 5.33 us -> 0 us
    dot_general x11 -> x0, matrix products: 129 us -> none  [the longest x3 37.4 us: spectra(): jnp.einsum('qk,rkb->rqb', sine_forward, block_list, preferred_element_typ...]
    all_gather x3 -> x0, waiting for transfers between devices: 65.6 us -> none  [the longest x1 49.5 us: shards(): lax.all_gather(grad_out, 'ch', axis=1, tiled=True)]
    gather x4 -> x0, local copies, waits for them, and re-layouts: 60.4 us -> none  [the longest x2 30.2 us: shards(): lag_ksin = jnp.take(kern_sin, lag_clip, axis=0)]
    reduce_scatter x1 -> x0, waiting for transfers between devices: 46.2 us -> none  [shards(): lax.psum_scatter(buffer[seg_len:].astype(jnp.bfloat16), 'seq', scatter_di...]
    dynamic_slice x24 -> x0, local copies, waits for them, and re-layouts: 44.4 us -> none  [the longest x16 39.8 us: place(): windows[item_index]]
    ppermute x0 -> x39, waiting for transfers between devices: none -> 42.8 us  [the longest x6 28.3 us: send_outer(): return lax.ppermute(x, 'ch', outer)]
    slice x3 -> x1, local copies, waits for them, and re-layouts: 32.4 us -> 0.02 us  [fast_shards(): own = [grad_out[:rows // CHUNKS], second]]
    add x1 -> x0, other arithmetic: 32.3 us -> none  [shards(): jnp.concatenate([jnp.zeros_like(tap_cos[:1]), tap_cos[:-1]], 0)]
  transfers between devices with their start and end apart: 4 -> 39, of which waited for: 3 -> 11; matrix products, arithmetic and copies ran while one was open for 36% -> 0% of each run, Pallas kernels for 0% -> 15%
where the time goes in v2:
time: 102 us
  waiting for transfers between devices  42.8 us (42%)
  Pallas kernels  29.6 us (29%)
  starting transfers between devices  27.4 us (27%)
  local copies, waits for them, and re-layouts  1.18 us (1%)
    pallas_call x11, Pallas kernels, call(): pl.pallas_call(kernel, grid_spec=pltpu.PrefetchScalarGridSpec(num_scalar_...  29.6 us
    ppermute x6, waiting for transfers between devices, send_outer(): return lax.ppermute(x, 'ch', outer)  28.3 us
    ppermute x29, starting transfers between devices, swap(): return lax.ppermute(x, 'seq', [(i, i ^ k) for i in range(n)]) if k else x  17.4 us
    ppermute x29, waiting for transfers between devices, swap(): return lax.ppermute(x, 'seq', [(i, i ^ k) for i in range(n)]) if k else x  14.4 us
    ppermute x6, starting transfers between devices, send_outer(): return lax.ppermute(x, 'ch', outer)  9.28 us
  transfers between devices with their start and end apart: 39, of which 11 were waited for; matrix products, arithmetic and copies ran while one was open for 0% of the time, Pallas kernels for 15%

profile of v2, /device:TPU:0, one launch (start us, length us, event | category | flops | bytes accessed | tf_op | source)
XLA Modules:
  0.0 101.9 jit_solution(5421500894876031434)
XLA Ops:
  0.8 1.0 %copy-done.4 = bf16[128,2048]{1,0:T(8,128)(2,1)S(1)} copy-done((bf16[128,2048]{1,0:T(8,128)(2,1)S(1)}, bf16[128,2048]{1,0:T(8,128)(2,1)}, u32[]{:S(2)}) %copy-start.4) | copy-done | bytes 524312
  1.8 6.6 %load_weight.1 = (bf16[4,256,8192]{2,1,0:T(8,128)(2,1)S(1)}, bf16[64,2048]{1,0:T(8,128)(2,1)S(1)}) custom-call(s32[7]{0:T(128)S(1)} %stack.31.ids, bf16[2048,8192]{1,0:T(8,128)(2,1)} %weight.1, bf16[128,2048]{1,0:T(8,128)(2,1)S(1)} %copy-done.4), custom_call_target="tpu_custom_call" | custom-call | bytes 16777216 | tf_op jit(solution)/shard_map/load_weight/pallas_call | solution.py:162
  8.9 2.6 %collective-permute-start.18 = (bf16[64,2048]{1,0:T(8,128)(2,1)S(1)}, bf16[64,2048]{1,0:T(8,128)(2,1)S(1)}, u32[]{:S(2)}, u32[]{:S(2)}) collective-permute-start(bf16[64,2048]{1,0:T(8,128)(2,1)S(1)} %get-tuple-element.31.refs_2_), channel_id=1, source_target_pairs={{0,1},{1,0},{2,3},{3,2},{4,5},{5,4},{6,7},{7,6},{8,9},{9,8},{10,11... | collective-permute-start | bytes 786440 | tf_op jit(solution)/shard_map/ppermute | solution.py:581
  12.4 6.3 %collective-permute-done.18.refs_2_ = bf16[64,2048]{1,0:T(8,128)(2,1)S(1)} collective-permute-done((bf16[64,2048]{1,0:T(8,128)(2,1)S(1)}, bf16[64,2048]{1,0:T(8,128)(2,1)S(1)}, u32[]{:S(2)}, u32[]{:S(2)}) %collective-permute-start.18) | collective-permute-done | bytes 262176 | tf_op jit(solution)/shard_map/ppermute | solution.py:581
  18.7 5.4 %collective-permute-done.4.refs_0_ = bf16[64,2048]{1,0:T(8,128)(2,1)S(1)} collective-permute-done((bf16[64,2048]{1,0:T(8,128)(2,1)S(1)}, bf16[64,2048]{1,0:T(8,128)(2,1)S(1)}, u32[]{:S(2)}, u32[]{:S(2)}) %collective-permute-start.4) | collective-permute-done | bytes 262176 | tf_op jit(solution)/shard_map/ppermute | solution.py:581
  25.4 1.8 %collective-permute-start.14 = (bf16[64,2048]{1,0:T(8,128)(2,1)S(1)}, bf16[64,2048]{1,0:T(8,128)(2,1)S(1)}, u32[]{:S(2)}, u32[]{:S(2)}) collective-permute-start(bf16[64,2048]{1,0:T(8,128)(2,1)S(1)} %collective-permute-done.13.refs_5_), channel_id=1, source_target_pairs={{0,1},{1,0},{2,3},{3,2},{4,5},{5,4},{6,7},{7,6},{8,9},{9,8},{10,11... | collective-permute-start | bytes 786440 | tf_op jit(solution)/shard_map/ppermute | solution.py:581
  28.3 6.3 %collective-permute-done.14.refs_4_ = bf16[64,2048]{1,0:T(8,128)(2,1)S(1)} collective-permute-done((bf16[64,2048]{1,0:T(8,128)(2,1)S(1)}, bf16[64,2048]{1,0:T(8,128)(2,1)S(1)}, u32[]{:S(2)}, u32[]{:S(2)}) %collective-permute-start.14) | collective-permute-done | bytes 262176 | tf_op jit(solution)/shard_map/ppermute | solution.py:581
  35.1 4.3 %collective-permute-done.10.refs_0_ = bf16[64,2048]{1,0:T(8,128)(2,1)S(1)} collective-permute-done((bf16[64,2048]{1,0:T(8,128)(2,1)S(1)}, bf16[64,2048]{1,0:T(8,128)(2,1)S(1)}, u32[]{:S(2)}, u32[]{:S(2)}) %collective-permute-start.10) | collective-permute-done | bytes 262176 | tf_op jit(solution)/shard_map/ppermute | solution.py:581
  39.3 1.7 %collective-permute-start.23 = (bf16[64,2048]{1,0:T(8,128)(2,1)S(1)}, bf16[64,2048]{1,0:T(8,128)(2,1)S(1)}, u32[]{:S(2)}, u32[]{:S(2)}) collective-permute-start(bf16[64,2048]{1,0:T(8,128)(2,1)S(1)} %collective-permute-done.22.refs_1_), channel_id=1, source_target_pairs={{0,1},{1,0},{2,3},{3,2},{4,5},{5,4},{6,7},{7,6},{8,9},{9,8},{10,11... | collective-permute-start | bytes 786440 | tf_op jit(solution)/shard_map/ppermute | solution.py:581
  41.1 2.2 %collective-permute-start.6 = (bf16[64,2048]{1,0:T(8,128)(2,1)S(1)}, bf16[64,2048]{1,0:T(8,128)(2,1)S(1)}, u32[]{:S(2)}, u32[]{:S(2)}) collective-permute-start(bf16[64,2048]{1,0:T(8,128)(2,1)S(1)} %collective-permute-done.5.refs_1_), channel_id=1, source_target_pairs={{0,1},{1,0},{2,3},{3,2},{4,5},{5,4},{6,7},{7,6},{8,9},{9,8},{10,11... | collective-permute-start | bytes 786440 | tf_op jit(solution)/shard_map/ppermute | solution.py:581
  43.8 4.7 %collective-permute-done.23.refs_0_ = bf16[64,2048]{1,0:T(8,128)(2,1)S(1)} collective-permute-done((bf16[64,2048]{1,0:T(8,128)(2,1)S(1)}, bf16[64,2048]{1,0:T(8,128)(2,1)S(1)}, u32[]{:S(2)}, u32[]{:S(2)}) %collective-permute-start.23) | collective-permute-done | bytes 262176 | tf_op jit(solution)/shard_map/ppermute | solution.py:581
  48.9 2.5 %mix.3.refs_5_ = f32[4,256,256]{2,1,0:T(8,128)S(1)} custom-call(s32[7]{0:T(128)S(1)} %stack.31.ids, bf16[64,2048]{1,0:T(8,128)(2,1)S(1)} %slice.3.refs_0_, bf16[64,2048]{1,0:T(8,128)(2,1)S(1)} %collective-permute-done.20.refs_1_, bf16[64,2048]{1,0:T(8,128)(2,1)S(1)} %get-tuple-element.31.refs_2_, bf16[64,2048]{1,0:T(8,128)(2,1)S(1)} %collective-permute-done.21.refs_3_, ...), custom_call_target="tpu_custom_call" | custom-call | flops 1073741824 | tf_op jit(solution)/shard_map/mix/pallas_call | solution.py:162
  52.2 1.4 %collective-permute-done.6.refs_0_ = bf16[64,2048]{1,0:T(8,128)(2,1)S(1)} collective-permute-done((bf16[64,2048]{1,0:T(8,128)(2,1)S(1)}, bf16[64,2048]{1,0:T(8,128)(2,1)S(1)}, u32[]{:S(2)}, u32[]{:S(2)}) %collective-permute-start.6) | collective-permute-done | bytes 262176 | tf_op jit(solution)/shard_map/ppermute | solution.py:581
  53.7 1.7 %collective-permute-start.1 = (bf16[2,2,128,256]{3,2,1,0:T(8,128)(2,1)S(1)}, bf16[2,2,128,256]{3,2,1,0:T(8,128)(2,1)S(1)}, u32[]{:S(2)}, u32[]{:S(2)}) collective-permute-start(bf16[2,2,128,256]{3,2,1,0:T(8,128)(2,1)S(1)} %get-tuple-element.27), channel_id=1, source_target_pairs={{0,8},{4,12},{8,0},{12,4},{16,24},{20,28},{24,16},{28,20},{1,9},{5... | collective-permute-start | bytes 786440 | tf_op jit(solution)/shard_map/ppermute | solution.py:549
  55.3 1.5 %collective-permute-start.2 = (bf16[2,2,128,256]{3,2,1,0:T(8,128)(2,1)S(1)}, bf16[2,2,128,256]{3,2,1,0:T(8,128)(2,1)S(1)}, u32[]{:S(2)}, u32[]{:S(2)}) collective-permute-start(bf16[2,2,128,256]{3,2,1,0:T(8,128)(2,1)S(1)} %get-tuple-element.28), channel_id=1, source_target_pairs={{0,16},{4,20},{8,24},{12,28},{16,0},{20,4},{24,8},{28,12},{1,17},{... | collective-permute-start | bytes 786440 | tf_op jit(solution)/shard_map/ppermute | solution.py:549
  57.2 2.5 %mix.4.refs_9_ = f32[4,256,256]{2,1,0:T(8,128)S(1)} custom-call(s32[7]{0:T(128)S(1)} %stack.31.ids, bf16[64,2048]{1,0:T(8,128)(2,1)S(1)} %collective-permute-done.4.refs_0_, bf16[64,2048]{1,0:T(8,128)(2,1)S(1)} %collective-permute-done.17.refs_1_, bf16[64,2048]{1,0:T(8,128)(2,1)S(1)} %collective-permute-done.18.refs_2_, ...), custom_call_target="tpu_custom_call" | custom-call | flops 1073741824 | tf_op jit(solution)/shard_map/mix/pallas_call | solution.py:162
  59.7 2.6 %mix.5.refs_5_ = f32[4,256,256]{2,1,0:T(8,128)S(1)} custom-call(s32[7]{0:T(128)S(1)} %stack.31.ids, bf16[64,2048]{1,0:T(8,128)(2,1)S(1)} %collective-permute-done.10.refs_0_, bf16[64,2048]{1,0:T(8,128)(2,1)S(1)} %collective-permute-done.9.refs_1_, bf16[64,2048]{1,0:T(8,128)(2,1)S(1)} %collective-permute-done.11.refs_2_, ...), custom_call_target="tpu_custom_call" | custom-call | flops 1073741824 | tf_op jit(solution)/shard_map/mix/pallas_call | solution.py:162
  62.3 2.2 %mix_gate.3 = (bf16[2,64,256]{2,1,0:T(8,128)(2,1)S(1)}, bf16[2,64,256]{2,1,0:T(8,128)(2,1)S(1)}, bf16[2,64,256]{2,1,0:T(8,128)(2,1)S(1)}, bf16[2,64,256]{2,1,0:T(8,128)(2,1)S(1)}) custom-call(s32[7]{0:T(128)S(1)} %stack.31.ids, bf16[64,2048]{1,0:T(8,128)(2,1)S(1)} %collective-permute-done.23.refs_0_, bf16[64,2048]{1,0:T(8,128)(2,1)S(1)} %collective-permute-done.22.refs_1_, ...), custom_call_target="tpu_custom_call" | custom-call | flops 536870912 | tf_op jit(solution)/shard_map/mix_gate/pallas_call | solution.py:162
  64.5 1.7 %collective-permute-start.27 = (bf16[2,64,256]{2,1,0:T(8,128)(2,1)S(1)}, bf16[2,64,256]{2,1,0:T(8,128)(2,1)S(1)}, u32[]{:S(2)}, u32[]{:S(2)}) collective-permute-start(bf16[2,64,256]{2,1,0:T(8,128)(2,1)S(1)} %get-tuple-element.36), channel_id=1, source_target_pairs={{0,8},{4,12},{8,0},{12,4},{16,24},{20,28},{24,16},{28,20},{1,9},{5... | collective-permute-start | bytes 196616 | tf_op jit(solution)/shard_map/ppermute | solution.py:549
  66.2 1.5 %collective-permute-start.29 = (bf16[2,64,256]{2,1,0:T(8,128)(2,1)S(1)}, bf16[2,64,256]{2,1,0:T(8,128)(2,1)S(1)}, u32[]{:S(2)}, u32[]{:S(2)}) collective-permute-start(bf16[2,64,256]{2,1,0:T(8,128)(2,1)S(1)} %get-tuple-element.38), channel_id=1, source_target_pairs={{0,16},{4,20},{8,24},{12,28},{16,0},{20,4},{24,8},{28,12},{1,17},{... | collective-permute-start | bytes 196616 | tf_op jit(solution)/shard_map/ppermute | solution.py:549
  67.8 2.1 %mix_gate.2 = (bf16[2,64,256]{2,1,0:T(8,128)(2,1)S(1)}, bf16[2,64,256]{2,1,0:T(8,128)(2,1)S(1)}, bf16[2,64,256]{2,1,0:T(8,128)(2,1)S(1)}, bf16[2,64,256]{2,1,0:T(8,128)(2,1)S(1)}) custom-call(s32[7]{0:T(128)S(1)} %stack.31.ids, bf16[64,2048]{1,0:T(8,128)(2,1)S(1)} %collective-permute-done.6.refs_0_, bf16[64,2048]{1,0:T(8,128)(2,1)S(1)} %collective-permute-done.5.refs_1_, ...), custom_call_target="tpu_custom_call" | custom-call | flops 536870912 | tf_op jit(solution)/shard_map/mix_gate/pallas_call | solution.py:162
  70.3 1.7 %collective-permute-start.26 = (bf16[2,64,256]{2,1,0:T(8,128)(2,1)S(1)}, bf16[2,64,256]{2,1,0:T(8,128)(2,1)S(1)}, u32[]{:S(2)}, u32[]{:S(2)}) collective-permute-start(bf16[2,64,256]{2,1,0:T(8,128)(2,1)S(1)} %get-tuple-element.35), channel_id=1, source_target_pairs={{0,8},{4,12},{8,0},{12,4},{16,24},{20,28},{24,16},{28,20},{1,9},{5... | collective-permute-start | bytes 196616 | tf_op jit(solution)/shard_map/ppermute | solution.py:549
  72.0 1.5 %collective-permute-start.28 = (bf16[2,64,256]{2,1,0:T(8,128)(2,1)S(1)}, bf16[2,64,256]{2,1,0:T(8,128)(2,1)S(1)}, u32[]{:S(2)}, u32[]{:S(2)}) collective-permute-start(bf16[2,64,256]{2,1,0:T(8,128)(2,1)S(1)} %get-tuple-element.37), channel_id=1, source_target_pairs={{0,16},{4,20},{8,24},{12,28},{16,0},{20,4},{24,8},{28,12},{1,17},{... | collective-permute-start | bytes 196616 | tf_op jit(solution)/shard_map/ppermute | solution.py:549
  73.8 2.0 %kernels.1.kern = bf16[2,4,512,256]{3,2,1,0:T(8,128)(2,1)S(1)} custom-call(s32[7]{0:T(128)S(1)} %stack.31.ids, bf16[512,256]{1,0:T(8,128)(2,1)S(1)} %copy-done.5, bf16[2,2,128,256]{3,2,1,0:T(8,128)(2,1)S(1)} %get-tuple-element.26.refs_0_, bf16[2,2,128,256]{3,2,1,0:T(8,128)(2,1)S(1)} %collective-permute-done.1.refs_1_, ...), custom_call_target="tpu_custom_call" | custom-call | flops 536870912 | tf_op jit(solution)/shard_map/kernels/pallas_call | solution.py:162
  76.8 1.9 %collective-permute-done.30.refs_6_ = bf16[2,64,256]{2,1,0:T(8,128)(2,1)S(1)} collective-permute-done((bf16[2,64,256]{2,1,0:T(8,128)(2,1)S(1)}, bf16[2,64,256]{2,1,0:T(8,128)(2,1)S(1)}, u32[]{:S(2)}, u32[]{:S(2)}) %collective-permute-start.30) | collective-permute-done | bytes 65568 | tf_op jit(solution)/shard_map/ppermute | solution.py:549
  78.7 4.1 %correlate.1 = (bf16[2,128,256]{2,1,0:T(8,128)(2,1)S(1)}, bf16[2,128,256]{2,1,0:T(8,128)(2,1)S(1)}, bf16[2,128,256]{2,1,0:T(8,128)(2,1)S(1)}, bf16[2,128,256]{2,...) custom-call(s32[7]{0:T(128)S(1)} %stack.31.ids, ...), custom_call_target="tpu_custom_call" | custom-call | flops 805306368 | tf_op jit(solution)/shard_map/correlate/pallas_call | solution.py:162
  83.4 1.3 %collective-permute-start.34 = (bf16[2,128,256]{2,1,0:T(8,128)(2,1)S(1)}, bf16[2,128,256]{2,1,0:T(8,128)(2,1)S(1)}, u32[]{:S(2)}, u32[]{:S(2)}) collective-permute-start(bf16[2,128,256]{2,1,0:T(8,128)(2,1)S(1)} %get-tuple-element.44), channel_id=1, source_target_pairs={{0,12},{4,8},{8,4},{12,0},{16,28},{20,24},{24,20},{28,16},{1,13},{... | collective-permute-start | bytes 393224 | tf_op jit(solution)/shard_map/ppermute | solution.py:549
  85.2 1.2 %collective-permute-start.36 = (bf16[2,128,256]{2,1,0:T(8,128)(2,1)S(1)}, bf16[2,128,256]{2,1,0:T(8,128)(2,1)S(1)}, u32[]{:S(2)}, u32[]{:S(2)}) collective-permute-start(bf16[2,128,256]{2,1,0:T(8,128)(2,1)S(1)} %get-tuple-element.46), channel_id=1, source_target_pairs={{0,20},{4,16},{8,28},{12,24},{16,4},{20,0},{24,12},{28,8},{1,21},{... | collective-permute-start | bytes 393224 | tf_op jit(solution)/shard_map/ppermute | solution.py:549
  86.7 2.5 %collective-permute-done.33.refs_2_ = bf16[2,128,256]{2,1,0:T(8,128)(2,1)S(1)} collective-permute-done((bf16[2,128,256]{2,1,0:T(8,128)(2,1)S(1)}, bf16[2,128,256]{2,1,0:T(8,128)(2,1)S(1)}, u32[]{:S(2)}, u32[]{:S(2)}) %collective-permute-start.33) | collective-permute-done | bytes 131104 | tf_op jit(solution)/shard_map/ppermute | solution.py:549
  89.2 1.9 %collective-permute-done.34.refs_3_ = bf16[2,128,256]{2,1,0:T(8,128)(2,1)S(1)} collective-permute-done((bf16[2,128,256]{2,1,0:T(8,128)(2,1)S(1)}, bf16[2,128,256]{2,1,0:T(8,128)(2,1)S(1)}, u32[]{:S(2)}, u32[]{:S(2)}) %collective-permute-start.34) | collective-permute-done | bytes 131104 | tf_op jit(solution)/shard_map/ppermute | solution.py:549
  91.1 7.2 %collective-permute-done.36.refs_5_ = bf16[2,128,256]{2,1,0:T(8,128)(2,1)S(1)} collective-permute-done((bf16[2,128,256]{2,1,0:T(8,128)(2,1)S(1)}, bf16[2,128,256]{2,1,0:T(8,128)(2,1)S(1)}, u32[]{:S(2)}, u32[]{:S(2)}) %collective-permute-start.36) | collective-permute-done | bytes 131104 | tf_op jit(solution)/shard_map/ppermute | solution.py:549
  98.3 3.6 %finish.1 = (bf16[128,2048]{1,0:T(8,128)(2,1)}, bf16[128,2048]{1,0:T(8,128)(2,1)}, f32[128,2048]{1,0:T(8,128)}) custom-call(s32[7]{0:T(128)S(1)} %stack.31.ids, bf16[128,2048]{1,0:T(8,128)(2,1)S(1)} %copy-done, bf16[128,2048]{1,0:T(8,128)(2,1)S(1)} %copy-done.1, bf16[2,128,256]{2,1,0:T(8,128)(2,1)S(1)} %get-tuple-element.41.refs_0_, ...), custom_call_target="tpu_custom_call" | custom-call | bytes 3145728 | tf_op jit(solution)/shard_map/finish/pallas_call | solution.py:162
  (73 shorter events, 9.6 us)
Async XLA Ops:
  8.9 9.8 %collective-permute-start.18 = (bf16[64,2048]{1,0:T(8,128)(2,1)S(1)}, bf16[64,2048]{1,0:T(8,128)(2,1)S(1)}, u32[]{:S(2)}, u32[]{:S(2)}) collective-permute-start(bf16[64,2048]{1,0:T(8,128)(2,1)S(1)} %get-tuple-element.31.refs_2_), channel_id=1, source_target_pairs={{0,1},{1,0},{2,3},{3,2},{4,5},{5,4},{6,7},{7,6},{8,9},{9,8},{10,11... | collective-permute-start | bytes 786440 | tf_op jit(solution)/shard_map/ppermute | solution.py:581
  11.6 12.5 %collective-permute-start.4 = (bf16[64,2048]{1,0:T(8,128)(2,1)S(1)}, bf16[64,2048]{1,0:T(8,128)(2,1)S(1)}, u32[]{:S(2)}, u32[]{:S(2)}) collective-permute-start(bf16[64,2048]{1,0:T(8,128)(2,1)S(1)} %slice.3.refs_0_), channel_id=1, source_target_pairs={{0,1},{1,0},{2,3},{3,2},{4,5},{5,4},{6,7},{7,6},{8,9},{9,8},{10,11... | collective-permute-start | bytes 786440 | tf_op jit(solution)/shard_map/ppermute | solution.py:581
  11.7 13.1 %collective-permute-start.20 = (bf16[64,2048]{1,0:T(8,128)(2,1)S(1)}, bf16[64,2048]{1,0:T(8,128)(2,1)S(1)}, u32[]{:S(2)}, u32[]{:S(2)}) collective-permute-start(bf16[64,2048]{1,0:T(8,128)(2,1)S(1)} %slice.3.refs_0_), channel_id=1, source_target_pairs={{0,4},{4,0},{8,12},{12,8},{16,20},{20,16},{24,28},{28,24},{1,5},{5... | collective-permute-start | bytes 786440 | tf_op jit(solution)/shard_map/ppermute | solution.py:549
  11.9 13.5 %collective-permute-start.13 = (bf16[64,2048]{1,0:T(8,128)(2,1)S(1)}, bf16[64,2048]{1,0:T(8,128)(2,1)S(1)}, u32[]{:S(2)}, u32[]{:S(2)}) collective-permute-start(bf16[64,2048]{1,0:T(8,128)(2,1)S(1)} %get-tuple-element.31.refs_2_), channel_id=1, source_target_pairs={{1,2},{2,1},{0,4},{3,7},{5,6},{6,5},{4,0},{7,3},{9,10},{10,9},{8,1... | collective-permute-start | bytes 786440 | tf_op jit(solution)/shard_map/ppermute | solution.py:584
  12.2 14.9 %collective-permute-start.9 = (bf16[64,2048]{1,0:T(8,128)(2,1)S(1)}, bf16[64,2048]{1,0:T(8,128)(2,1)S(1)}, u32[]{:S(2)}, u32[]{:S(2)}) collective-permute-start(bf16[64,2048]{1,0:T(8,128)(2,1)S(1)} %slice.3.refs_0_), channel_id=1, source_target_pairs={{1,2},{2,1},{0,4},{3,7},{5,6},{6,5},{4,0},{7,3},{9,10},{10,9},{8,1... | collective-permute-start | bytes 786440 | tf_op jit(solution)/shard_map/ppermute | solution.py:584
  18.7 8.4 %collective-permute-start.19 = (bf16[64,2048]{1,0:T(8,128)(2,1)S(1)}, bf16[64,2048]{1,0:T(8,128)(2,1)S(1)}, u32[]{:S(2)}, u32[]{:S(2)}) collective-permute-start(bf16[64,2048]{1,0:T(8,128)(2,1)S(1)} %collective-permute-done.18.refs_2_), channel_id=1, source_target_pairs={{0,4},{4,0},{8,12},{12,8},{16,20},{20,16},{24,28},{28,24},{1,5},{5... | collective-permute-start | bytes 786440 | tf_op jit(solution)/shard_map/ppermute | solution.py:549
  24.8 23.6 %collective-permute-start = (bf16[3,4,128,256]{3,2,1,0:T(8,128)(2,1)S(1)}, bf16[3,4,128,256]{3,2,1,0:T(8,128)(2,1)S(1)}, u32[]{:S(2)}, u32[]{:S(2)}) collective-permute-start(bf16[3,4,128,256]{3,2,1,0:T(8,128)(2,1)S(1)} %pack_core.1), channel_id=1, source_target_pairs={{0,4},{4,0},{8,12},{12,8},{16,20},{20,16},{24,28},{28,24},{1,5},{5... | collective-permute-start | bytes 2359304 | tf_op jit(solution)/shard_map/ppermute | solution.py:549
  25.4 9.2 %collective-permute-start.14 = (bf16[64,2048]{1,0:T(8,128)(2,1)S(1)}, bf16[64,2048]{1,0:T(8,128)(2,1)S(1)}, u32[]{:S(2)}, u32[]{:S(2)}) collective-permute-start(bf16[64,2048]{1,0:T(8,128)(2,1)S(1)} %collective-permute-done.13.refs_5_), channel_id=1, source_target_pairs={{0,1},{1,0},{2,3},{3,2},{4,5},{5,4},{6,7},{7,6},{8,9},{9,8},{10,11... | collective-permute-start | bytes 786440 | tf_op jit(solution)/shard_map/ppermute | solution.py:581
  27.1 7.4 %collective-permute-start.16 = (bf16[64,2048]{1,0:T(8,128)(2,1)S(1)}, bf16[64,2048]{1,0:T(8,128)(2,1)S(1)}, u32[]{:S(2)}, u32[]{:S(2)}) collective-permute-start(bf16[64,2048]{1,0:T(8,128)(2,1)S(1)} %collective-permute-done.13.refs_5_), channel_id=1, source_target_pairs={{0,4},{4,0},{8,12},{12,8},{16,20},{20,16},{24,28},{28,24},{1,5},{5... | collective-permute-start | bytes 786440 | tf_op jit(solution)/shard_map/ppermute | solution.py:549
  27.1 12.2 %collective-permute-start.10 = (bf16[64,2048]{1,0:T(8,128)(2,1)S(1)}, bf16[64,2048]{1,0:T(8,128)(2,1)S(1)}, u32[]{:S(2)}, u32[]{:S(2)}) collective-permute-start(bf16[64,2048]{1,0:T(8,128)(2,1)S(1)} %collective-permute-done.9.refs_1_), channel_id=1, source_target_pairs={{0,1},{1,0},{2,3},{3,2},{4,5},{5,4},{6,7},{7,6},{8,9},{9,8},{10,11... | collective-permute-start | bytes 786440 | tf_op jit(solution)/shard_map/ppermute | solution.py:581
  28.0 11.3 %collective-permute-start.22 = (bf16[64,2048]{1,0:T(8,128)(2,1)S(1)}, bf16[64,2048]{1,0:T(8,128)(2,1)S(1)}, u32[]{:S(2)}, u32[]{:S(2)}) collective-permute-start(bf16[64,2048]{1,0:T(8,128)(2,1)S(1)} %collective-permute-done.18.refs_2_), channel_id=1, source_target_pairs={{1,2},{2,1},{0,4},{3,7},{5,6},{6,5},{4,0},{7,3},{9,10},{10,9},{8,1... | collective-permute-start | bytes 786440 | tf_op jit(solution)/shard_map/ppermute | solution.py:584
  34.5 6.5 %collective-permute-start.5 = (bf16[64,2048]{1,0:T(8,128)(2,1)S(1)}, bf16[64,2048]{1,0:T(8,128)(2,1)S(1)}, u32[]{:S(2)}, u32[]{:S(2)}) collective-permute-start(bf16[64,2048]{1,0:T(8,128)(2,1)S(1)} %collective-permute-done.4.refs_0_), channel_id=1, source_target_pairs={{1,2},{2,1},{0,4},{3,7},{5,6},{6,5},{4,0},{7,3},{9,10},{10,9},{8,1... | collective-permute-start | bytes 786440 | tf_op jit(solution)/shard_map/ppermute | solution.py:584
  34.5 8.7 %collective-permute-start.12 = (bf16[64,2048]{1,0:T(8,128)(2,1)S(1)}, bf16[64,2048]{1,0:T(8,128)(2,1)S(1)}, u32[]{:S(2)}, u32[]{:S(2)}) collective-permute-start(bf16[64,2048]{1,0:T(8,128)(2,1)S(1)} %collective-permute-done.9.refs_1_), channel_id=1, source_target_pairs={{0,4},{4,0},{8,12},{12,8},{16,20},{20,16},{24,28},{28,24},{1,5},{5... | collective-permute-start | bytes 786440 | tf_op jit(solution)/shard_map/ppermute | solution.py:549
  39.3 9.1 %collective-permute-start.23 = (bf16[64,2048]{1,0:T(8,128)(2,1)S(1)}, bf16[64,2048]{1,0:T(8,128)(2,1)S(1)}, u32[]{:S(2)}, u32[]{:S(2)}) collective-permute-start(bf16[64,2048]{1,0:T(8,128)(2,1)S(1)} %collective-permute-done.22.refs_1_), channel_id=1, source_target_pairs={{0,1},{1,0},{2,3},{3,2},{4,5},{5,4},{6,7},{7,6},{8,9},{9,8},{10,11... | collective-permute-start | bytes 786440 | tf_op jit(solution)/shard_map/ppermute | solution.py:581
  41.1 12.6 %collective-permute-start.6 = (bf16[64,2048]{1,0:T(8,128)(2,1)S(1)}, bf16[64,2048]{1,0:T(8,128)(2,1)S(1)}, u32[]{:S(2)}, u32[]{:S(2)}) collective-permute-start(bf16[64,2048]{1,0:T(8,128)(2,1)S(1)} %collective-permute-done.5.refs_1_), channel_id=1, source_target_pairs={{0,1},{1,0},{2,3},{3,2},{4,5},{5,4},{6,7},{7,6},{8,9},{9,8},{10,11... | collective-permute-start | bytes 786440 | tf_op jit(solution)/shard_map/ppermute | solution.py:581
  43.2 10.4 %collective-permute-start.11 = (bf16[64,2048]{1,0:T(8,128)(2,1)S(1)}, bf16[64,2048]{1,0:T(8,128)(2,1)S(1)}, u32[]{:S(2)}, u32[]{:S(2)}) collective-permute-start(bf16[64,2048]{1,0:T(8,128)(2,1)S(1)} %collective-permute-done.10.refs_0_), channel_id=1, source_target_pairs={{0,4},{4,0},{8,12},{12,8},{16,20},{20,16},{24,28},{28,24},{1,5},{5... | collective-permute-start | bytes 786440 | tf_op jit(solution)/shard_map/ppermute | solution.py:549
  43.2 12.1 %collective-permute-start.25 = (bf16[64,2048]{1,0:T(8,128)(2,1)S(1)}, bf16[64,2048]{1,0:T(8,128)(2,1)S(1)}, u32[]{:S(2)}, u32[]{:S(2)}) collective-permute-start(bf16[64,2048]{1,0:T(8,128)(2,1)S(1)} %collective-permute-done.22.refs_1_), channel_id=1, source_target_pairs={{0,4},{4,0},{8,12},{12,8},{16,20},{20,16},{24,28},{28,24},{1,5},{5... | collective-permute-start | bytes 786440 | tf_op jit(solution)/shard_map/ppermute | solution.py:549
  48.4 8.4 %collective-permute-start.24 = (bf16[64,2048]{1,0:T(8,128)(2,1)S(1)}, bf16[64,2048]{1,0:T(8,128)(2,1)S(1)}, u32[]{:S(2)}, u32[]{:S(2)}) collective-permute-start(bf16[64,2048]{1,0:T(8,128)(2,1)S(1)} %collective-permute-done.23.refs_0_), channel_id=1, source_target_pairs={{0,4},{4,0},{8,12},{12,8},{16,20},{20,16},{24,28},{28,24},{1,5},{5... | collective-permute-start | bytes 786440 | tf_op jit(solution)/shard_map/ppermute | solution.py:549
  48.4 16.1 %collective-permute-start.8 = (bf16[64,2048]{1,0:T(8,128)(2,1)S(1)}, bf16[64,2048]{1,0:T(8,128)(2,1)S(1)}, u32[]{:S(2)}, u32[]{:S(2)}) collective-permute-start(bf16[64,2048]{1,0:T(8,128)(2,1)S(1)} %collective-permute-done.5.refs_1_), channel_id=1, source_target_pairs={{0,4},{4,0},{8,12},{12,8},{16,20},{20,16},{24,28},{28,24},{1,5},{5... | collective-permute-start | bytes 786440 | tf_op jit(solution)/shard_map/ppermute | solution.py:549
  53.7 12.6 %collective-permute-start.7 = (bf16[64,2048]{1,0:T(8,128)(2,1)S(1)}, bf16[64,2048]{1,0:T(8,128)(2,1)S(1)}, u32[]{:S(2)}, u32[]{:S(2)}) collective-permute-start(bf16[64,2048]{1,0:T(8,128)(2,1)S(1)} %collective-permute-done.6.refs_0_), channel_id=1, source_target_pairs={{0,4},{4,0},{8,12},{12,8},{16,20},{20,16},{24,28},{28,24},{1,5},{5... | collective-permute-start | bytes 786440 | tf_op jit(solution)/shard_map/ppermute | solution.py:549
  53.7 16.3 %collective-permute-start.1 = (bf16[2,2,128,256]{3,2,1,0:T(8,128)(2,1)S(1)}, bf16[2,2,128,256]{3,2,1,0:T(8,128)(2,1)S(1)}, u32[]{:S(2)}, u32[]{:S(2)}) collective-permute-start(bf16[2,2,128,256]{3,2,1,0:T(8,128)(2,1)S(1)} %get-tuple-element.27), channel_id=1, source_target_pairs={{0,8},{4,12},{8,0},{12,4},{16,24},{20,28},{24,16},{28,20},{1,9},{5... | collective-permute-start | bytes 786440 | tf_op jit(solution)/shard_map/ppermute | solution.py:549
  55.3 15.0 %collective-permute-start.2 = (bf16[2,2,128,256]{3,2,1,0:T(8,128)(2,1)S(1)}, bf16[2,2,128,256]{3,2,1,0:T(8,128)(2,1)S(1)}, u32[]{:S(2)}, u32[]{:S(2)}) collective-permute-start(bf16[2,2,128,256]{3,2,1,0:T(8,128)(2,1)S(1)} %get-tuple-element.28), channel_id=1, source_target_pairs={{0,16},{4,20},{8,24},{12,28},{16,0},{20,4},{24,8},{28,12},{1,17},{... | collective-permute-start | bytes 786440 | tf_op jit(solution)/shard_map/ppermute | solution.py:549
  56.8 15.1 %collective-permute-start.3 = (bf16[2,2,128,256]{3,2,1,0:T(8,128)(2,1)S(1)}, bf16[2,2,128,256]{3,2,1,0:T(8,128)(2,1)S(1)}, u32[]{:S(2)}, u32[]{:S(2)}) collective-permute-start(bf16[2,2,128,256]{3,2,1,0:T(8,128)(2,1)S(1)} %get-tuple-element.29), channel_id=1, source_target_pairs={{0,24},{4,28},{8,16},{12,20},{16,8},{20,12},{24,0},{28,4},{1,25},{... | collective-permute-start | bytes 786440 | tf_op jit(solution)/shard_map/ppermute | solution.py:549
  64.5 9.0 %collective-permute-start.27 = (bf16[2,64,256]{2,1,0:T(8,128)(2,1)S(1)}, bf16[2,64,256]{2,1,0:T(8,128)(2,1)S(1)}, u32[]{:S(2)}, u32[]{:S(2)}) collective-permute-start(bf16[2,64,256]{2,1,0:T(8,128)(2,1)S(1)} %get-tuple-element.36), channel_id=1, source_target_pairs={{0,8},{4,12},{8,0},{12,4},{16,24},{20,28},{24,16},{28,20},{1,9},{5... | collective-permute-start | bytes 196616 | tf_op jit(solution)/shard_map/ppermute | solution.py:549
  66.2 9.6 %collective-permute-start.29 = (bf16[2,64,256]{2,1,0:T(8,128)(2,1)S(1)}, bf16[2,64,256]{2,1,0:T(8,128)(2,1)S(1)}, u32[]{:S(2)}, u32[]{:S(2)}) collective-permute-start(bf16[2,64,256]{2,1,0:T(8,128)(2,1)S(1)} %get-tuple-element.38), channel_id=1, source_target_pairs={{0,16},{4,20},{8,24},{12,28},{16,0},{20,4},{24,8},{28,12},{1,17},{... | collective-permute-start | bytes 196616 | tf_op jit(solution)/shard_map/ppermute | solution.py:549
  69.9 5.9 %collective-permute-start.31 = (bf16[2,64,256]{2,1,0:T(8,128)(2,1)S(1)}, bf16[2,64,256]{2,1,0:T(8,128)(2,1)S(1)}, u32[]{:S(2)}, u32[]{:S(2)}) collective-permute-start(bf16[2,64,256]{2,1,0:T(8,128)(2,1)S(1)} %get-tuple-element.40), channel_id=1, source_target_pairs={{0,24},{4,28},{8,16},{12,20},{16,8},{20,12},{24,0},{28,4},{1,25},{... | collective-permute-start | bytes 196616 | tf_op jit(solution)/shard_map/ppermute | solution.py:549
  82.8 6.4 %collective-permute-start.33 = (bf16[2,128,256]{2,1,0:T(8,128)(2,1)S(1)}, bf16[2,128,256]{2,1,0:T(8,128)(2,1)S(1)}, u32[]{:S(2)}, u32[]{:S(2)}) collective-permute-start(bf16[2,128,256]{2,1,0:T(8,128)(2,1)S(1)} %get-tuple-element.43), channel_id=1, source_target_pairs={{0,8},{4,12},{8,0},{12,4},{16,24},{20,28},{24,16},{28,20},{1,9},{5... | collective-permute-start | bytes 393224 | tf_op jit(solution)/shard_map/ppermute | solution.py:549
  83.4 7.7 %collective-permute-start.34 = (bf16[2,128,256]{2,1,0:T(8,128)(2,1)S(1)}, bf16[2,128,256]{2,1,0:T(8,128)(2,1)S(1)}, u32[]{:S(2)}, u32[]{:S(2)}) collective-permute-start(bf16[2,128,256]{2,1,0:T(8,128)(2,1)S(1)} %get-tuple-element.44), channel_id=1, source_target_pairs={{0,12},{4,8},{8,4},{12,0},{16,28},{20,24},{24,20},{28,16},{1,13},{... | collective-permute-start | bytes 393224 | tf_op jit(solution)/shard_map/ppermute | solution.py:549
  84.7 6.4 %collective-permute-start.35 = (bf16[2,128,256]{2,1,0:T(8,128)(2,1)S(1)}, bf16[2,128,256]{2,1,0:T(8,128)(2,1)S(1)}, u32[]{:S(2)}, u32[]{:S(2)}) collective-permute-start(bf16[2,128,256]{2,1,0:T(8,128)(2,1)S(1)} %get-tuple-element.45), channel_id=1, source_target_pairs={{0,16},{4,20},{8,24},{12,28},{16,0},{20,4},{24,8},{28,12},{1,17},{... | collective-permute-start | bytes 393224 | tf_op jit(solution)/shard_map/ppermute | solution.py:549
  85.2 13.1 %collective-permute-start.36 = (bf16[2,128,256]{2,1,0:T(8,128)(2,1)S(1)}, bf16[2,128,256]{2,1,0:T(8,128)(2,1)S(1)}, u32[]{:S(2)}, u32[]{:S(2)}) collective-permute-start(bf16[2,128,256]{2,1,0:T(8,128)(2,1)S(1)} %get-tuple-element.46), channel_id=1, source_target_pairs={{0,20},{4,16},{8,28},{12,24},{16,4},{20,0},{24,12},{28,8},{1,21},{... | collective-permute-start | bytes 393224 | tf_op jit(solution)/shard_map/ppermute | solution.py:549
  86.4 11.9 %collective-permute-start.37 = (bf16[2,128,256]{2,1,0:T(8,128)(2,1)S(1)}, bf16[2,128,256]{2,1,0:T(8,128)(2,1)S(1)}, u32[]{:S(2)}, u32[]{:S(2)}) collective-permute-start(bf16[2,128,256]{2,1,0:T(8,128)(2,1)S(1)} %get-tuple-element.47), channel_id=1, source_target_pairs={{0,24},{4,28},{8,16},{12,20},{16,8},{20,12},{24,0},{28,4},{1,25},{... | collective-permute-start | bytes 393224 | tf_op jit(solution)/shard_map/ppermute | solution.py:549
  89.2 9.1 %collective-permute-start.38 = (bf16[2,128,256]{2,1,0:T(8,128)(2,1)S(1)}, bf16[2,128,256]{2,1,0:T(8,128)(2,1)S(1)}, u32[]{:S(2)}, u32[]{:S(2)}) collective-permute-start(bf16[2,128,256]{2,1,0:T(8,128)(2,1)S(1)} %get-tuple-element.48), channel_id=1, source_target_pairs={{0,28},{4,24},{8,20},{12,16},{16,12},{20,8},{24,4},{28,0},{1,29},{... | collective-permute-start | bytes 393224 | tf_op jit(solution)/shard_map/ppermute | solution.py:549
  (14 other events, 148.9 us)

commit v3 on v2

--- a/solution.py
+++ b/solution.py
@@ -153,26 +153,42 @@
     return forward.astype(ml_dtypes.bfloat16), back.astype(ml_dtypes.bfloat16)
 
 
-CHIP, CORE, OUTER, BLOCKS = 0, 1, 2, 3
 ANY = pl.BlockSpec(memory_space=pl.ANY)
 VMEM = pl.BlockSpec(memory_space=pltpu.VMEM)
-
-
-def call(kernel, ids, args, in_specs, outs, out_specs, name, scratch=(), flops=0, moved=0, limit=16):
+MARK = jax.ShapeDtypeStruct((8, LANES), jnp.float32)
+
+
+class Spot:
+    def __init__(self):
+        me, plane, planes = lax.axis_index("seq"), lax.axis_index("ch"), lax.axis_size("ch")
+        low = plane < planes // 2
+        self.chip, self.core = me // 2, me % 2
+        self.outer = (plane == 0) | (plane == planes - 1)
+        self.blocks = (plane, plane ^ 1, jnp.where(low, 2, 1), jnp.where(low, 3, 0))
+
+
+def call(kernel, args, in_specs, outs, out_specs, name, scratch=(), limit=24, flops=0, update=(), carry=(), after=()):
+    same = (*update, *carry)
+    count, results, written = len(args), len(outs), len(outs) + len(update)
+
+    def body(*refs):
+        rest = refs[count + len(same) + len(after) :]
+        mark, *scratch_refs = rest[results + len(same) :]
+        mark[...] = jnp.zeros_like(mark)
+        kernel(Spot(), *refs[:count], *rest[:written], *scratch_refs)
+
     return pl.pallas_call(
-        kernel,
-        grid_spec=pltpu.PrefetchScalarGridSpec(
-            num_scalar_prefetch=1,
-            grid=(1,),
-            in_specs=in_specs,
-            out_specs=out_specs,
-            scratch_shapes=scratch,
-        ),
-        out_shape=outs,
+        body,
+        input_output_aliases={count + i: results + i for i in range(len(same))},
+        grid=(1,),
+        in_specs=[*in_specs, *[ANY] * (len(same) + len(after))],
+        out_specs=[*out_specs, *[ANY] * len(same), whole(MARK)],
+        scratch_shapes=scratch,
+        out_shape=[*outs, *[array(x.shape, x.dtype) for x in same], MARK],
         compiler_params=pltpu.CompilerParams(vmem_limit_bytes=limit * 2**20),
-        cost_estimate=pl.CostEstimate(flops=flops, bytes_accessed=moved, transcendentals=0),
+        cost_estimate=pl.CostEstimate(flops=flops, bytes_accessed=0, transcendentals=0),
         name=name,
-    )(ids, *args)
+    )(*args, *same, *after)
 
 
 def whole(x):
@@ -183,18 +199,18 @@
     return jax.ShapeDtypeStruct(shape, dtype)
 
 
-def place(ids, k, core, width):
-    return pl.multiple_of(((ids[CHIP] ^ k) * 2 + core) * width, width)
-
-
-def load_kernel(chips, ids, weight, grad, held, second, sem):
+def place(spot, k, core, width):
+    return pl.multiple_of(((spot.chip ^ k) * 2 + core) * width, width)
+
+
+def load_kernel(chips, spot, weight, held, sem):
     width = held.shape[1]
+    depth = held.shape[2] // 4
     copies = []
     for b in range(4):
-        depth = held.shape[2] // 4
-        at = pl.multiple_of(ids[BLOCKS + b] * depth, depth)
+        at = pl.multiple_of(spot.blocks[b] * depth, depth)
         for k in range(chips):
-            rows = pl.ds(place(ids, k, ids[CORE], width), width)
+            rows = pl.ds(place(spot, k, spot.core, width), width)
             copies.append(
                 pltpu.make_async_copy(
                     weight.at[rows, pl.ds(at, depth)],
@@ -202,91 +218,106 @@
                     sem.at[b * chips + k],
                 )
             )
-    half = second.shape[0]
-    copies.append(pltpu.make_async_copy(grad.at[pl.ds(half, half)], second, sem.at[4 * chips]))
     for copy in copies:
         copy.start()
     for copy in copies:
         copy.wait()
 
 
-def load(ids, weight, grad, chips):
-    width = weight.shape[0] // (2 * chips)
-    held = (chips, width, weight.shape[1])
-    second = (grad.shape[0] // 2, grad.shape[1])
+def load(weight, chips, **order):
+    held = (chips, weight.shape[0] // (2 * chips), weight.shape[1])
     return call(
         functools.partial(load_kernel, chips),
-        ids,
-        (weight, grad),
-        [ANY, ANY],
-        [pltpu.VMEM(held, weight.dtype), array(second)],
-        [VMEM, ANY],
+        (weight,),
+        [ANY],
+        [pltpu.VMEM(held, weight.dtype)],
+        [VMEM],
         "load_weight",
-        [pltpu.SemaphoreType.DMA((4 * chips + 1,))],
-        moved=2 * math.prod(held),
-    )
-
-
-def pack_kernel(chips, ids, gate, key, value, taps, out):
-    width = out.shape[3]
-    for k in range(chips):
-        here = (slice(None), pl.ds(place(ids, k, 1 - ids[CORE], width), width))
-        out[0, k] = gate[here]
-        out[1, k] = taps[here]
-        out[2, k] = (key[here].astype(jnp.float32) * value[here].astype(jnp.float32)).astype(jnp.bfloat16)
-
-
-def pack(ids, gate, key, value, taps, chips):
+        [pltpu.SemaphoreType.DMA((4 * chips,))],
+        **order,
+    )
+
+
+def pack_kernel(chips, spot, gate, key, value, taps, mine, theirs_0, theirs_1, all_in, sem):
+    width = mine.shape[3]
+    half = theirs_0.shape[2]
+    loads = [pltpu.make_async_copy(ref, all_in.at[i], sem.at[i]) for i, ref in enumerate((gate, taps, key, value))]
+    for copy in loads:
+        copy.start()
+    for copy in loads:
+        copy.wait()
+    upper, lower = slice(0, half), slice(half, 2 * half)
+    for out, core, rows in (
+        (theirs_0, 1 - spot.core, upper),
+        (theirs_1, 1 - spot.core, lower),
+        (mine, spot.core, slice(None)),
+    ):
+        for k in range(chips):
+            here = (rows, pl.ds(place(spot, k, core, width), width))
+            out[0, k] = all_in[(0, *here)]
+            out[1, k] = all_in[(1, *here)]
+            product = all_in[(2, *here)].astype(jnp.float32) * all_in[(3, *here)].astype(jnp.float32)
+            out[2, k] = product.astype(jnp.bfloat16)
+
+
+def pack(gate, key, value, taps, chips, **order):
     rows, channels = key.shape
     out = (3, chips, rows, channels // (2 * chips))
+    half = array((3, chips, rows // 2, channels // (2 * chips)))
     return call(
         functools.partial(pack_kernel, chips),
-        ids,
         (gate, key, value, taps),
-        [whole(key)] * 4,
-        array(out),
-        whole(array(out)),
+        [ANY] * 4,
+        [pltpu.VMEM(out, jnp.bfloat16), half, half],
+        [VMEM, whole(half), whole(half)],
         "pack_core",
-        moved=8 * key.size,
-    )
-
-
-def merge_kernel(chips, ids, gate, key, value, taps, other, gates, *outs):
-    width = other.shape[3]
-    mine, theirs = ids[CORE], 1 - ids[CORE]
+        [pltpu.VMEM((4, rows, channels), jnp.bfloat16), pltpu.SemaphoreType.DMA((4,))],
+        limit=58,
+        **order,
+    )
+
+
+def merge_kernel(spot, mine, other_0, other_1, gates, *refs):
+    *outs, sem = refs
+    own, theirs = spot.core, 1 - spot.core
+    half = other_0.shape[2]
+    loads = []
+    for h, other in enumerate((other_0, other_1)):
+        rows = pl.ds(h * half, half)
+        for k, out in enumerate(outs):
+            for i, to in enumerate((gates.at[k, 1, rows], out.at[0, theirs, rows], out.at[1, theirs, rows])):
+                loads.append(pltpu.make_async_copy(other.at[i, k], to, sem.at[len(loads)]))
+    for copy in loads:
+        copy.start()
     for k, out in enumerate(outs):
-        here = (slice(None), pl.ds(place(ids, k, mine, width), width))
-        gates[k, 0] = gate[here]
-        gates[k, 1] = other[0, k]
-        out[0, mine] = taps[here]
-        out[0, theirs] = other[1, k]
-        out[1, mine] = (key[here].astype(jnp.float32) * value[here].astype(jnp.float32)).astype(jnp.bfloat16)
-        out[1, theirs] = other[2, k]
-
-
-def merge(ids, gate, key, value, taps, other, chips):
-    rows, channels = key.shape
-    width = channels // (2 * chips)
+        gates[k, 0] = mine[0, k]
+        out[0, own] = mine[1, k]
+        out[1, own] = mine[2, k]
+    for copy in loads:
+        copy.wait()
+
+
+def merge(mine, others, **order):
+    _, chips, rows, width = mine.shape
     piece = array((2, 2, rows, width))
-    gates = array((chips, 2, rows, width))
     out = call(
-        functools.partial(merge_kernel, chips),
-        ids,
-        (gate, key, value, taps, other),
-        [whole(key)] * 4 + [whole(other)],
-        [gates] + [piece] * chips,
-        [whole(gates)] + [whole(piece)] * chips,
+        merge_kernel,
+        (mine, *others),
+        [VMEM, ANY, ANY],
+        [pltpu.VMEM((chips, 2, rows, width), jnp.bfloat16)] + [piece] * chips,
+        [VMEM] + [whole(piece)] * chips,
         "merge_cores",
-        moved=12 * key.size,
-    )
-    return out[0], out[1:]
+        [pltpu.SemaphoreType.DMA((6 * chips,))],
+        **order,
+    )
+    return out[0], out[1 : 1 + chips], out[1 + chips :]
 
 
 def contract(x, w):
     return lax.dot_general(x, w, (((1,), (1,)), ((), ())), preferred_element_type=jnp.float32)
 
 
-def fetch(ids, groups, x, sem):
+def fetch(spot, groups, x, sem):
     rows = groups[0][0].shape[0]
     for i, group in enumerate(groups):
         to = x.at[pl.ds(i * rows, rows)]
@@ -295,7 +326,7 @@
             if len(group) == 1:
                 copy.start()
             else:
-                pl.when(ids[OUTER] == 1 - j)(copy.start)
+                pl.when(spot.outer if j == 0 else ~spot.outer)(copy.start)
     for i, group in enumerate(groups):
         pltpu.make_async_copy(group[0], x.at[pl.ds(i * rows, rows)], sem.at[i]).wait()
 
@@ -305,13 +336,13 @@
     return [[refs.pop(0) for _ in range(s)] for s in sizes]
 
 
-def mix_kernel(block, sizes, has_total, ids, *refs):
+def mix_kernel(block, sizes, has_total, spot, *refs):
     count = sum(sizes)
     groups = grouped(refs[:count], sizes)
     held, *rest = refs[count:]
     total, out, x, sem = rest if has_total else (None, *rest)
     depth = x.shape[1]
-    fetch(ids, groups, x, sem)
+    fetch(spot, groups, x, sem)
 
     @pl.loop(0, held.shape[0])
     def _(k):
@@ -319,7 +350,7 @@
         out[k] = value + total[k] if has_total else value
 
 
-def mix(ids, block, groups, held, total):
+def mix(block, groups, held, total, **order):
     chips, width, _ = held.shape
     sizes = [len(g) for g in groups]
     flat = [x for g in groups for x in g]
@@ -328,35 +359,34 @@
     out = (chips, rows, width)
     return call(
         functools.partial(mix_kernel, block, sizes, total is not None),
-        ids,
         (*flat, held) + ((total,) if total is not None else ()),
         [ANY] * len(flat) + [VMEM] + ([VMEM] if total is not None else []),
-        pltpu.VMEM(out, jnp.float32),
-        VMEM,
+        [pltpu.VMEM(out, jnp.float32)],
+        [VMEM],
         "mix",
         [pltpu.VMEM((rows, depth), jnp.bfloat16), pltpu.SemaphoreType.DMA((len(groups),))],
-        flops=2 * rows * depth * chips * width,
-    )
-
-
-def gate_kernel(chunk, parts, sizes, ids, *refs):
+        **order,
+    )
+
+
+def gate_kernel(chunk, parts, sizes, spot, *refs):
     count = sum(sizes)
     groups = grouped(refs[:count], sizes)
     held, total, gates, *outs, x, sem = refs[count:]
     depth = x.shape[1]
     rows = x.shape[0] // 2
     own_rows = rows * parts
-    fetch(ids, groups, x, sem)
+    fetch(spot, groups, x, sem)
     for k, out in enumerate(outs):
         value = contract(x[...], held[k, :, 3 * depth : 4 * depth])
-        for h, core in enumerate((ids[CORE], 1 - ids[CORE])):
-            at = 2 * rows * chunk + h * rows
+        for h, core in enumerate((spot.core, 1 - spot.core)):
+            at = h * own_rows + chunk * rows
             mixed = total[k, at : at + rows] + value[h * rows : (h + 1) * rows]
             gate = gates[k, h, chunk * rows : (chunk + 1) * rows].astype(jnp.float32)
             out[core] = (mixed * gate).astype(jnp.bfloat16)
 
 
-def mix_gate(ids, chunk, parts, groups, held, total, gates):
+def mix_gate(chunk, parts, groups, held, total, gates):
     chips, width, _ = held.shape
     sizes = [len(g) for g in groups]
     flat = [x for g in groups for x in g]
@@ -364,18 +394,16 @@
     piece = array((2, rows, width))
     return call(
         functools.partial(gate_kernel, chunk, parts, sizes),
-        ids,
         (*flat, held, total, gates),
-        [ANY] * len(flat) + [VMEM, VMEM, whole(gates)],
+        [ANY] * len(flat) + [VMEM] * 3,
         [piece] * chips,
         [whole(piece)] * chips,
         "mix_gate",
         [pltpu.VMEM((2 * rows, depth), jnp.bfloat16), pltpu.SemaphoreType.DMA((len(groups),))],
-        flops=4 * rows * depth * chips * width,
-    )
-
-
-def tap_kernel(ids, forward, *refs):
+    )
+
+
+def tap_kernel(spot, forward, *refs):
     *pieces, out, spec = refs
     segs = len(pieces)
     seg = forward.shape[1]
@@ -385,7 +413,7 @@
     for x in range(2):
         for k, piece in enumerate(pieces):
             block = piece[x].reshape(seg, width)
-            spec[ids[CHIP] ^ k] = jnp.dot(forward[...], block, preferred_element_type=jnp.float32)
+            spec[spot.chip ^ k] = jnp.dot(forward[...], block, preferred_element_type=jnp.float32)
         for r in range(segs):
             kern = sign * spec[r]
             if r:
@@ -393,24 +421,24 @@
             out[x, r] = kern.astype(jnp.bfloat16)
 
 
-def tap_kernels(ids, forward, pieces):
+def tap_kernels(forward, pieces, **order):
     segs = len(pieces)
     width = pieces[0].shape[3]
     shape = (2, segs, *forward.shape[:1], width)
     return call(
         tap_kernel,
-        ids,
         (forward, *pieces),
         [whole(forward)] + [whole(p) for p in pieces],
-        pltpu.VMEM(shape, jnp.bfloat16),
-        VMEM,
+        [pltpu.VMEM(shape, jnp.bfloat16)],
+        [VMEM],
         "kernels",
         [pltpu.VMEM(shape[1:], jnp.float32)],
-        flops=2 * math.prod(shape) * forward.shape[1],
-    )
-
-
-def correlate_kernel(parts, ids, forward, back, kern, *refs):
+        flops=12 * math.prod(shape) * forward.shape[1],
+        **order,
+    )
+
+
+def correlate_kernel(parts, spot, forward, back, kern, *refs):
     segs = kern.shape[1]
     n = 2 * segs
     pieces = refs[: segs * parts]
@@ -424,7 +452,7 @@
         for c in range(parts):
             for core in range(2):
                 at = core * rows + c * part
-                data[ids[CHIP] ^ k, at : at + part] = pieces[k * parts + c][core]
+                data[spot.chip ^ k, at : at + part] = pieces[k * parts + c][core]
     for i in range(segs):
         spec[i] = jnp.dot(forward[...], data[i], preferred_element_type=jnp.float32)
 
@@ -463,12 +491,12 @@
             value = jnp.dot(back[...], acc[j], preferred_element_type=jnp.float32).astype(jnp.bfloat16)
             for core in range(2):
                 result[2 * j + core, x] = value[core * rows : (core + 1) * rows]
-    me = 2 * ids[CHIP] + ids[CORE]
+    me = 2 * spot.chip + spot.core
     for k in range(n):
         outs[k][...] = result[me ^ k]
 
 
-def correlate(ids, forward, back, kern, pieces):
+def correlate(forward, back, kern, pieces):
     segs, parts = len(pieces), len(pieces[0])
     flat = [p for group in pieces for p in group]
     width = flat[0].shape[2]
@@ -478,7 +506,6 @@
     out = array((2, rows, width))
     return call(
         functools.partial(correlate_kernel, parts),
-        ids,
         (forward, back, kern, *flat),
         [whole(forward), whole(back), VMEM] + [whole(p) for p in flat],
         [out] * n,
@@ -490,59 +517,65 @@
             pltpu.VMEM((segs, 2 * seg, width), jnp.bfloat16),
             pltpu.VMEM((n, *out.shape), jnp.bfloat16),
         ],
-        flops=2 * segs * seg * seg * 2 * width * 3,
-    )
-
-
-def finish_kernel(factor, ids, key, value, *refs):
-    n = len(refs) - 11
-    pieces = refs[:n]
-    outs = refs[n : n + 3]
-    key_v, value_v, piece_v, key_o, value_o, filter_o, in_sem, out_sem = refs[n + 3 :]
+    )
+
+
+def finish_kernel(ks, factor, fetch_branches, spot, *refs):
+    n = len(ks)
+    if fetch_branches:
+        (key, value, *pieces), refs = refs[: 2 + n], refs[2 + n :]
+        branches, *outs, piece_v, key_o, value_o, filter_o, in_sem, out_sem = refs
+    else:
+        (branches, *pieces), refs = refs[: 1 + n], refs[1 + n :]
+        *outs, piece_v, key_o, value_o, filter_o, in_sem, out_sem = refs
     width = piece_v.shape[3]
-    me = 2 * ids[CHIP] + ids[CORE]
-    loads = [pltpu.make_async_copy(p, piece_v.at[k], in_sem.at[k]) for k, p in enumerate(pieces)]
-    loads += [pltpu.make_async_copy(key, key_v, in_sem.at[n]), pltpu.make_async_copy(value, value_v, in_sem.at[n + 1])]
-    for copy in loads[::-1]:
+    me = 2 * spot.chip + spot.core
+    loads = [pltpu.make_async_copy(p, piece_v.at[i], in_sem.at[i]) for i, p in enumerate(pieces)]
+    if fetch_branches:
+        loads.append(pltpu.make_async_copy(key, branches.at[0], in_sem.at[n]))
+        loads.append(pltpu.make_async_copy(value, branches.at[1], in_sem.at[n + 1]))
+    for copy in loads:
         copy.start()
-    for copy in loads[n:]:
+    for copy in loads:
         copy.wait()
     stores = []
-    for k in range(n):
+    for i, k in enumerate(ks):
         here = (slice(None), pl.ds(pl.multiple_of((me ^ k) * width, width), width))
-        loads[k].wait()
-        conv_grad = piece_v[k, 0].astype(jnp.float32)
-        key_o[here] = (conv_grad * value_v[here].astype(jnp.float32)).astype(jnp.bfloat16)
-        value_o[here] = (conv_grad * key_v[here].astype(jnp.float32)).astype(jnp.bfloat16)
-        filter_o[here] = piece_v[k, 1].astype(jnp.float32) * factor
+        conv_grad = piece_v[i, 0].astype(jnp.float32)
+        key_o[i] = (conv_grad * branches[(1, *here)].astype(jnp.float32)).astype(jnp.bfloat16)
+        value_o[i] = (conv_grad * branches[(0, *here)].astype(jnp.float32)).astype(jnp.bfloat16)
+        filter_o[i] = piece_v[i, 1].astype(jnp.float32) * factor
         for o, (src, dst) in enumerate(zip((key_o, value_o, filter_o), outs)):
-            stores.append(pltpu.make_async_copy(src.at[here], dst.at[here], out_sem.at[o, k]))
+            stores.append(pltpu.make_async_copy(src.at[i], dst.at[here], out_sem.at[o, i]))
             stores[-1].start()
     for copy in stores:
         copy.wait()
 
 
-def finish(ids, key, value, pieces, factor):
-    n = len(pieces)
-    outs = [array(key.shape), array(key.shape), array(key.shape, jnp.float32)]
-    return call(
-        functools.partial(finish_kernel, factor),
-        ids,
-        (key, value, *pieces),
-        [ANY] * (2 + n),
-        outs,
-        [ANY] * 3,
-        "finish",
-        [
-            pltpu.VMEM(key.shape, key.dtype),
-            pltpu.VMEM(key.shape, key.dtype),
-            pltpu.VMEM((n, *pieces[0].shape), pieces[0].dtype),
-            *[pltpu.VMEM(o.shape, o.dtype) for o in outs],
-            pltpu.SemaphoreType.DMA((n + 2,)),
-            pltpu.SemaphoreType.DMA((3, n)),
-        ],
-        moved=12 * key.size,
-    )
+def finish(ks, pieces, factor, key=None, value=None, branches=None, grads=None):
+    begin = branches is None
+    n = len(ks)
+    rows, width = pieces[0].shape[1:]
+    scratch = [
+        pltpu.VMEM((n, 2, rows, width), jnp.bfloat16),
+        pltpu.VMEM((n, rows, width), jnp.bfloat16),
+        pltpu.VMEM((n, rows, width), jnp.bfloat16),
+        pltpu.VMEM((n, rows, width), jnp.float32),
+        pltpu.SemaphoreType.DMA((n + 2,)),
+        pltpu.SemaphoreType.DMA((3, n)),
+    ]
+    kernel = functools.partial(finish_kernel, ks, factor, begin)
+    if begin:
+        both = pltpu.VMEM((2, *key.shape), key.dtype)
+        outs = [both, array(key.shape), array(key.shape), array(key.shape, jnp.float32)]
+        args = (key, value, *pieces)
+        return call(kernel, args, [ANY] * len(args), outs, [VMEM, *[ANY] * 3], "finish", scratch)
+    args = (branches, *pieces)
+    return call(kernel, args, [VMEM, *[ANY] * n], [], [], "finish", scratch, update=grads)
+
+
+def hold(arrays, after):
+    return call(lambda spot: None, (), [], [], [], "hold", carry=arrays, after=after)
 
 
 def swap(x, k, n):
@@ -552,25 +585,10 @@
 def fast_shards(grad_out, out_weight, query_gate, key_branch, value_branch, filter_taps):
     n = lax.axis_size("seq")
     planes = lax.axis_size("ch")
-    me = lax.axis_index("seq")
-    plane = lax.axis_index("ch")
     rows = grad_out.shape[0]
     chips = n // 2
     factor = 1.0 / math.sqrt(rows * n)
-    forward, back = half_tables(2 * rows)
-    low = plane < planes // 2
-    ids = jnp.stack(
-        [
-            me // 2,
-            me % 2,
-            jnp.where((plane == 0) | (plane == planes - 1), 1, 0),
-            plane,
-            plane ^ 1,
-            jnp.where(low, 2, 1),
-            jnp.where(low, 3, 0),
-        ]
-    ).astype(jnp.int32)
-
+    forward, back = (jnp.asarray(t) for t in half_tables(2 * rows))
     outer = [(i, i ^ 1) for i in range(planes)]
     inner = []
     for s in range(n):
@@ -583,32 +601,31 @@
     def send_inner(x):
         return lax.ppermute(x, ("seq", "ch"), inner)
 
-    def both(*candidates):
-        return [list(candidates), [swap(x, 1, n) for x in candidates]]
-
-    held, second = load(ids, out_weight, grad_out, chips)
-    own = [grad_out[: rows // CHUNKS], second]
-    outer_0 = [send_outer(x) for x in own]
-    inner_0 = [send_inner(x) for x in own]
-    outer_1 = [send_outer(x) for x in inner_0]
-    inner_1 = [send_inner(x) for x in outer_0]
-    outer_2 = [send_outer(x) for x in inner_1]
-
-    other = swap(pack(ids, query_gate, key_branch, value_branch, filter_taps, chips), 1, n)
-    gates, taps_input = merge(ids, query_gate, key_branch, value_branch, filter_taps, other, chips)
+    def other(x):
+        return swap(x, 1, n)
+
+    outer_0, inner_0, others = send_outer(grad_out), send_inner(grad_out), other(grad_out)
+    mine, *packed, packed_mark = pack(query_gate, key_branch, value_branch, filter_taps, chips)
+    gates, taps_input, (merged,) = merge(mine, [other(x) for x in packed], after=[packed_mark])
     taps_input = [swap(x, 2 * k, n) for k, x in enumerate(taps_input)]
-
-    total = mix(ids, 0, [g for x in own for g in both(x)], held, None)
-    total = mix(ids, 1, [g for x in outer_0 for g in both(x)], held, total)
-    total = mix(ids, 2, [g for x in zip(outer_1, inner_0) for g in both(*x)], held, total)
-    kern = tap_kernels(ids, forward, taps_input)
-    gated = []
-    for c, x in enumerate(zip(outer_2, inner_1)):
-        pieces = mix_gate(ids, c, CHUNKS, both(*x), held, total, gates)
-        gated.append([swap(p, 2 * k, n) for k, p in enumerate(pieces)])
-    results = correlate(ids, forward, back, kern, list(zip(*gated)))
+    outer_1, inner_1 = send_outer(inner_0), send_inner(outer_0)
+    kern, tapped = tap_kernels(forward, taps_input, after=[merged])
+    outer_1, inner_1, gone = hold([outer_1, inner_1], after=[tapped])
+    outer_2 = send_outer(inner_1)
+
+    held, loaded = load(out_weight, chips, after=[gone])
+    total, first = mix(0, [[grad_out], [others]], held, None, after=[loaded])
+    total, outer_1, second = mix(1, [[outer_0], [other(outer_0)]], held, total, carry=[outer_1], after=[first])
+    blocks = [[outer_1, inner_0], [other(outer_1), other(inner_0)]]
+    total, _ = mix(2, blocks, held, total, after=[second])
+    gated = mix_gate(0, 1, [[outer_2, inner_1], [other(outer_2), other(inner_1)]], held, total, gates)[:chips]
+    gated = [[swap(p, 2 * k, n)] for k, p in enumerate(gated)]
+
+    results = correlate(forward, back, kern, gated)[:n]
     results = [swap(x, k, n) for k, x in enumerate(results)]
-    return finish(ids, key_branch, value_branch, results, factor)
+    near, far = list(range(n // 2)), list(range(n // 2, n))
+    branches, *grads, _ = finish(near, results[: n // 2], factor, key=key_branch, value=value_branch)
+    return tuple(finish(far, results[n // 2 :], factor, branches=branches, grads=grads)[:3])
 
 
 def solution(mesh):

time: 102 us -> 79.8 us (0.78)
  waiting for transfers between devices: 42.8 us -> 27.6 us
  starting transfers between devices: 27.4 us -> 21.8 us
  Pallas kernels: 29.6 us -> 27.6 us
    ppermute x6 -> x3, waiting for transfers between devices: 28.3 us -> 2.47 us  [send_outer(): return lax.ppermute(x, 'ch', outer)]
    ppermute x29 -> x21, waiting for transfers between devices: 14.4 us -> 25.1 us  [swap(): return lax.ppermute(x, 'seq', [(i, i ^ k) for i in range(n)]) if k else x]
    ppermute x29 -> x21, starting transfers between devices: 17.4 us -> 14.3 us  [swap(): return lax.ppermute(x, 'seq', [(i, i ^ k) for i in range(n)]) if k else x]
    ppermute x6 -> x3, starting transfers between devices: 9.28 us -> 7.01 us  [send_outer(): return lax.ppermute(x, 'ch', outer)]
    pallas_call x11 -> x12, Pallas kernels: 29.6 us -> 27.6 us  [call(): pl.pallas_call(body, input_output_aliases={count + i: results + i for i i...]
  transfers between devices with their start and end apart: 39 -> 26, of which waited for: 11 -> 11; matrix products, arithmetic and copies ran while one was open for 0% -> 0% of each run, Pallas kernels for 15% -> 25%
where the time goes in v3:
time: 79.8 us; the launch traced here: 79.5 us
  Pallas kernels  27.6 us (35%)
  waiting for transfers between devices  27.6 us (35%)
  starting transfers between devices  21.8 us (27%)
  local copies, waits for them, and re-layouts  1.67 us (2%)
  between operations  0.84 us (1%)
    pallas_call x12, Pallas kernels, call(): pl.pallas_call(body, input_output_aliases={count + i: results + i for i i...  27.6 us
    ppermute x21, waiting for transfers between devices, swap(): return lax.ppermute(x, 'seq', [(i, i ^ k) for i in range(n)]) if k else x  25.1 us
    ppermute x21, starting transfers between devices, swap(): return lax.ppermute(x, 'seq', [(i, i ^ k) for i in range(n)]) if k else x  14.3 us
    ppermute x3, starting transfers between devices, send_outer(): return lax.ppermute(x, 'ch', outer)  7.01 us
    ppermute x3, waiting for transfers between devices, send_outer(): return lax.ppermute(x, 'ch', outer)  2.47 us
    unnamed x14, local copies, waits for them, and re-layouts  1.67 us
  transfers between devices with their start and end apart: 26, of which 11 were waited for; matrix products, arithmetic and copies ran while one was open for 0% of the time, Pallas kernels for 25%

profile of v3, /device:TPU:0, one launch (start us, length us, event | category | flops | bytes accessed | tf_op | source)
XLA Modules:
  0.0 79.5 jit_solution(18283451950616337558)
XLA Ops:
  1.1 4.1 %collective-permute-start.7 = (bf16[128,2048]{1,0:T(8,128)(2,1)}, bf16[128,2048]{1,0:T(8,128)(2,1)S(1)}, u32[]{:S(2)}, u32[]{:S(2)}) collective-permute-start(bf16[128,2048]{1,0:T(8,128)(2,1)} %refs_0_.8), channel_id=1, source_target_pairs={{0,1},{1,0},{2,3},{3,2},{4,5},{5,4},{6,7},{7,6},{8,9},{9,8},{10,11... | collective-permute-start | bytes 1572872 | tf_op jit(solution)/shard_map/ppermute | solution.py:599
  5.3 2.5 %pack_core.1 = (bf16[3,4,128,256]{3,2,1,0:T(8,128)(2,1)S(1)}, bf16[3,4,64,256]{3,2,1,0:T(8,128)(2,1)}, bf16[3,4,64,256]{3,2,1,0:T(8,128)(2,1)}, f32[8,128]{1,0:T(8,128)}) custom-call(bf16[128,2048]{1,0:T(8,128)(2,1)} %refs_0_.6, bf16[128,2048]{1,0:T(8,128)(2,1)} %refs_0_.9, bf16[128,2048]{1,0:T(8,128)(2,1)} %refs_1_.4, bf16[128,2048]{1,0:T(8,128)(2,1)} %refs_3_.1), custom_call_target="tpu_custom_call" | custom-call | tf_op jit(solution)/shard_map/pack_core/pallas_call | solution.py:180
  8.4 1.4 %collective-permute-done.refs_1_ = bf16[3,4,64,256]{3,2,1,0:T(8,128)(2,1)S(1)} collective-permute-done((bf16[3,4,64,256]{3,2,1,0:T(8,128)(2,1)}, bf16[3,4,64,256]{3,2,1,0:T(8,128)(2,1)S(1)}, u32[]{:S(2)}, u32[]{:S(2)}) %collective-permute-start) | collective-permute-done | bytes 393248 | tf_op jit(solution)/shard_map/ppermute | solution.py:582
  11.1 1.3 %merge_cores.1 = (bf16[4,2,128,256]{3,2,1,0:T(8,128)(2,1)S(1)}, bf16[2,2,128,256]{3,2,1,0:T(8,128)(2,1)S(1)}, bf16[2,2,128,256]{3,2,1,0:T(8,128)(2,1)S(1)}, bf16...) custom-call(bf16[3,4,128,256]{3,2,1,0:T(8,128)(2,1)S(1)} %get-tuple-element.45.refs_0_, ...), custom_call_target="tpu_custom_call" | custom-call | tf_op jit(solution)/shard_map/merge_cores/pallas_call | solution.py:180
  12.4 1.6 %collective-permute-start.2 = (bf16[2,2,128,256]{3,2,1,0:T(8,128)(2,1)S(1)}, bf16[2,2,128,256]{3,2,1,0:T(8,128)(2,1)S(1)}, u32[]{:S(2)}, u32[]{:S(2)}) collective-permute-start(bf16[2,2,128,256]{3,2,1,0:T(8,128)(2,1)S(1)} %get-tuple-element.50), channel_id=1, source_target_pairs={{0,8},{4,12},{8,0},{12,4},{16,24},{20,28},{24,16},{28,20},{1,9},{5... | collective-permute-start | bytes 786440 | tf_op jit(solution)/shard_map/ppermute | solution.py:582
  14.0 1.5 %collective-permute-start.3 = (bf16[2,2,128,256]{3,2,1,0:T(8,128)(2,1)S(1)}, bf16[2,2,128,256]{3,2,1,0:T(8,128)(2,1)S(1)}, u32[]{:S(2)}, u32[]{:S(2)}) collective-permute-start(bf16[2,2,128,256]{3,2,1,0:T(8,128)(2,1)S(1)} %get-tuple-element.51), channel_id=1, source_target_pairs={{0,16},{4,20},{8,24},{12,28},{16,0},{20,4},{24,8},{28,12},{1,17},{... | collective-permute-start | bytes 786440 | tf_op jit(solution)/shard_map/ppermute | solution.py:582
  16.0 1.6 %collective-permute-start.6 = (bf16[128,2048]{1,0:T(8,128)(2,1)S(1)}, bf16[128,2048]{1,0:T(8,128)(2,1)S(1)}, u32[]{:S(2)}, u32[]{:S(2)}) collective-permute-start(bf16[128,2048]{1,0:T(8,128)(2,1)S(1)} %collective-permute-done.5.refs_1_), channel_id=1, source_target_pairs={{0,1},{1,0},{2,3},{3,2},{4,5},{5,4},{6,7},{7,6},{8,9},{9,8},{10,11... | collective-permute-start | bytes 1572872 | tf_op jit(solution)/shard_map/ppermute | solution.py:599
  17.6 4.0 %collective-permute-done.2.refs_2_ = bf16[2,2,128,256]{3,2,1,0:T(8,128)(2,1)S(1)} collective-permute-done((bf16[2,2,128,256]{3,2,1,0:T(8,128)(2,1)S(1)}, bf16[2,2,128,256]{3,2,1,0:T(8,128)(2,1)S(1)}, u32[]{:S(2)}, u32[]{:S(2)}) %collective-permute-start.2) | collective-permute-done | bytes 262176 | tf_op jit(solution)/shard_map/ppermute | solution.py:582
  21.6 6.0 %collective-permute-done.3.refs_3_ = bf16[2,2,128,256]{3,2,1,0:T(8,128)(2,1)S(1)} collective-permute-done((bf16[2,2,128,256]{3,2,1,0:T(8,128)(2,1)S(1)}, bf16[2,2,128,256]{3,2,1,0:T(8,128)(2,1)S(1)}, u32[]{:S(2)}, u32[]{:S(2)}) %collective-permute-start.3) | collective-permute-done | bytes 262176 | tf_op jit(solution)/shard_map/ppermute | solution.py:582
  27.7 0.9 %copy-done.3 = bf16[512,256]{1,0:T(8,128)(2,1)S(1)} copy-done((bf16[512,256]{1,0:T(8,128)(2,1)S(1)}, bf16[512,256]{1,0:T(8,128)(2,1)}, u32[]{:S(2)}) %copy-start.3) | copy-done | bytes 262168
  28.6 1.5 %kernels.1 = (bf16[2,4,512,256]{3,2,1,0:T(8,128)(2,1)S(1)}, f32[8,128]{1,0:T(8,128)S(1)}) custom-call(bf16[512,256]{1,0:T(8,128)(2,1)S(1)} %copy-done.3, bf16[2,2,128,256]{3,2,1,0:T(8,128)(2,1)S(1)} %get-tuple-element.49.refs_1_, bf16[2,2,128,256]{3,2,1,0:T(8,128)(2,1)S(1)} %collective-permute-done.2.refs_2_, ...), custom_call_target="tpu_custom_call" | custom-call | flops 3221225472 | tf_op jit(solution)/shard_map/kernels/pallas_call | solution.py:180
  30.1 1.2 %collective-permute-start.9 = (bf16[128,2048]{1,0:T(8,128)(2,1)S(1)}, bf16[128,2048]{1,0:T(8,128)(2,1)S(1)}, u32[]{:S(2)}, u32[]{:S(2)}) collective-permute-start(bf16[128,2048]{1,0:T(8,128)(2,1)S(1)} %get-tuple-element.56.refs_1_), channel_id=1, source_target_pairs={{0,1},{1,0},{2,3},{3,2},{4,5},{5,4},{6,7},{7,6},{8,9},{9,8},{10,11... | collective-permute-start | bytes 1572872 | tf_op jit(solution)/shard_map/ppermute | solution.py:599
  31.4 6.0 %load_weight.1 = (bf16[4,256,8192]{2,1,0:T(8,128)(2,1)S(1)}, f32[8,128]{1,0:T(8,128)S(1)}) custom-call(bf16[2048,8192]{1,0:T(8,128)(2,1)} %refs_0_.7, f32[8,128]{1,0:T(8,128)S(1)} %get-tuple-element.57.refs_1_), custom_call_target="tpu_custom_call" | custom-call | tf_op jit(solution)/shard_map/load_weight/pallas_call | solution.py:180
  37.4 2.0 %mix.3 = (f32[4,256,256]{2,1,0:T(8,128)S(1)}, f32[8,128]{1,0:T(8,128)S(1)}) custom-call(bf16[128,2048]{1,0:T(8,128)(2,1)S(1)} %copy-done.2, bf16[128,2048]{1,0:T(8,128)(2,1)S(1)} %collective-permute-done.13.refs_1_, bf16[4,256,8192]{2,1,0:T(8,128)(2,1)S(1)} %get-tuple-element.58.refs_2_.refs_4_, f32[8,128]{1,0:T(8,128)S(1)} %get-tuple-element.59.refs_3_), custom_call_target="tpu_custom_call" | custom-call | tf_op jit(solution)/shard_map/mix/pallas_call | solution.py:180
  39.4 2.0 %mix.4 = (f32[4,256,256]{2,1,0:T(8,128)S(1)}, bf16[128,2048]{1,0:T(8,128)(2,1)S(1)}, f32[8,128]{1,0:T(8,128)S(1)}) custom-call(bf16[128,2048]{1,0:T(8,128)(2,1)S(1)} %collective-permute-done.7.refs_0_, bf16[128,2048]{1,0:T(8,128)(2,1)S(1)} %collective-permute-done.12.refs_1_, ...), custom_call_target="tpu_custom_call", output_to_operand_aliasing={{1}: (4, {})} | custom-call | tf_op jit(solution)/shard_map/mix/pallas_call | solution.py:180
  42.1 2.5 %collective-permute-done.9.refs_0_ = bf16[128,2048]{1,0:T(8,128)(2,1)S(1)} collective-permute-done((bf16[128,2048]{1,0:T(8,128)(2,1)S(1)}, bf16[128,2048]{1,0:T(8,128)(2,1)S(1)}, u32[]{:S(2)}, u32[]{:S(2)}) %collective-permute-start.9) | collective-permute-done | bytes 524320 | tf_op jit(solution)/shard_map/ppermute | solution.py:599
  44.6 2.1 %mix.5 = (f32[4,256,256]{2,1,0:T(8,128)S(1)}, f32[8,128]{1,0:T(8,128)}) custom-call(bf16[128,2048]{1,0:T(8,128)(2,1)S(1)} %get-tuple-element.63.refs_0_, bf16[128,2048]{1,0:T(8,128)(2,1)S(1)} %collective-permute-done.5.refs_1_, bf16[128,2048]{1,0:T(8,128)(2,1)S(1)} %collective-permute-done.14.refs_2_, bf16[128,2048]{1,0:T(8,128)(2,1)S(1)} %collective-permute-done.15.refs_3_, ...), custom_call_target="tpu_custom_call" | custom-call | tf_op jit(solution)/shard_map/mix/pallas_call | solution.py:180
  46.7 1.4 %mix_gate.1 = (bf16[2,128,256]{2,1,0:T(8,128)(2,1)S(1)}, bf16[2,128,256]{2,1,0:T(8,128)(2,1)S(1)}, bf16[2,128,256]{2,1,0:T(8,128)(2,1)S(1)}, bf16[2,128,256]{2,1,0:T(8,128)(2,1)S(1)}, f32[8,128]{1,0:T(8,128)}) custom-call(bf16[128,2048]{1,0:T(8,128)(2,1)S(1)} %collective-permute-done.9.refs_0_, bf16[128,2048]{1,0:T(8,128)(2,1)S(1)} %get-tuple-element.56.refs_1_, ...), custom_call_target="tpu_custom_call" | custom-call | tf_op jit(solution)/shard_map/mix_gate/pallas_call | solution.py:180
  48.7 1.6 %collective-permute-start.17 = (bf16[2,128,256]{2,1,0:T(8,128)(2,1)S(1)}, bf16[2,128,256]{2,1,0:T(8,128)(2,1)S(1)}, u32[]{:S(2)}, u32[]{:S(2)}) collective-permute-start(bf16[2,128,256]{2,1,0:T(8,128)(2,1)S(1)} %get-tuple-element.70), channel_id=1, source_target_pairs={{0,16},{4,20},{8,24},{12,28},{16,0},{20,4},{24,8},{28,12},{1,17},{... | collective-permute-start | bytes 393224 | tf_op jit(solution)/shard_map/ppermute | solution.py:582
  50.3 1.4 %collective-permute-start.18 = (bf16[2,128,256]{2,1,0:T(8,128)(2,1)S(1)}, bf16[2,128,256]{2,1,0:T(8,128)(2,1)S(1)}, u32[]{:S(2)}, u32[]{:S(2)}) collective-permute-start(bf16[2,128,256]{2,1,0:T(8,128)(2,1)S(1)} %get-tuple-element.71), channel_id=1, source_target_pairs={{0,24},{4,28},{8,16},{12,20},{16,8},{20,12},{24,0},{28,4},{1,25},{... | collective-permute-start | bytes 393224 | tf_op jit(solution)/shard_map/ppermute | solution.py:582
  51.7 2.8 %collective-permute-done.16.refs_4_ = bf16[2,128,256]{2,1,0:T(8,128)(2,1)S(1)} collective-permute-done((bf16[2,128,256]{2,1,0:T(8,128)(2,1)S(1)}, bf16[2,128,256]{2,1,0:T(8,128)(2,1)S(1)}, u32[]{:S(2)}, u32[]{:S(2)}) %collective-permute-start.16) | collective-permute-done | bytes 131104 | tf_op jit(solution)/shard_map/ppermute | solution.py:582
  54.5 1.8 %collective-permute-done.17.refs_5_ = bf16[2,128,256]{2,1,0:T(8,128)(2,1)S(1)} collective-permute-done((bf16[2,128,256]{2,1,0:T(8,128)(2,1)S(1)}, bf16[2,128,256]{2,1,0:T(8,128)(2,1)S(1)}, u32[]{:S(2)}, u32[]{:S(2)}) %collective-permute-start.17) | collective-permute-done | bytes 131104 | tf_op jit(solution)/shard_map/ppermute | solution.py:582
  56.3 1.6 %collective-permute-done.18.refs_6_ = bf16[2,128,256]{2,1,0:T(8,128)(2,1)S(1)} collective-permute-done((bf16[2,128,256]{2,1,0:T(8,128)(2,1)S(1)}, bf16[2,128,256]{2,1,0:T(8,128)(2,1)S(1)}, u32[]{:S(2)}, u32[]{:S(2)}) %collective-permute-start.18) | collective-permute-done | bytes 131104 | tf_op jit(solution)/shard_map/ppermute | solution.py:582
  57.9 3.9 %correlate.1 = (bf16[2,128,256]{2,1,0:T(8,128)(2,1)S(1)}, bf16[2,128,256]{2,1,0:T(8,128)(2,1)S(1)}, bf16[2,128,256]{2,1,0:T(8,128)(2,1)S(1)}, bf16[2,128,256]{2,...) custom-call(bf16[512,256]{1,0:T(8,128)(2,1)S(1)} %copy-done.4, ...), custom_call_target="tpu_custom_call" | custom-call | tf_op jit(solution)/shard_map/correlate/pallas_call | solution.py:180
  62.6 1.1 %collective-permute-start.21 = (bf16[2,128,256]{2,1,0:T(8,128)(2,1)S(1)}, bf16[2,128,256]{2,1,0:T(8,128)(2,1)S(1)}, u32[]{:S(2)}, u32[]{:S(2)}) collective-permute-start(bf16[2,128,256]{2,1,0:T(8,128)(2,1)S(1)} %get-tuple-element.75), channel_id=1, source_target_pairs={{0,12},{4,8},{8,4},{12,0},{16,28},{20,24},{24,20},{28,16},{1,13},{... | collective-permute-start | bytes 393224 | tf_op jit(solution)/shard_map/ppermute | solution.py:582
  63.7 0.8 %collective-permute-start.22 = (bf16[2,128,256]{2,1,0:T(8,128)(2,1)S(1)}, bf16[2,128,256]{2,1,0:T(8,128)(2,1)S(1)}, u32[]{:S(2)}, u32[]{:S(2)}) collective-permute-start(bf16[2,128,256]{2,1,0:T(8,128)(2,1)S(1)} %get-tuple-element.77), channel_id=1, source_target_pairs={{0,16},{4,20},{8,24},{12,28},{16,0},{20,4},{24,8},{28,12},{1,17},{... | collective-permute-start | bytes 393224 | tf_op jit(solution)/shard_map/ppermute | solution.py:582
  65.3 1.8 %collective-permute-start.24 = (bf16[2,128,256]{2,1,0:T(8,128)(2,1)S(1)}, bf16[2,128,256]{2,1,0:T(8,128)(2,1)S(1)}, u32[]{:S(2)}, u32[]{:S(2)}) collective-permute-start(bf16[2,128,256]{2,1,0:T(8,128)(2,1)S(1)} %get-tuple-element.79), channel_id=1, source_target_pairs={{0,24},{4,28},{8,16},{12,20},{16,8},{20,12},{24,0},{28,4},{1,25},{... | collective-permute-start | bytes 393224 | tf_op jit(solution)/shard_map/ppermute | solution.py:582
  67.1 1.0 %collective-permute-done.20.refs_4_ = bf16[2,128,256]{2,1,0:T(8,128)(2,1)S(1)} collective-permute-done((bf16[2,128,256]{2,1,0:T(8,128)(2,1)S(1)}, bf16[2,128,256]{2,1,0:T(8,128)(2,1)S(1)}, u32[]{:S(2)}, u32[]{:S(2)}) %collective-permute-start.20) | collective-permute-done | bytes 131104 | tf_op jit(solution)/shard_map/ppermute | solution.py:582
  68.8 1.3 %collective-permute-done.21.refs_5_ = bf16[2,128,256]{2,1,0:T(8,128)(2,1)S(1)} collective-permute-done((bf16[2,128,256]{2,1,0:T(8,128)(2,1)S(1)}, bf16[2,128,256]{2,1,0:T(8,128)(2,1)S(1)}, u32[]{:S(2)}, u32[]{:S(2)}) %collective-permute-start.21) | collective-permute-done | bytes 131104 | tf_op jit(solution)/shard_map/ppermute | solution.py:582
  70.1 2.5 %finish.2 = (bf16[2,128,2048]{2,1,0:T(8,128)(2,1)S(1)}, bf16[128,2048]{1,0:T(8,128)(2,1)}, bf16[128,2048]{1,0:T(8,128)(2,1)}, f32[128,2048]{1,0:T(8,128)}, f32[8,128]{1,0:T(8,128)}) custom-call(bf16[128,2048]{1,0:T(8,128)(2,1)S(1)} %copy-done, bf16[128,2048]{1,0:T(8,128)(2,1)S(1)} %copy-done.1, bf16[2,128,256]{2,1,0:T(8,128)(2,1)S(1)} %get-tuple-element.72.refs_2_, ...), custom_call_target="tpu_custom_call" | custom-call | tf_op jit(solution)/shard_map/finish/pallas_call | solution.py:180
  72.6 4.5 %collective-permute-done.23.refs_2_ = bf16[2,128,256]{2,1,0:T(8,128)(2,1)S(1)} collective-permute-done((bf16[2,128,256]{2,1,0:T(8,128)(2,1)S(1)}, bf16[2,128,256]{2,1,0:T(8,128)(2,1)S(1)}, u32[]{:S(2)}, u32[]{:S(2)}) %collective-permute-start.23) | collective-permute-done | bytes 131104 | tf_op jit(solution)/shard_map/ppermute | solution.py:582
  77.1 2.4 %finish.3 = (bf16[128,2048]{1,0:T(8,128)(2,1)}, bf16[128,2048]{1,0:T(8,128)(2,1)}, f32[128,2048]{1,0:T(8,128)}, f32[8,128]{1,0:T(8,128)}) custom-call(bf16[2,128,2048]{2,1,0:T(8,128)(2,1)S(1)} %get-tuple-element.76.refs_0_, bf16[2,128,256]{2,1,0:T(8,128)(2,1)S(1)} %collective-permute-done.22.refs_1_, ...), custom_call_target="tpu_custom_call", output_to_operand_aliasing={{0}: (5, {}), {1}: (6, {}), {2}: (7, {})} | custom-call | tf_op jit(solution)/shard_map/finish/pallas_call | solution.py:180
  (46 shorter events, 6.4 us)
Async XLA Ops:
  0.6 15.3 %collective-permute-start.5 = (bf16[128,2048]{1,0:T(8,128)(2,1)}, bf16[128,2048]{1,0:T(8,128)(2,1)S(1)}, u32[]{:S(2)}, u32[]{:S(2)}) collective-permute-start(bf16[128,2048]{1,0:T(8,128)(2,1)} %refs_0_.8), channel_id=1, source_target_pairs={{1,2},{2,1},{0,4},{3,7},{5,6},{6,5},{4,0},{7,3},{9,10},{10,9},{8,1... | collective-permute-start | bytes 1572872 | tf_op jit(solution)/shard_map/ppermute | solution.py:602
  1.1 16.4 %collective-permute-start.7 = (bf16[128,2048]{1,0:T(8,128)(2,1)}, bf16[128,2048]{1,0:T(8,128)(2,1)S(1)}, u32[]{:S(2)}, u32[]{:S(2)}) collective-permute-start(bf16[128,2048]{1,0:T(8,128)(2,1)} %refs_0_.8), channel_id=1, source_target_pairs={{0,1},{1,0},{2,3},{3,2},{4,5},{5,4},{6,7},{7,6},{8,9},{9,8},{10,11... | collective-permute-start | bytes 1572872 | tf_op jit(solution)/shard_map/ppermute | solution.py:599
  7.9 2.0 %collective-permute-start = (bf16[3,4,64,256]{3,2,1,0:T(8,128)(2,1)}, bf16[3,4,64,256]{3,2,1,0:T(8,128)(2,1)S(1)}, u32[]{:S(2)}, u32[]{:S(2)}) collective-permute-start(bf16[3,4,64,256]{3,2,1,0:T(8,128)(2,1)} %get-tuple-element.46), channel_id=1, source_target_pairs={{0,4},{4,0},{8,12},{12,8},{16,20},{20,16},{24,28},{28,24},{1,5},{5... | collective-permute-start | bytes 1179656 | tf_op jit(solution)/shard_map/ppermute | solution.py:582
  7.9 2.5 %collective-permute-start.1 = (bf16[3,4,64,256]{3,2,1,0:T(8,128)(2,1)}, bf16[3,4,64,256]{3,2,1,0:T(8,128)(2,1)S(1)}, u32[]{:S(2)}, u32[]{:S(2)}) collective-permute-start(bf16[3,4,64,256]{3,2,1,0:T(8,128)(2,1)} %get-tuple-element.47), channel_id=1, source_target_pairs={{0,4},{4,0},{8,12},{12,8},{16,20},{20,16},{24,28},{28,24},{1,5},{5... | collective-permute-start | bytes 1179656 | tf_op jit(solution)/shard_map/ppermute | solution.py:582
  12.4 9.2 %collective-permute-start.2 = (bf16[2,2,128,256]{3,2,1,0:T(8,128)(2,1)S(1)}, bf16[2,2,128,256]{3,2,1,0:T(8,128)(2,1)S(1)}, u32[]{:S(2)}, u32[]{:S(2)}) collective-permute-start(bf16[2,2,128,256]{3,2,1,0:T(8,128)(2,1)S(1)} %get-tuple-element.50), channel_id=1, source_target_pairs={{0,8},{4,12},{8,0},{12,4},{16,24},{20,28},{24,16},{28,20},{1,9},{5... | collective-permute-start | bytes 786440 | tf_op jit(solution)/shard_map/ppermute | solution.py:582
  14.0 13.7 %collective-permute-start.3 = (bf16[2,2,128,256]{3,2,1,0:T(8,128)(2,1)S(1)}, bf16[2,2,128,256]{3,2,1,0:T(8,128)(2,1)S(1)}, u32[]{:S(2)}, u32[]{:S(2)}) collective-permute-start(bf16[2,2,128,256]{3,2,1,0:T(8,128)(2,1)S(1)} %get-tuple-element.51), channel_id=1, source_target_pairs={{0,16},{4,20},{8,24},{12,28},{16,0},{20,4},{24,8},{28,12},{1,17},{... | collective-permute-start | bytes 786440 | tf_op jit(solution)/shard_map/ppermute | solution.py:582
  15.5 12.2 %collective-permute-start.4 = (bf16[2,2,128,256]{3,2,1,0:T(8,128)(2,1)S(1)}, bf16[2,2,128,256]{3,2,1,0:T(8,128)(2,1)S(1)}, u32[]{:S(2)}, u32[]{:S(2)}) collective-permute-start(bf16[2,2,128,256]{3,2,1,0:T(8,128)(2,1)S(1)} %get-tuple-element.52), channel_id=1, source_target_pairs={{0,24},{4,28},{8,16},{12,20},{16,8},{20,12},{24,0},{28,4},{1,25},{... | collective-permute-start | bytes 786440 | tf_op jit(solution)/shard_map/ppermute | solution.py:582
  16.0 14.1 %collective-permute-start.6 = (bf16[128,2048]{1,0:T(8,128)(2,1)S(1)}, bf16[128,2048]{1,0:T(8,128)(2,1)S(1)}, u32[]{:S(2)}, u32[]{:S(2)}) collective-permute-start(bf16[128,2048]{1,0:T(8,128)(2,1)S(1)} %collective-permute-done.5.refs_1_), channel_id=1, source_target_pairs={{0,1},{1,0},{2,3},{3,2},{4,5},{5,4},{6,7},{7,6},{8,9},{9,8},{10,11... | collective-permute-start | bytes 1572872 | tf_op jit(solution)/shard_map/ppermute | solution.py:599
  17.6 12.5 %collective-permute-start.8 = (bf16[128,2048]{1,0:T(8,128)(2,1)S(1)}, bf16[128,2048]{1,0:T(8,128)(2,1)S(1)}, u32[]{:S(2)}, u32[]{:S(2)}) collective-permute-start(bf16[128,2048]{1,0:T(8,128)(2,1)S(1)} %collective-permute-done.7.refs_0_), channel_id=1, source_target_pairs={{1,2},{2,1},{0,4},{3,7},{5,6},{6,5},{4,0},{7,3},{9,10},{10,9},{8,1... | collective-permute-start | bytes 1572872 | tf_op jit(solution)/shard_map/ppermute | solution.py:602
  21.6 15.8 %collective-permute-start.13 = (bf16[128,2048]{1,0:T(8,128)(2,1)}, bf16[128,2048]{1,0:T(8,128)(2,1)S(1)}, u32[]{:S(2)}, u32[]{:S(2)}) collective-permute-start(bf16[128,2048]{1,0:T(8,128)(2,1)} %refs_0_.8), channel_id=1, source_target_pairs={{0,4},{4,0},{8,12},{12,8},{16,20},{20,16},{24,28},{28,24},{1,5},{5... | collective-permute-start | bytes 1572872 | tf_op jit(solution)/shard_map/ppermute | solution.py:582
  27.7 11.8 %collective-permute-start.12 = (bf16[128,2048]{1,0:T(8,128)(2,1)S(1)}, bf16[128,2048]{1,0:T(8,128)(2,1)S(1)}, u32[]{:S(2)}, u32[]{:S(2)}) collective-permute-start(bf16[128,2048]{1,0:T(8,128)(2,1)S(1)} %collective-permute-done.7.refs_0_), channel_id=1, source_target_pairs={{0,4},{4,0},{8,12},{12,8},{16,20},{20,16},{24,28},{28,24},{1,5},{5... | collective-permute-start | bytes 1572872 | tf_op jit(solution)/shard_map/ppermute | solution.py:582
  27.7 1.0 %copy-start.3 = (bf16[512,256]{1,0:T(8,128)(2,1)S(1)}, bf16[512,256]{1,0:T(8,128)(2,1)}, u32[]{:S(2)}) copy-start(bf16[512,256]{1,0:T(8,128)(2,1)} %constant.4.clone.refs_0_) | copy-start | bytes 786436
  30.1 14.4 %collective-permute-start.9 = (bf16[128,2048]{1,0:T(8,128)(2,1)S(1)}, bf16[128,2048]{1,0:T(8,128)(2,1)S(1)}, u32[]{:S(2)}, u32[]{:S(2)}) collective-permute-start(bf16[128,2048]{1,0:T(8,128)(2,1)S(1)} %get-tuple-element.56.refs_1_), channel_id=1, source_target_pairs={{0,1},{1,0},{2,3},{3,2},{4,5},{5,4},{6,7},{7,6},{8,9},{9,8},{10,11... | collective-permute-start | bytes 1572872 | tf_op jit(solution)/shard_map/ppermute | solution.py:599
  31.4 13.2 %collective-permute-start.15 = (bf16[128,2048]{1,0:T(8,128)(2,1)S(1)}, bf16[128,2048]{1,0:T(8,128)(2,1)S(1)}, u32[]{:S(2)}, u32[]{:S(2)}) collective-permute-start(bf16[128,2048]{1,0:T(8,128)(2,1)S(1)} %collective-permute-done.5.refs_1_), channel_id=1, source_target_pairs={{0,4},{4,0},{8,12},{12,8},{16,20},{20,16},{24,28},{28,24},{1,5},{5... | collective-permute-start | bytes 1572872 | tf_op jit(solution)/shard_map/ppermute | solution.py:582
  31.4 6.0 %copy-start.2 = (bf16[128,2048]{1,0:T(8,128)(2,1)S(1)}, bf16[128,2048]{1,0:T(8,128)(2,1)}, u32[]{:S(2)}) copy-start(bf16[128,2048]{1,0:T(8,128)(2,1)} %refs_0_.8) | copy-start | bytes 1572868
  41.4 3.1 %collective-permute-start.14 = (bf16[128,2048]{1,0:T(8,128)(2,1)S(1)}, bf16[128,2048]{1,0:T(8,128)(2,1)S(1)}, u32[]{:S(2)}, u32[]{:S(2)}) collective-permute-start(bf16[128,2048]{1,0:T(8,128)(2,1)S(1)} %get-tuple-element.63.refs_0_), channel_id=1, source_target_pairs={{0,4},{4,0},{8,12},{12,8},{16,20},{20,16},{24,28},{28,24},{1,5},{5... | collective-permute-start | bytes 1572872 | tf_op jit(solution)/shard_map/ppermute | solution.py:582
  42.0 4.7 %collective-permute-start.11 = (bf16[128,2048]{1,0:T(8,128)(2,1)S(1)}, bf16[128,2048]{1,0:T(8,128)(2,1)S(1)}, u32[]{:S(2)}, u32[]{:S(2)}) collective-permute-start(bf16[128,2048]{1,0:T(8,128)(2,1)S(1)} %get-tuple-element.56.refs_1_), channel_id=1, source_target_pairs={{0,4},{4,0},{8,12},{12,8},{16,20},{20,16},{24,28},{28,24},{1,5},{5... | collective-permute-start | bytes 1572872 | tf_op jit(solution)/shard_map/ppermute | solution.py:582
  44.5 2.2 %collective-permute-start.10 = (bf16[128,2048]{1,0:T(8,128)(2,1)S(1)}, bf16[128,2048]{1,0:T(8,128)(2,1)S(1)}, u32[]{:S(2)}, u32[]{:S(2)}) collective-permute-start(bf16[128,2048]{1,0:T(8,128)(2,1)S(1)} %collective-permute-done.9.refs_0_), channel_id=1, source_target_pairs={{0,4},{4,0},{8,12},{12,8},{16,20},{20,16},{24,28},{28,24},{1,5},{5... | collective-permute-start | bytes 1572872 | tf_op jit(solution)/shard_map/ppermute | solution.py:582
  44.5 13.4 %copy-start.4 = (bf16[512,256]{1,0:T(8,128)(2,1)S(1)}, bf16[512,256]{1,0:T(8,128)(2,1)}, u32[]{:S(2)}) copy-start(bf16[512,256]{1,0:T(8,128)(2,1)} %constant.4.clone.refs_0_) | copy-start | bytes 786436
  44.6 13.4 %copy-start.5 = (bf16[256,512]{1,0:T(8,128)(2,1)S(1)}, bf16[256,512]{1,0:T(8,128)(2,1)}, u32[]{:S(2)}) copy-start(bf16[256,512]{1,0:T(8,128)(2,1)} %constant.5.clone.refs_1_) | copy-start | bytes 786436
  46.7 23.4 %copy-start = (bf16[128,2048]{1,0:T(8,128)(2,1)S(1)}, bf16[128,2048]{1,0:T(8,128)(2,1)}, u32[]{:S(2)}) copy-start(bf16[128,2048]{1,0:T(8,128)(2,1)} %refs_0_.9) | copy-start | bytes 1572868
  46.7 23.4 %copy-start.1 = (bf16[128,2048]{1,0:T(8,128)(2,1)S(1)}, bf16[128,2048]{1,0:T(8,128)(2,1)}, u32[]{:S(2)}) copy-start(bf16[128,2048]{1,0:T(8,128)(2,1)} %refs_1_.4) | copy-start | bytes 1572868
  48.2 6.4 %collective-permute-start.16 = (bf16[2,128,256]{2,1,0:T(8,128)(2,1)S(1)}, bf16[2,128,256]{2,1,0:T(8,128)(2,1)S(1)}, u32[]{:S(2)}, u32[]{:S(2)}) collective-permute-start(bf16[2,128,256]{2,1,0:T(8,128)(2,1)S(1)} %get-tuple-element.69), channel_id=1, source_target_pairs={{0,8},{4,12},{8,0},{12,4},{16,24},{20,28},{24,16},{28,20},{1,9},{5... | collective-permute-start | bytes 393224 | tf_op jit(solution)/shard_map/ppermute | solution.py:582
  48.7 7.6 %collective-permute-start.17 = (bf16[2,128,256]{2,1,0:T(8,128)(2,1)S(1)}, bf16[2,128,256]{2,1,0:T(8,128)(2,1)S(1)}, u32[]{:S(2)}, u32[]{:S(2)}) collective-permute-start(bf16[2,128,256]{2,1,0:T(8,128)(2,1)S(1)} %get-tuple-element.70), channel_id=1, source_target_pairs={{0,16},{4,20},{8,24},{12,28},{16,0},{20,4},{24,8},{28,12},{1,17},{... | collective-permute-start | bytes 393224 | tf_op jit(solution)/shard_map/ppermute | solution.py:582
  50.3 7.6 %collective-permute-start.18 = (bf16[2,128,256]{2,1,0:T(8,128)(2,1)S(1)}, bf16[2,128,256]{2,1,0:T(8,128)(2,1)S(1)}, u32[]{:S(2)}, u32[]{:S(2)}) collective-permute-start(bf16[2,128,256]{2,1,0:T(8,128)(2,1)S(1)} %get-tuple-element.71), channel_id=1, source_target_pairs={{0,24},{4,28},{8,16},{12,20},{16,8},{20,12},{24,0},{28,4},{1,25},{... | collective-permute-start | bytes 393224 | tf_op jit(solution)/shard_map/ppermute | solution.py:582
  61.8 3.5 %collective-permute-start.19 = (bf16[2,128,256]{2,1,0:T(8,128)(2,1)S(1)}, bf16[2,128,256]{2,1,0:T(8,128)(2,1)S(1)}, u32[]{:S(2)}, u32[]{:S(2)}) collective-permute-start(bf16[2,128,256]{2,1,0:T(8,128)(2,1)S(1)} %get-tuple-element.73), channel_id=1, source_target_pairs={{0,4},{4,0},{8,12},{12,8},{16,20},{20,16},{24,28},{28,24},{1,5},{5... | collective-permute-start | bytes 393224 | tf_op jit(solution)/shard_map/ppermute | solution.py:582
  61.8 6.3 %collective-permute-start.20 = (bf16[2,128,256]{2,1,0:T(8,128)(2,1)S(1)}, bf16[2,128,256]{2,1,0:T(8,128)(2,1)S(1)}, u32[]{:S(2)}, u32[]{:S(2)}) collective-permute-start(bf16[2,128,256]{2,1,0:T(8,128)(2,1)S(1)} %get-tuple-element.74), channel_id=1, source_target_pairs={{0,8},{4,12},{8,0},{12,4},{16,24},{20,28},{24,16},{28,20},{1,9},{5... | collective-permute-start | bytes 393224 | tf_op jit(solution)/shard_map/ppermute | solution.py:582
  62.6 7.5 %collective-permute-start.21 = (bf16[2,128,256]{2,1,0:T(8,128)(2,1)S(1)}, bf16[2,128,256]{2,1,0:T(8,128)(2,1)S(1)}, u32[]{:S(2)}, u32[]{:S(2)}) collective-permute-start(bf16[2,128,256]{2,1,0:T(8,128)(2,1)S(1)} %get-tuple-element.75), channel_id=1, source_target_pairs={{0,12},{4,8},{8,4},{12,0},{16,28},{20,24},{24,20},{28,16},{1,13},{... | collective-permute-start | bytes 393224 | tf_op jit(solution)/shard_map/ppermute | solution.py:582
  63.7 9.0 %collective-permute-start.22 = (bf16[2,128,256]{2,1,0:T(8,128)(2,1)S(1)}, bf16[2,128,256]{2,1,0:T(8,128)(2,1)S(1)}, u32[]{:S(2)}, u32[]{:S(2)}) collective-permute-start(bf16[2,128,256]{2,1,0:T(8,128)(2,1)S(1)} %get-tuple-element.77), channel_id=1, source_target_pairs={{0,16},{4,20},{8,24},{12,28},{16,0},{20,4},{24,8},{28,12},{1,17},{... | collective-permute-start | bytes 393224 | tf_op jit(solution)/shard_map/ppermute | solution.py:582
  64.5 12.6 %collective-permute-start.23 = (bf16[2,128,256]{2,1,0:T(8,128)(2,1)S(1)}, bf16[2,128,256]{2,1,0:T(8,128)(2,1)S(1)}, u32[]{:S(2)}, u32[]{:S(2)}) collective-permute-start(bf16[2,128,256]{2,1,0:T(8,128)(2,1)S(1)} %get-tuple-element.78), channel_id=1, source_target_pairs={{0,20},{4,16},{8,28},{12,24},{16,4},{20,0},{24,12},{28,8},{1,21},{... | collective-permute-start | bytes 393224 | tf_op jit(solution)/shard_map/ppermute | solution.py:582
  65.3 11.8 %collective-permute-start.24 = (bf16[2,128,256]{2,1,0:T(8,128)(2,1)S(1)}, bf16[2,128,256]{2,1,0:T(8,128)(2,1)S(1)}, u32[]{:S(2)}, u32[]{:S(2)}) collective-permute-start(bf16[2,128,256]{2,1,0:T(8,128)(2,1)S(1)} %get-tuple-element.79), channel_id=1, source_target_pairs={{0,24},{4,28},{8,16},{12,20},{16,8},{20,12},{24,0},{28,4},{1,25},{... | collective-permute-start | bytes 393224 | tf_op jit(solution)/shard_map/ppermute | solution.py:582
  68.1 9.0 %collective-permute-start.25 = (bf16[2,128,256]{2,1,0:T(8,128)(2,1)S(1)}, bf16[2,128,256]{2,1,0:T(8,128)(2,1)S(1)}, u32[]{:S(2)}, u32[]{:S(2)}) collective-permute-start(bf16[2,128,256]{2,1,0:T(8,128)(2,1)S(1)} %get-tuple-element.80), channel_id=1, source_target_pairs={{0,28},{4,24},{8,20},{12,16},{16,12},{20,8},{24,4},{28,0},{1,29},{... | collective-permute-start | bytes 393224 | tf_op jit(solution)/shard_map/ppermute | solution.py:582
  (1 other events, 0.7 us)

commit v4 on v3

--- a/solution.py
+++ b/solution.py
@@ -11,7 +11,6 @@
 from jax.sharding import PartitionSpec as P
 
 LANES = 128
-CHUNKS = 2
 
 
 def build_tables(seg_len):
@@ -369,31 +368,29 @@
     )
 
 
-def gate_kernel(chunk, parts, sizes, spot, *refs):
+def gate_kernel(sizes, spot, *refs):
     count = sum(sizes)
     groups = grouped(refs[:count], sizes)
     held, total, gates, *outs, x, sem = refs[count:]
     depth = x.shape[1]
     rows = x.shape[0] // 2
-    own_rows = rows * parts
     fetch(spot, groups, x, sem)
     for k, out in enumerate(outs):
         value = contract(x[...], held[k, :, 3 * depth : 4 * depth])
         for h, core in enumerate((spot.core, 1 - spot.core)):
-            at = h * own_rows + chunk * rows
-            mixed = total[k, at : at + rows] + value[h * rows : (h + 1) * rows]
-            gate = gates[k, h, chunk * rows : (chunk + 1) * rows].astype(jnp.float32)
-            out[core] = (mixed * gate).astype(jnp.bfloat16)
-
-
-def mix_gate(chunk, parts, groups, held, total, gates):
+            own = slice(h * rows, (h + 1) * rows)
+            mixed = total[k, own] + value[own]
+            out[core] = (mixed * gates[k, h].astype(jnp.float32)).astype(jnp.bfloat16)
+
+
+def mix_gate(groups, held, total, gates):
     chips, width, _ = held.shape
     sizes = [len(g) for g in groups]
     flat = [x for g in groups for x in g]
     rows, depth = flat[0].shape
     piece = array((2, rows, width))
     return call(
-        functools.partial(gate_kernel, chunk, parts, sizes),
+        functools.partial(gate_kernel, sizes),
         (*flat, held, total, gates),
         [ANY] * len(flat) + [VMEM] * 3,
         [piece] * chips,
@@ -483,7 +480,7 @@
         for lane in range(0, width, LANES):
             products(x, 0, lane, True)
 
-            @pl.loop(1, seg // tile)
+            @pl.loop(1, seg // tile, unroll=seg // tile - 1)
             def _(t):
                 products(x, pl.multiple_of(t * tile, tile), lane, False)
 
@@ -609,23 +606,23 @@
     gates, taps_input, (merged,) = merge(mine, [other(x) for x in packed], after=[packed_mark])
     taps_input = [swap(x, 2 * k, n) for k, x in enumerate(taps_input)]
     outer_1, inner_1 = send_outer(inner_0), send_inner(outer_0)
-    kern, tapped = tap_kernels(forward, taps_input, after=[merged])
+    held, loaded = load(out_weight, chips, after=[merged])
+    total, first = mix(0, [[grad_out], [others]], held, None, after=[loaded])
+    kern, tapped = tap_kernels(forward, taps_input, after=[first])
     outer_1, inner_1, gone = hold([outer_1, inner_1], after=[tapped])
     outer_2 = send_outer(inner_1)
-
-    held, loaded = load(out_weight, chips, after=[gone])
-    total, first = mix(0, [[grad_out], [others]], held, None, after=[loaded])
-    total, outer_1, second = mix(1, [[outer_0], [other(outer_0)]], held, total, carry=[outer_1], after=[first])
+    total, outer_1, second = mix(1, [[outer_0], [other(outer_0)]], held, total, carry=[outer_1], after=[gone])
     blocks = [[outer_1, inner_0], [other(outer_1), other(inner_0)]]
     total, _ = mix(2, blocks, held, total, after=[second])
-    gated = mix_gate(0, 1, [[outer_2, inner_1], [other(outer_2), other(inner_1)]], held, total, gates)[:chips]
+    gated = mix_gate([[outer_2, inner_1], [other(outer_2), other(inner_1)]], held, total, gates)[:chips]
     gated = [[swap(p, 2 * k, n)] for k, p in enumerate(gated)]
 
     results = correlate(forward, back, kern, gated)[:n]
-    results = [swap(x, k, n) for k, x in enumerate(results)]
-    near, far = list(range(n // 2)), list(range(n // 2, n))
-    branches, *grads, _ = finish(near, results[: n // 2], factor, key=key_branch, value=value_branch)
-    return tuple(finish(far, results[n // 2 :], factor, branches=branches, grads=grads)[:3])
+    order = sorted(range(n), key=lambda k: ((k // 2).bit_count(), k % 2, k))
+    results = {k: swap(results[k], k, n) for k in order}
+    near, far = order[: n // 2], order[n // 2 :]
+    branches, *grads, _ = finish(near, [results[k] for k in near], factor, key=key_branch, value=value_branch)
+    return tuple(finish(far, [results[k] for k in far], factor, branches=branches, grads=grads)[:3])
 
 
 def solution(mesh):

time: 79.8 us -> 77.7 us (0.974)
  waiting for transfers between devices: 27.6 us -> 24.6 us
  starting transfers between devices: 21.8 us -> 24.3 us
  local copies, waits for them, and re-layouts: 1.67 us -> 0.72 us
    ppermute x21, waiting for transfers between devices: 25.1 us -> 16 us  [swap(): return lax.ppermute(x, 'seq', [(i, i ^ k) for i in range(n)]) if k else x]
    ppermute x3, waiting for transfers between devices: 2.47 us -> 8.65 us  [send_outer(): return lax.ppermute(x, 'ch', outer)]
    ppermute x3, starting transfers between devices: 7.01 us -> 9.09 us  [send_outer(): return lax.ppermute(x, 'ch', outer)]
    unnamed x14 -> x12, local copies, waits for them, and re-layouts: 1.67 us -> 0.72 us
    ppermute x21, starting transfers between devices: 14.3 us -> 15.1 us  [swap(): return lax.ppermute(x, 'seq', [(i, i ^ k) for i in range(n)]) if k else x]
  transfers between devices with their start and end apart: 26 -> 26, of which waited for: 11 -> 11; matrix products, arithmetic and copies ran while one was open for 0% -> 0% of each run, Pallas kernels for 25% -> 26%
where the time goes in v4:
time: 77.7 us; the launch traced here: 77.5 us
  Pallas kernels  27.1 us (35%)
  waiting for transfers between devices  24.6 us (32%)
  starting transfers between devices  24.3 us (31%)
  between operations  0.81 us (1%)
    pallas_call x12, Pallas kernels, call(): pl.pallas_call(body, input_output_aliases={count + i: results + i for i i...  27.1 us
    ppermute x21, waiting for transfers between devices, swap(): return lax.ppermute(x, 'seq', [(i, i ^ k) for i in range(n)]) if k else x  16 us
    ppermute x21, starting transfers between devices, swap(): return lax.ppermute(x, 'seq', [(i, i ^ k) for i in range(n)]) if k else x  15.1 us
    ppermute x3, starting transfers between devices, send_outer(): return lax.ppermute(x, 'ch', outer)  9.09 us
    ppermute x3, waiting for transfers between devices, send_outer(): return lax.ppermute(x, 'ch', outer)  8.65 us
  transfers between devices with their start and end apart: 26, of which 11 were waited for; matrix products, arithmetic and copies ran while one was open for 0% of the time, Pallas kernels for 26%

profile of v4, /device:TPU:0, one launch (start us, length us, event | category | flops | bytes accessed | tf_op | source)
XLA Modules:
  0.0 77.5 jit_solution(9670867197006695684)
XLA Ops:
  1.2 4.1 %collective-permute-start.8 = (bf16[128,2048]{1,0:T(8,128)(2,1)}, bf16[128,2048]{1,0:T(8,128)(2,1)S(1)}, u32[]{:S(2)}, u32[]{:S(2)}) collective-permute-start(bf16[128,2048]{1,0:T(8,128)(2,1)} %refs_0_.8), channel_id=1, source_target_pairs={{0,1},{1,0},{2,3},{3,2},{4,5},{5,4},{6,7},{7,6},{8,9},{9,8},{10,11... | collective-permute-start | bytes 1572872 | tf_op jit(solution)/shard_map/ppermute | solution.py:596
  5.4 2.5 %pack_core.1 = (bf16[3,4,128,256]{3,2,1,0:T(8,128)(2,1)S(1)}, bf16[3,4,64,256]{3,2,1,0:T(8,128)(2,1)}, bf16[3,4,64,256]{3,2,1,0:T(8,128)(2,1)}, f32[8,128]{1,0:T(8,128)}) custom-call(bf16[128,2048]{1,0:T(8,128)(2,1)} %refs_0_.6, bf16[128,2048]{1,0:T(8,128)(2,1)} %refs_0_.9, bf16[128,2048]{1,0:T(8,128)(2,1)} %refs_1_.4, bf16[128,2048]{1,0:T(8,128)(2,1)} %refs_3_.1), custom_call_target="tpu_custom_call" | custom-call | tf_op jit(solution)/shard_map/pack_core/pallas_call | solution.py:179
  8.5 1.4 %collective-permute-done.refs_1_ = bf16[3,4,64,256]{3,2,1,0:T(8,128)(2,1)S(1)} collective-permute-done((bf16[3,4,64,256]{3,2,1,0:T(8,128)(2,1)}, bf16[3,4,64,256]{3,2,1,0:T(8,128)(2,1)S(1)}, u32[]{:S(2)}, u32[]{:S(2)}) %collective-permute-start) | collective-permute-done | bytes 393248 | tf_op jit(solution)/shard_map/ppermute | solution.py:579
  11.2 1.3 %merge_cores.1 = (bf16[4,2,128,256]{3,2,1,0:T(8,128)(2,1)S(1)}, bf16[2,2,128,256]{3,2,1,0:T(8,128)(2,1)S(1)}, bf16[2,2,128,256]{3,2,1,0:T(8,128)(2,1)S(1)}, bf16...) custom-call(bf16[3,4,128,256]{3,2,1,0:T(8,128)(2,1)S(1)} %get-tuple-element.45.refs_0_, ...), custom_call_target="tpu_custom_call" | custom-call | tf_op jit(solution)/shard_map/merge_cores/pallas_call | solution.py:179
  12.5 1.6 %collective-permute-start.2 = (bf16[2,2,128,256]{3,2,1,0:T(8,128)(2,1)S(1)}, bf16[2,2,128,256]{3,2,1,0:T(8,128)(2,1)S(1)}, u32[]{:S(2)}, u32[]{:S(2)}) collective-permute-start(bf16[2,2,128,256]{3,2,1,0:T(8,128)(2,1)S(1)} %get-tuple-element.50), channel_id=1, source_target_pairs={{0,8},{4,12},{8,0},{12,4},{16,24},{20,28},{24,16},{28,20},{1,9},{5... | collective-permute-start | bytes 786440 | tf_op jit(solution)/shard_map/ppermute | solution.py:579
  14.1 1.5 %collective-permute-start.3 = (bf16[2,2,128,256]{3,2,1,0:T(8,128)(2,1)S(1)}, bf16[2,2,128,256]{3,2,1,0:T(8,128)(2,1)S(1)}, u32[]{:S(2)}, u32[]{:S(2)}) collective-permute-start(bf16[2,2,128,256]{3,2,1,0:T(8,128)(2,1)S(1)} %get-tuple-element.51), channel_id=1, source_target_pairs={{0,16},{4,20},{8,24},{12,28},{16,0},{20,4},{24,8},{28,12},{1,17},{... | collective-permute-start | bytes 786440 | tf_op jit(solution)/shard_map/ppermute | solution.py:579
  16.1 2.2 %collective-permute-start.7 = (bf16[128,2048]{1,0:T(8,128)(2,1)S(1)}, bf16[128,2048]{1,0:T(8,128)(2,1)S(1)}, u32[]{:S(2)}, u32[]{:S(2)}) collective-permute-start(bf16[128,2048]{1,0:T(8,128)(2,1)S(1)} %collective-permute-done.6.refs_1_), channel_id=1, source_target_pairs={{0,1},{1,0},{2,3},{3,2},{4,5},{5,4},{6,7},{7,6},{8,9},{9,8},{10,11... | collective-permute-start | bytes 1572872 | tf_op jit(solution)/shard_map/ppermute | solution.py:596
  18.3 6.0 %load_weight.1 = (bf16[4,256,8192]{2,1,0:T(8,128)(2,1)S(1)}, f32[8,128]{1,0:T(8,128)S(1)}) custom-call(bf16[2048,8192]{1,0:T(8,128)(2,1)} %refs_0_.7, f32[8,128]{1,0:T(8,128)S(1)} %get-tuple-element.53.refs_1_), custom_call_target="tpu_custom_call" | custom-call | tf_op jit(solution)/shard_map/load_weight/pallas_call | solution.py:179
  24.4 2.0 %mix.3 = (f32[4,256,256]{2,1,0:T(8,128)S(1)}, f32[8,128]{1,0:T(8,128)S(1)}) custom-call(bf16[128,2048]{1,0:T(8,128)(2,1)S(1)} %copy-done.2, bf16[128,2048]{1,0:T(8,128)(2,1)S(1)} %collective-permute-done.5.refs_1_, bf16[4,256,8192]{2,1,0:T(8,128)(2,1)S(1)} %get-tuple-element.54.refs_2_.refs_4_, f32[8,128]{1,0:T(8,128)S(1)} %get-tuple-element.55.refs_3_), custom_call_target="tpu_custom_call" | custom-call | tf_op jit(solution)/shard_map/mix/pallas_call | solution.py:179
  26.9 0.8 %collective-permute-done.3.refs_3_ = bf16[2,2,128,256]{3,2,1,0:T(8,128)(2,1)S(1)} collective-permute-done((bf16[2,2,128,256]{3,2,1,0:T(8,128)(2,1)S(1)}, bf16[2,2,128,256]{3,2,1,0:T(8,128)(2,1)S(1)}, u32[]{:S(2)}, u32[]{:S(2)}) %collective-permute-start.3) | collective-permute-done | bytes 262176 | tf_op jit(solution)/shard_map/ppermute | solution.py:579
  27.7 1.5 %kernels.1 = (bf16[2,4,512,256]{3,2,1,0:T(8,128)(2,1)S(1)}, f32[8,128]{1,0:T(8,128)S(1)}) custom-call(bf16[512,256]{1,0:T(8,128)(2,1)S(1)} %copy-done.3, bf16[2,2,128,256]{3,2,1,0:T(8,128)(2,1)S(1)} %get-tuple-element.49.refs_1_, bf16[2,2,128,256]{3,2,1,0:T(8,128)(2,1)S(1)} %collective-permute-done.2.refs_2_, ...), custom_call_target="tpu_custom_call" | custom-call | flops 3221225472 | tf_op jit(solution)/shard_map/kernels/pallas_call | solution.py:179
  29.2 0.8 %collective-permute-done.7.refs_0_ = bf16[128,2048]{1,0:T(8,128)(2,1)S(1)} collective-permute-done((bf16[128,2048]{1,0:T(8,128)(2,1)S(1)}, bf16[128,2048]{1,0:T(8,128)(2,1)S(1)}, u32[]{:S(2)}, u32[]{:S(2)}) %collective-permute-start.7) | collective-permute-done | bytes 524320 | tf_op jit(solution)/shard_map/ppermute | solution.py:596
  30.0 2.7 %collective-permute-start.10 = (bf16[128,2048]{1,0:T(8,128)(2,1)S(1)}, bf16[128,2048]{1,0:T(8,128)(2,1)S(1)}, u32[]{:S(2)}, u32[]{:S(2)}) collective-permute-start(bf16[128,2048]{1,0:T(8,128)(2,1)S(1)} %get-tuple-element.59.refs_1_), channel_id=1, source_target_pairs={{0,1},{1,0},{2,3},{3,2},{4,5},{5,4},{6,7},{7,6},{8,9},{9,8},{10,11... | collective-permute-start | bytes 1572872 | tf_op jit(solution)/shard_map/ppermute | solution.py:596
  32.8 2.0 %mix.4 = (f32[4,256,256]{2,1,0:T(8,128)S(1)}, bf16[128,2048]{1,0:T(8,128)(2,1)S(1)}, f32[8,128]{1,0:T(8,128)S(1)}) custom-call(bf16[128,2048]{1,0:T(8,128)(2,1)S(1)} %collective-permute-done.8.refs_0_, bf16[128,2048]{1,0:T(8,128)(2,1)S(1)} %collective-permute-done.13.refs_1_, ...), custom_call_target="tpu_custom_call", output_to_operand_aliasing={{1}: (4, {})} | custom-call | tf_op jit(solution)/shard_map/mix/pallas_call | solution.py:179
  35.4 7.8 %collective-permute-done.10.refs_0_ = bf16[128,2048]{1,0:T(8,128)(2,1)S(1)} collective-permute-done((bf16[128,2048]{1,0:T(8,128)(2,1)S(1)}, bf16[128,2048]{1,0:T(8,128)(2,1)S(1)}, u32[]{:S(2)}, u32[]{:S(2)}) %collective-permute-start.10) | collective-permute-done | bytes 524320 | tf_op jit(solution)/shard_map/ppermute | solution.py:596
  43.3 2.1 %mix.5 = (f32[4,256,256]{2,1,0:T(8,128)S(1)}, f32[8,128]{1,0:T(8,128)}) custom-call(bf16[128,2048]{1,0:T(8,128)(2,1)S(1)} %get-tuple-element.63.refs_0_, bf16[128,2048]{1,0:T(8,128)(2,1)S(1)} %collective-permute-done.6.refs_1_, bf16[128,2048]{1,0:T(8,128)(2,1)S(1)} %collective-permute-done.14.refs_2_, bf16[128,2048]{1,0:T(8,128)(2,1)S(1)} %collective-permute-done.15.refs_3_, ...), custom_call_target="tpu_custom_call" | custom-call | tf_op jit(solution)/shard_map/mix/pallas_call | solution.py:179
  45.4 1.4 %mix_gate.1 = (bf16[2,128,256]{2,1,0:T(8,128)(2,1)S(1)}, bf16[2,128,256]{2,1,0:T(8,128)(2,1)S(1)}, bf16[2,128,256]{2,1,0:T(8,128)(2,1)S(1)}, bf16[2,128,256]{2,1,0:T(8,128)(2,1)S(1)}, f32[8,128]{1,0:T(8,128)}) custom-call(bf16[128,2048]{1,0:T(8,128)(2,1)S(1)} %collective-permute-done.10.refs_0_, bf16[128,2048]{1,0:T(8,128)(2,1)S(1)} %get-tuple-element.59.refs_1_, ...), custom_call_target="tpu_custom_call" | custom-call | tf_op jit(solution)/shard_map/mix_gate/pallas_call | solution.py:179
  46.9 1.6 %collective-permute-start.16 = (bf16[2,128,256]{2,1,0:T(8,128)(2,1)S(1)}, bf16[2,128,256]{2,1,0:T(8,128)(2,1)S(1)}, u32[]{:S(2)}, u32[]{:S(2)}) collective-permute-start(bf16[2,128,256]{2,1,0:T(8,128)(2,1)S(1)} %get-tuple-element.69), channel_id=1, source_target_pairs={{0,8},{4,12},{8,0},{12,4},{16,24},{20,28},{24,16},{28,20},{1,9},{5... | collective-permute-start | bytes 393224 | tf_op jit(solution)/shard_map/ppermute | solution.py:579
  48.4 1.5 %collective-permute-start.17 = (bf16[2,128,256]{2,1,0:T(8,128)(2,1)S(1)}, bf16[2,128,256]{2,1,0:T(8,128)(2,1)S(1)}, u32[]{:S(2)}, u32[]{:S(2)}) collective-permute-start(bf16[2,128,256]{2,1,0:T(8,128)(2,1)S(1)} %get-tuple-element.70), channel_id=1, source_target_pairs={{0,16},{4,20},{8,24},{12,28},{16,0},{20,4},{24,8},{28,12},{1,17},{... | collective-permute-start | bytes 393224 | tf_op jit(solution)/shard_map/ppermute | solution.py:579
  50.4 2.8 %collective-permute-done.16.refs_4_ = bf16[2,128,256]{2,1,0:T(8,128)(2,1)S(1)} collective-permute-done((bf16[2,128,256]{2,1,0:T(8,128)(2,1)S(1)}, bf16[2,128,256]{2,1,0:T(8,128)(2,1)S(1)}, u32[]{:S(2)}, u32[]{:S(2)}) %collective-permute-start.16) | collective-permute-done | bytes 131104 | tf_op jit(solution)/shard_map/ppermute | solution.py:579
  53.2 3.6 %collective-permute-done.17.refs_5_ = bf16[2,128,256]{2,1,0:T(8,128)(2,1)S(1)} collective-permute-done((bf16[2,128,256]{2,1,0:T(8,128)(2,1)S(1)}, bf16[2,128,256]{2,1,0:T(8,128)(2,1)S(1)}, u32[]{:S(2)}, u32[]{:S(2)}) %collective-permute-start.17) | collective-permute-done | bytes 131104 | tf_op jit(solution)/shard_map/ppermute | solution.py:579
  56.9 3.4 %correlate.1 = (bf16[2,128,256]{2,1,0:T(8,128)(2,1)S(1)}, bf16[2,128,256]{2,1,0:T(8,128)(2,1)S(1)}, bf16[2,128,256]{2,1,0:T(8,128)(2,1)S(1)}, bf16[2,128,256]{2,...) custom-call(bf16[512,256]{1,0:T(8,128)(2,1)S(1)} %copy-done.3, ...), custom_call_target="tpu_custom_call" | custom-call | tf_op jit(solution)/shard_map/correlate/pallas_call | solution.py:179
  60.2 1.2 %collective-permute-start.20 = (bf16[2,128,256]{2,1,0:T(8,128)(2,1)S(1)}, bf16[2,128,256]{2,1,0:T(8,128)(2,1)S(1)}, u32[]{:S(2)}, u32[]{:S(2)}) collective-permute-start(bf16[2,128,256]{2,1,0:T(8,128)(2,1)S(1)} %get-tuple-element.74), channel_id=1, source_target_pairs={{0,8},{4,12},{8,0},{12,4},{16,24},{20,28},{24,16},{28,20},{1,9},{5... | collective-permute-start | bytes 393224 | tf_op jit(solution)/shard_map/ppermute | solution.py:579
  61.5 0.8 %collective-permute-start.21 = (bf16[2,128,256]{2,1,0:T(8,128)(2,1)S(1)}, bf16[2,128,256]{2,1,0:T(8,128)(2,1)S(1)}, u32[]{:S(2)}, u32[]{:S(2)}) collective-permute-start(bf16[2,128,256]{2,1,0:T(8,128)(2,1)S(1)} %get-tuple-element.75), channel_id=1, source_target_pairs={{0,16},{4,20},{8,24},{12,28},{16,0},{20,4},{24,8},{28,12},{1,17},{... | collective-permute-start | bytes 393224 | tf_op jit(solution)/shard_map/ppermute | solution.py:579
  62.3 1.0 %collective-permute-start.22 = (bf16[2,128,256]{2,1,0:T(8,128)(2,1)S(1)}, bf16[2,128,256]{2,1,0:T(8,128)(2,1)S(1)}, u32[]{:S(2)}, u32[]{:S(2)}) collective-permute-start(bf16[2,128,256]{2,1,0:T(8,128)(2,1)S(1)} %get-tuple-element.77), channel_id=1, source_target_pairs={{0,12},{4,8},{8,4},{12,0},{16,28},{20,24},{24,20},{28,16},{1,13},{... | collective-permute-start | bytes 393224 | tf_op jit(solution)/shard_map/ppermute | solution.py:579
  64.0 1.5 %collective-permute-start.24 = (bf16[2,128,256]{2,1,0:T(8,128)(2,1)S(1)}, bf16[2,128,256]{2,1,0:T(8,128)(2,1)S(1)}, u32[]{:S(2)}, u32[]{:S(2)}) collective-permute-start(bf16[2,128,256]{2,1,0:T(8,128)(2,1)S(1)} %get-tuple-element.79), channel_id=1, source_target_pairs={{0,24},{4,28},{8,16},{12,20},{16,8},{20,12},{24,0},{28,4},{1,25},{... | collective-permute-start | bytes 393224 | tf_op jit(solution)/shard_map/ppermute | solution.py:579
  65.5 1.0 %collective-permute-done.20.refs_4_ = bf16[2,128,256]{2,1,0:T(8,128)(2,1)S(1)} collective-permute-done((bf16[2,128,256]{2,1,0:T(8,128)(2,1)S(1)}, bf16[2,128,256]{2,1,0:T(8,128)(2,1)S(1)}, u32[]{:S(2)}, u32[]{:S(2)}) %collective-permute-start.20) | collective-permute-done | bytes 131104 | tf_op jit(solution)/shard_map/ppermute | solution.py:579
  67.0 0.8 %collective-permute-done.21.refs_5_ = bf16[2,128,256]{2,1,0:T(8,128)(2,1)S(1)} collective-permute-done((bf16[2,128,256]{2,1,0:T(8,128)(2,1)S(1)}, bf16[2,128,256]{2,1,0:T(8,128)(2,1)S(1)}, u32[]{:S(2)}, u32[]{:S(2)}) %collective-permute-start.21) | collective-permute-done | bytes 131104 | tf_op jit(solution)/shard_map/ppermute | solution.py:579
  67.8 2.5 %finish.2 = (bf16[2,128,2048]{2,1,0:T(8,128)(2,1)S(1)}, bf16[128,2048]{1,0:T(8,128)(2,1)}, bf16[128,2048]{1,0:T(8,128)(2,1)}, f32[128,2048]{1,0:T(8,128)}, f32[8,128]{1,0:T(8,128)}) custom-call(bf16[128,2048]{1,0:T(8,128)(2,1)S(1)} %copy-done, bf16[128,2048]{1,0:T(8,128)(2,1)S(1)} %copy-done.1, bf16[2,128,256]{2,1,0:T(8,128)(2,1)S(1)} %get-tuple-element.72.refs_2_, ...), custom_call_target="tpu_custom_call" | custom-call | tf_op jit(solution)/shard_map/finish/pallas_call | solution.py:179
  70.3 3.6 %collective-permute-done.23.refs_2_ = bf16[2,128,256]{2,1,0:T(8,128)(2,1)S(1)} collective-permute-done((bf16[2,128,256]{2,1,0:T(8,128)(2,1)S(1)}, bf16[2,128,256]{2,1,0:T(8,128)(2,1)S(1)}, u32[]{:S(2)}, u32[]{:S(2)}) %collective-permute-start.23) | collective-permute-done | bytes 131104 | tf_op jit(solution)/shard_map/ppermute | solution.py:579
  73.9 1.2 %collective-permute-done.25.refs_4_ = bf16[2,128,256]{2,1,0:T(8,128)(2,1)S(1)} collective-permute-done((bf16[2,128,256]{2,1,0:T(8,128)(2,1)S(1)}, bf16[2,128,256]{2,1,0:T(8,128)(2,1)S(1)}, u32[]{:S(2)}, u32[]{:S(2)}) %collective-permute-start.25) | collective-permute-done | bytes 131104 | tf_op jit(solution)/shard_map/ppermute | solution.py:579
  75.1 2.4 %finish.3 = (bf16[128,2048]{1,0:T(8,128)(2,1)}, bf16[128,2048]{1,0:T(8,128)(2,1)}, f32[128,2048]{1,0:T(8,128)}, f32[8,128]{1,0:T(8,128)}) custom-call(bf16[2,128,2048]{2,1,0:T(8,128)(2,1)S(1)} %get-tuple-element.76.refs_0_, bf16[2,128,256]{2,1,0:T(8,128)(2,1)S(1)} %collective-permute-done.22.refs_1_, ...), custom_call_target="tpu_custom_call", output_to_operand_aliasing={{0}: (5, {}), {1}: (6, {}), {2}: (7, {})} | custom-call | tf_op jit(solution)/shard_map/finish/pallas_call | solution.py:179
  (44 shorter events, 5.8 us)
Async XLA Ops:
  0.6 14.9 %collective-permute-start.5 = (bf16[128,2048]{1,0:T(8,128)(2,1)}, bf16[128,2048]{1,0:T(8,128)(2,1)S(1)}, u32[]{:S(2)}, u32[]{:S(2)}) collective-permute-start(bf16[128,2048]{1,0:T(8,128)(2,1)} %refs_0_.8), channel_id=1, source_target_pairs={{0,4},{4,0},{8,12},{12,8},{16,20},{20,16},{24,28},{28,24},{1,5},{5... | collective-permute-start | bytes 1572872 | tf_op jit(solution)/shard_map/ppermute | solution.py:579
  1.1 14.9 %collective-permute-start.6 = (bf16[128,2048]{1,0:T(8,128)(2,1)}, bf16[128,2048]{1,0:T(8,128)(2,1)S(1)}, u32[]{:S(2)}, u32[]{:S(2)}) collective-permute-start(bf16[128,2048]{1,0:T(8,128)(2,1)} %refs_0_.8), channel_id=1, source_target_pairs={{1,2},{2,1},{0,4},{3,7},{5,6},{6,5},{4,0},{7,3},{9,10},{10,9},{8,1... | collective-permute-start | bytes 1572872 | tf_op jit(solution)/shard_map/ppermute | solution.py:599
  1.2 17.1 %collective-permute-start.8 = (bf16[128,2048]{1,0:T(8,128)(2,1)}, bf16[128,2048]{1,0:T(8,128)(2,1)S(1)}, u32[]{:S(2)}, u32[]{:S(2)}) collective-permute-start(bf16[128,2048]{1,0:T(8,128)(2,1)} %refs_0_.8), channel_id=1, source_target_pairs={{0,1},{1,0},{2,3},{3,2},{4,5},{5,4},{6,7},{7,6},{8,9},{9,8},{10,11... | collective-permute-start | bytes 1572872 | tf_op jit(solution)/shard_map/ppermute | solution.py:596
  7.9 2.0 %collective-permute-start = (bf16[3,4,64,256]{3,2,1,0:T(8,128)(2,1)}, bf16[3,4,64,256]{3,2,1,0:T(8,128)(2,1)S(1)}, u32[]{:S(2)}, u32[]{:S(2)}) collective-permute-start(bf16[3,4,64,256]{3,2,1,0:T(8,128)(2,1)} %get-tuple-element.46), channel_id=1, source_target_pairs={{0,4},{4,0},{8,12},{12,8},{16,20},{20,16},{24,28},{28,24},{1,5},{5... | collective-permute-start | bytes 1179656 | tf_op jit(solution)/shard_map/ppermute | solution.py:579
  8.0 2.5 %collective-permute-start.1 = (bf16[3,4,64,256]{3,2,1,0:T(8,128)(2,1)}, bf16[3,4,64,256]{3,2,1,0:T(8,128)(2,1)S(1)}, u32[]{:S(2)}, u32[]{:S(2)}) collective-permute-start(bf16[3,4,64,256]{3,2,1,0:T(8,128)(2,1)} %get-tuple-element.47), channel_id=1, source_target_pairs={{0,4},{4,0},{8,12},{12,8},{16,20},{20,16},{24,28},{28,24},{1,5},{5... | collective-permute-start | bytes 1179656 | tf_op jit(solution)/shard_map/ppermute | solution.py:579
  10.5 0.7 copy-start.5
  12.5 13.9 %collective-permute-start.2 = (bf16[2,2,128,256]{3,2,1,0:T(8,128)(2,1)S(1)}, bf16[2,2,128,256]{3,2,1,0:T(8,128)(2,1)S(1)}, u32[]{:S(2)}, u32[]{:S(2)}) collective-permute-start(bf16[2,2,128,256]{3,2,1,0:T(8,128)(2,1)S(1)} %get-tuple-element.50), channel_id=1, source_target_pairs={{0,8},{4,12},{8,0},{12,4},{16,24},{20,28},{24,16},{28,20},{1,9},{5... | collective-permute-start | bytes 786440 | tf_op jit(solution)/shard_map/ppermute | solution.py:579
  14.1 13.7 %collective-permute-start.3 = (bf16[2,2,128,256]{3,2,1,0:T(8,128)(2,1)S(1)}, bf16[2,2,128,256]{3,2,1,0:T(8,128)(2,1)S(1)}, u32[]{:S(2)}, u32[]{:S(2)}) collective-permute-start(bf16[2,2,128,256]{3,2,1,0:T(8,128)(2,1)S(1)} %get-tuple-element.51), channel_id=1, source_target_pairs={{0,16},{4,20},{8,24},{12,28},{16,0},{20,4},{24,8},{28,12},{1,17},{... | collective-permute-start | bytes 786440 | tf_op jit(solution)/shard_map/ppermute | solution.py:579
  15.6 12.2 %collective-permute-start.4 = (bf16[2,2,128,256]{3,2,1,0:T(8,128)(2,1)S(1)}, bf16[2,2,128,256]{3,2,1,0:T(8,128)(2,1)S(1)}, u32[]{:S(2)}, u32[]{:S(2)}) collective-permute-start(bf16[2,2,128,256]{3,2,1,0:T(8,128)(2,1)S(1)} %get-tuple-element.52), channel_id=1, source_target_pairs={{0,24},{4,28},{8,16},{12,20},{16,8},{20,12},{24,0},{28,4},{1,25},{... | collective-permute-start | bytes 786440 | tf_op jit(solution)/shard_map/ppermute | solution.py:579
  16.1 14.0 %collective-permute-start.7 = (bf16[128,2048]{1,0:T(8,128)(2,1)S(1)}, bf16[128,2048]{1,0:T(8,128)(2,1)S(1)}, u32[]{:S(2)}, u32[]{:S(2)}) collective-permute-start(bf16[128,2048]{1,0:T(8,128)(2,1)S(1)} %collective-permute-done.6.refs_1_), channel_id=1, source_target_pairs={{0,1},{1,0},{2,3},{3,2},{4,5},{5,4},{6,7},{7,6},{8,9},{9,8},{10,11... | collective-permute-start | bytes 1572872 | tf_op jit(solution)/shard_map/ppermute | solution.py:596
  18.3 11.7 %collective-permute-start.9 = (bf16[128,2048]{1,0:T(8,128)(2,1)S(1)}, bf16[128,2048]{1,0:T(8,128)(2,1)S(1)}, u32[]{:S(2)}, u32[]{:S(2)}) collective-permute-start(bf16[128,2048]{1,0:T(8,128)(2,1)S(1)} %collective-permute-done.8.refs_0_), channel_id=1, source_target_pairs={{1,2},{2,1},{0,4},{3,7},{5,6},{6,5},{4,0},{7,3},{9,10},{10,9},{8,1... | collective-permute-start | bytes 1572872 | tf_op jit(solution)/shard_map/ppermute | solution.py:599
  18.3 6.1 %copy-start.2 = (bf16[128,2048]{1,0:T(8,128)(2,1)S(1)}, bf16[128,2048]{1,0:T(8,128)(2,1)}, u32[]{:S(2)}) copy-start(bf16[128,2048]{1,0:T(8,128)(2,1)} %refs_0_.8) | copy-start | bytes 1572868
  24.3 3.4 %copy-start.3 = (bf16[512,256]{1,0:T(8,128)(2,1)S(1)}, bf16[512,256]{1,0:T(8,128)(2,1)}, u32[]{:S(2)}) copy-start(bf16[512,256]{1,0:T(8,128)(2,1)} %constant.4.clone.refs_0_) | copy-start | bytes 786436
  26.4 6.4 %collective-permute-start.13 = (bf16[128,2048]{1,0:T(8,128)(2,1)S(1)}, bf16[128,2048]{1,0:T(8,128)(2,1)S(1)}, u32[]{:S(2)}, u32[]{:S(2)}) collective-permute-start(bf16[128,2048]{1,0:T(8,128)(2,1)S(1)} %collective-permute-done.8.refs_0_), channel_id=1, source_target_pairs={{0,4},{4,0},{8,12},{12,8},{16,20},{20,16},{24,28},{28,24},{1,5},{5... | collective-permute-start | bytes 1572872 | tf_op jit(solution)/shard_map/ppermute | solution.py:579
  30.0 13.2 %collective-permute-start.10 = (bf16[128,2048]{1,0:T(8,128)(2,1)S(1)}, bf16[128,2048]{1,0:T(8,128)(2,1)S(1)}, u32[]{:S(2)}, u32[]{:S(2)}) collective-permute-start(bf16[128,2048]{1,0:T(8,128)(2,1)S(1)} %get-tuple-element.59.refs_1_), channel_id=1, source_target_pairs={{0,1},{1,0},{2,3},{3,2},{4,5},{5,4},{6,7},{7,6},{8,9},{9,8},{10,11... | collective-permute-start | bytes 1572872 | tf_op jit(solution)/shard_map/ppermute | solution.py:596
  32.7 10.5 %collective-permute-start.15 = (bf16[128,2048]{1,0:T(8,128)(2,1)S(1)}, bf16[128,2048]{1,0:T(8,128)(2,1)S(1)}, u32[]{:S(2)}, u32[]{:S(2)}) collective-permute-start(bf16[128,2048]{1,0:T(8,128)(2,1)S(1)} %collective-permute-done.6.refs_1_), channel_id=1, source_target_pairs={{0,4},{4,0},{8,12},{12,8},{16,20},{20,16},{24,28},{28,24},{1,5},{5... | collective-permute-start | bytes 1572872 | tf_op jit(solution)/shard_map/ppermute | solution.py:579
  34.7 8.5 %collective-permute-start.14 = (bf16[128,2048]{1,0:T(8,128)(2,1)S(1)}, bf16[128,2048]{1,0:T(8,128)(2,1)S(1)}, u32[]{:S(2)}, u32[]{:S(2)}) collective-permute-start(bf16[128,2048]{1,0:T(8,128)(2,1)S(1)} %get-tuple-element.63.refs_0_), channel_id=1, source_target_pairs={{0,4},{4,0},{8,12},{12,8},{16,20},{20,16},{24,28},{28,24},{1,5},{5... | collective-permute-start | bytes 1572872 | tf_op jit(solution)/shard_map/ppermute | solution.py:579
  35.3 10.1 %collective-permute-start.12 = (bf16[128,2048]{1,0:T(8,128)(2,1)S(1)}, bf16[128,2048]{1,0:T(8,128)(2,1)S(1)}, u32[]{:S(2)}, u32[]{:S(2)}) collective-permute-start(bf16[128,2048]{1,0:T(8,128)(2,1)S(1)} %get-tuple-element.59.refs_1_), channel_id=1, source_target_pairs={{0,4},{4,0},{8,12},{12,8},{16,20},{20,16},{24,28},{28,24},{1,5},{5... | collective-permute-start | bytes 1572872 | tf_op jit(solution)/shard_map/ppermute | solution.py:579
  43.2 2.2 %collective-permute-start.11 = (bf16[128,2048]{1,0:T(8,128)(2,1)S(1)}, bf16[128,2048]{1,0:T(8,128)(2,1)S(1)}, u32[]{:S(2)}, u32[]{:S(2)}) collective-permute-start(bf16[128,2048]{1,0:T(8,128)(2,1)S(1)} %collective-permute-done.10.refs_0_), channel_id=1, source_target_pairs={{0,4},{4,0},{8,12},{12,8},{16,20},{20,16},{24,28},{28,24},{1,5},{5... | collective-permute-start | bytes 1572872 | tf_op jit(solution)/shard_map/ppermute | solution.py:579
  43.3 13.6 %copy-start.4 = (bf16[256,512]{1,0:T(8,128)(2,1)S(1)}, bf16[256,512]{1,0:T(8,128)(2,1)}, u32[]{:S(2)}) copy-start(bf16[256,512]{1,0:T(8,128)(2,1)} %constant.5.clone.refs_1_) | copy-start | bytes 786436
  45.4 22.4 %copy-start = (bf16[128,2048]{1,0:T(8,128)(2,1)S(1)}, bf16[128,2048]{1,0:T(8,128)(2,1)}, u32[]{:S(2)}) copy-start(bf16[128,2048]{1,0:T(8,128)(2,1)} %refs_0_.9) | copy-start | bytes 1572868
  45.4 22.4 %copy-start.1 = (bf16[128,2048]{1,0:T(8,128)(2,1)S(1)}, bf16[128,2048]{1,0:T(8,128)(2,1)}, u32[]{:S(2)}) copy-start(bf16[128,2048]{1,0:T(8,128)(2,1)} %refs_1_.4) | copy-start | bytes 1572868
  46.9 6.4 %collective-permute-start.16 = (bf16[2,128,256]{2,1,0:T(8,128)(2,1)S(1)}, bf16[2,128,256]{2,1,0:T(8,128)(2,1)S(1)}, u32[]{:S(2)}, u32[]{:S(2)}) collective-permute-start(bf16[2,128,256]{2,1,0:T(8,128)(2,1)S(1)} %get-tuple-element.69), channel_id=1, source_target_pairs={{0,8},{4,12},{8,0},{12,4},{16,24},{20,28},{24,16},{28,20},{1,9},{5... | collective-permute-start | bytes 393224 | tf_op jit(solution)/shard_map/ppermute | solution.py:579
  48.4 8.4 %collective-permute-start.17 = (bf16[2,128,256]{2,1,0:T(8,128)(2,1)S(1)}, bf16[2,128,256]{2,1,0:T(8,128)(2,1)S(1)}, u32[]{:S(2)}, u32[]{:S(2)}) collective-permute-start(bf16[2,128,256]{2,1,0:T(8,128)(2,1)S(1)} %get-tuple-element.70), channel_id=1, source_target_pairs={{0,16},{4,20},{8,24},{12,28},{16,0},{20,4},{24,8},{28,12},{1,17},{... | collective-permute-start | bytes 393224 | tf_op jit(solution)/shard_map/ppermute | solution.py:579
  50.0 6.9 %collective-permute-start.18 = (bf16[2,128,256]{2,1,0:T(8,128)(2,1)S(1)}, bf16[2,128,256]{2,1,0:T(8,128)(2,1)S(1)}, u32[]{:S(2)}, u32[]{:S(2)}) collective-permute-start(bf16[2,128,256]{2,1,0:T(8,128)(2,1)S(1)} %get-tuple-element.71), channel_id=1, source_target_pairs={{0,24},{4,28},{8,16},{12,20},{16,8},{20,12},{24,0},{28,4},{1,25},{... | collective-permute-start | bytes 393224 | tf_op jit(solution)/shard_map/ppermute | solution.py:579
  60.2 3.8 %collective-permute-start.19 = (bf16[2,128,256]{2,1,0:T(8,128)(2,1)S(1)}, bf16[2,128,256]{2,1,0:T(8,128)(2,1)S(1)}, u32[]{:S(2)}, u32[]{:S(2)}) collective-permute-start(bf16[2,128,256]{2,1,0:T(8,128)(2,1)S(1)} %get-tuple-element.73), channel_id=1, source_target_pairs={{0,4},{4,0},{8,12},{12,8},{16,20},{20,16},{24,28},{28,24},{1,5},{5... | collective-permute-start | bytes 393224 | tf_op jit(solution)/shard_map/ppermute | solution.py:579
  60.2 6.3 %collective-permute-start.20 = (bf16[2,128,256]{2,1,0:T(8,128)(2,1)S(1)}, bf16[2,128,256]{2,1,0:T(8,128)(2,1)S(1)}, u32[]{:S(2)}, u32[]{:S(2)}) collective-permute-start(bf16[2,128,256]{2,1,0:T(8,128)(2,1)S(1)} %get-tuple-element.74), channel_id=1, source_target_pairs={{0,8},{4,12},{8,0},{12,4},{16,24},{20,28},{24,16},{28,20},{1,9},{5... | collective-permute-start | bytes 393224 | tf_op jit(solution)/shard_map/ppermute | solution.py:579
  61.5 6.3 %collective-permute-start.21 = (bf16[2,128,256]{2,1,0:T(8,128)(2,1)S(1)}, bf16[2,128,256]{2,1,0:T(8,128)(2,1)S(1)}, u32[]{:S(2)}, u32[]{:S(2)}) collective-permute-start(bf16[2,128,256]{2,1,0:T(8,128)(2,1)S(1)} %get-tuple-element.75), channel_id=1, source_target_pairs={{0,16},{4,20},{8,24},{12,28},{16,0},{20,4},{24,8},{28,12},{1,17},{... | collective-permute-start | bytes 393224 | tf_op jit(solution)/shard_map/ppermute | solution.py:579
  62.3 8.0 %collective-permute-start.22 = (bf16[2,128,256]{2,1,0:T(8,128)(2,1)S(1)}, bf16[2,128,256]{2,1,0:T(8,128)(2,1)S(1)}, u32[]{:S(2)}, u32[]{:S(2)}) collective-permute-start(bf16[2,128,256]{2,1,0:T(8,128)(2,1)S(1)} %get-tuple-element.77), channel_id=1, source_target_pairs={{0,12},{4,8},{8,4},{12,0},{16,28},{20,24},{24,20},{28,16},{1,13},{... | collective-permute-start | bytes 393224 | tf_op jit(solution)/shard_map/ppermute | solution.py:579
  63.3 10.6 %collective-permute-start.23 = (bf16[2,128,256]{2,1,0:T(8,128)(2,1)S(1)}, bf16[2,128,256]{2,1,0:T(8,128)(2,1)S(1)}, u32[]{:S(2)}, u32[]{:S(2)}) collective-permute-start(bf16[2,128,256]{2,1,0:T(8,128)(2,1)S(1)} %get-tuple-element.78), channel_id=1, source_target_pairs={{0,20},{4,16},{8,28},{12,24},{16,4},{20,0},{24,12},{28,8},{1,21},{... | collective-permute-start | bytes 393224 | tf_op jit(solution)/shard_map/ppermute | solution.py:579
  64.0 9.9 %collective-permute-start.24 = (bf16[2,128,256]{2,1,0:T(8,128)(2,1)S(1)}, bf16[2,128,256]{2,1,0:T(8,128)(2,1)S(1)}, u32[]{:S(2)}, u32[]{:S(2)}) collective-permute-start(bf16[2,128,256]{2,1,0:T(8,128)(2,1)S(1)} %get-tuple-element.79), channel_id=1, source_target_pairs={{0,24},{4,28},{8,16},{12,20},{16,8},{20,12},{24,0},{28,4},{1,25},{... | collective-permute-start | bytes 393224 | tf_op jit(solution)/shard_map/ppermute | solution.py:579
  66.5 8.6 %collective-permute-start.25 = (bf16[2,128,256]{2,1,0:T(8,128)(2,1)S(1)}, bf16[2,128,256]{2,1,0:T(8,128)(2,1)S(1)}, u32[]{:S(2)}, u32[]{:S(2)}) collective-permute-start(bf16[2,128,256]{2,1,0:T(8,128)(2,1)S(1)} %get-tuple-element.80), channel_id=1, source_target_pairs={{0,28},{4,24},{8,20},{12,16},{16,12},{20,8},{24,4},{28,0},{1,29},{... | collective-permute-start | bytes 393224 | tf_op jit(solution)/shard_map/ppermute | solution.py:579

commit v5 on v4

--- a/solution.py
+++ b/solution.py
@@ -435,21 +435,18 @@
     )
 
 
-def correlate_kernel(parts, spot, forward, back, kern, *refs):
+def correlate_kernel(ks, spot, forward, back, kern, *refs):
     segs = kern.shape[1]
     n = 2 * segs
-    pieces = refs[: segs * parts]
-    outs = refs[segs * parts : segs * parts + n]
-    data, spec, acc, result = refs[segs * parts + n :]
-    part = pieces[0].shape[1]
-    rows = part * parts
+    pieces = refs[:segs]
+    outs = refs[segs : segs + n]
+    data, spec, acc, result = refs[segs + n :]
+    rows = pieces[0].shape[1]
     seg = 2 * rows
     width = data.shape[2]
-    for k in range(segs):
-        for c in range(parts):
-            for core in range(2):
-                at = core * rows + c * part
-                data[spot.chip ^ k, at : at + part] = pieces[k * parts + c][core]
+    for k, piece in zip(ks, pieces):
+        for core in range(2):
+            data[spot.chip ^ k, core * rows : (core + 1) * rows] = piece[core]
     for i in range(segs):
         spec[i] = jnp.dot(forward[...], data[i], preferred_element_type=jnp.float32)
 
@@ -494,15 +491,14 @@
 
 
 def correlate(forward, back, kern, pieces):
-    segs, parts = len(pieces), len(pieces[0])
-    flat = [p for group in pieces for p in group]
-    width = flat[0].shape[2]
-    rows = flat[0].shape[1] * parts
+    ks, flat = tuple(pieces), tuple(pieces.values())
+    segs = len(flat)
+    _, rows, width = flat[0].shape
     seg = 2 * rows
     n = 2 * segs
     out = array((2, rows, width))
     return call(
-        functools.partial(correlate_kernel, parts),
+        functools.partial(correlate_kernel, ks),
         (forward, back, kern, *flat),
         [whole(forward), whole(back), VMEM] + [whole(p) for p in flat],
         [out] * n,
@@ -521,13 +517,13 @@
     n = len(ks)
     if fetch_branches:
         (key, value, *pieces), refs = refs[: 2 + n], refs[2 + n :]
-        branches, *outs, piece_v, key_o, value_o, filter_o, in_sem, out_sem = refs
+        branches, *outs, key_o, value_o, filter_o, in_sem, out_sem = refs
     else:
         (branches, *pieces), refs = refs[: 1 + n], refs[1 + n :]
-        *outs, piece_v, key_o, value_o, filter_o, in_sem, out_sem = refs
-    width = piece_v.shape[3]
+        *outs, key_o, value_o, filter_o, in_sem, out_sem = refs
+    width = pieces[0].shape[2]
     me = 2 * spot.chip + spot.core
-    loads = [pltpu.make_async_copy(p, piece_v.at[i], in_sem.at[i]) for i, p in enumerate(pieces)]
+    loads = []
     if fetch_branches:
         loads.append(pltpu.make_async_copy(key, branches.at[0], in_sem.at[n]))
         loads.append(pltpu.make_async_copy(value, branches.at[1], in_sem.at[n + 1]))
@@ -538,10 +534,10 @@
     stores = []
     for i, k in enumerate(ks):
         here = (slice(None), pl.ds(pl.multiple_of((me ^ k) * width, width), width))
-        conv_grad = piece_v[i, 0].astype(jnp.float32)
+        conv_grad = pieces[i][0].astype(jnp.float32)
         key_o[i] = (conv_grad * branches[(1, *here)].astype(jnp.float32)).astype(jnp.bfloat16)
         value_o[i] = (conv_grad * branches[(0, *here)].astype(jnp.float32)).astype(jnp.bfloat16)
-        filter_o[i] = piece_v[i, 1].astype(jnp.float32) * factor
+        filter_o[i] = pieces[i][1].astype(jnp.float32) * factor
         for o, (src, dst) in enumerate(zip((key_o, value_o, filter_o), outs)):
             stores.append(pltpu.make_async_copy(src.at[i], dst.at[here], out_sem.at[o, i]))
             stores[-1].start()
@@ -554,7 +550,6 @@
     n = len(ks)
     rows, width = pieces[0].shape[1:]
     scratch = [
-        pltpu.VMEM((n, 2, rows, width), jnp.bfloat16),
         pltpu.VMEM((n, rows, width), jnp.bfloat16),
         pltpu.VMEM((n, rows, width), jnp.bfloat16),
         pltpu.VMEM((n, rows, width), jnp.float32),
@@ -566,9 +561,9 @@
         both = pltpu.VMEM((2, *key.shape), key.dtype)
         outs = [both, array(key.shape), array(key.shape), array(key.shape, jnp.float32)]
         args = (key, value, *pieces)
-        return call(kernel, args, [ANY] * len(args), outs, [VMEM, *[ANY] * 3], "finish", scratch)
+        return call(kernel, args, [ANY, ANY, *[VMEM] * n], outs, [VMEM, *[ANY] * 3], "finish", scratch)
     args = (branches, *pieces)
-    return call(kernel, args, [VMEM, *[ANY] * n], [], [], "finish", scratch, update=grads)
+    return call(kernel, args, [VMEM] * (1 + n), [], [], "finish", scratch, update=grads)
 
 
 def hold(arrays, after):
@@ -615,7 +610,8 @@
     blocks = [[outer_1, inner_0], [other(outer_1), other(inner_0)]]
     total, _ = mix(2, blocks, held, total, after=[second])
     gated = mix_gate([[outer_2, inner_1], [other(outer_2), other(inner_1)]], held, total, gates)[:chips]
-    gated = [[swap(p, 2 * k, n)] for k, p in enumerate(gated)]
+    order = [0, *sorted(range(1, chips), key=lambda k: (-k.bit_count(), -k))]
+    gated = {k: swap(gated[k], 2 * k, n) for k in order}
 
     results = correlate(forward, back, kern, gated)[:n]
     order = sorted(range(n), key=lambda k: ((k // 2).bit_count(), k % 2, k))

time: 77.7 us -> 76.9 us (0.990)
  Pallas kernels: 27.1 us -> 25.8 us
    pallas_call x12, Pallas kernels: 27.1 us -> 25.8 us  [call(): pl.pallas_call(body, input_output_aliases={count + i: results + i for i i...]
  transfers between devices with their start and end apart: 26 -> 26, of which waited for: 11 -> 12; matrix products, arithmetic and copies ran while one was open for 0% -> 0% of each run, Pallas kernels for 26% -> 25%
where the time goes in v5:
time: 76.9 us; the launch traced here: 76.6 us
  Pallas kernels  25.8 us (34%)
  waiting for transfers between devices  24.7 us (32%)
  starting transfers between devices  24.6 us (32%)
  between operations  0.81 us (1%)
    pallas_call x12, Pallas kernels, call(): pl.pallas_call(body, input_output_aliases={count + i: results + i for i i...  25.8 us
    ppermute x21, waiting for transfers between devices, swap(): return lax.ppermute(x, 'seq', [(i, i ^ k) for i in range(n)]) if k else x  16.1 us
    ppermute x21, starting transfers between devices, swap(): return lax.ppermute(x, 'seq', [(i, i ^ k) for i in range(n)]) if k else x  15.4 us
    ppermute x3, starting transfers between devices, send_outer(): return lax.ppermute(x, 'ch', outer)  9.09 us
    ppermute x3, waiting for transfers between devices, send_outer(): return lax.ppermute(x, 'ch', outer)  8.65 us
  transfers between devices with their start and end apart: 26, of which 12 were waited for; matrix products, arithmetic and copies ran while one was open for 0% of the time, Pallas kernels for 25%

profile of v5, /device:TPU:0, one launch (start us, length us, event | category | flops | bytes accessed | tf_op | source)
XLA Modules:
  0.0 76.6 jit_solution(17857506939487838435)
XLA Ops:
  1.2 4.1 %collective-permute-start.8 = (bf16[128,2048]{1,0:T(8,128)(2,1)}, bf16[128,2048]{1,0:T(8,128)(2,1)S(1)}, u32[]{:S(2)}, u32[]{:S(2)}) collective-permute-start(bf16[128,2048]{1,0:T(8,128)(2,1)} %refs_0_.8), channel_id=1, source_target_pairs={{0,1},{1,0},{2,3},{3,2},{4,5},{5,4},{6,7},{7,6},{8,9},{9,8},{10,11... | collective-permute-start | bytes 1572872 | tf_op jit(solution)/shard_map/ppermute | solution.py:591
  5.4 2.5 %pack_core.1 = (bf16[3,4,128,256]{3,2,1,0:T(8,128)(2,1)S(1)}, bf16[3,4,64,256]{3,2,1,0:T(8,128)(2,1)}, bf16[3,4,64,256]{3,2,1,0:T(8,128)(2,1)}, f32[8,128]{1,0:T(8,128)}) custom-call(bf16[128,2048]{1,0:T(8,128)(2,1)} %refs_0_.6, bf16[128,2048]{1,0:T(8,128)(2,1)} %refs_0_.9, bf16[128,2048]{1,0:T(8,128)(2,1)} %refs_1_.4, bf16[128,2048]{1,0:T(8,128)(2,1)} %refs_3_.1), custom_call_target="tpu_custom_call" | custom-call | tf_op jit(solution)/shard_map/pack_core/pallas_call | solution.py:179
  8.5 1.4 %collective-permute-done.refs_1_ = bf16[3,4,64,256]{3,2,1,0:T(8,128)(2,1)S(1)} collective-permute-done((bf16[3,4,64,256]{3,2,1,0:T(8,128)(2,1)}, bf16[3,4,64,256]{3,2,1,0:T(8,128)(2,1)S(1)}, u32[]{:S(2)}, u32[]{:S(2)}) %collective-permute-start) | collective-permute-done | bytes 393248 | tf_op jit(solution)/shard_map/ppermute | solution.py:574
  11.2 1.3 %merge_cores.1 = (bf16[4,2,128,256]{3,2,1,0:T(8,128)(2,1)S(1)}, bf16[2,2,128,256]{3,2,1,0:T(8,128)(2,1)S(1)}, bf16[2,2,128,256]{3,2,1,0:T(8,128)(2,1)S(1)}, bf16...) custom-call(bf16[3,4,128,256]{3,2,1,0:T(8,128)(2,1)S(1)} %get-tuple-element.45.refs_0_, ...), custom_call_target="tpu_custom_call" | custom-call | tf_op jit(solution)/shard_map/merge_cores/pallas_call | solution.py:179
  12.5 1.6 %collective-permute-start.2 = (bf16[2,2,128,256]{3,2,1,0:T(8,128)(2,1)S(1)}, bf16[2,2,128,256]{3,2,1,0:T(8,128)(2,1)S(1)}, u32[]{:S(2)}, u32[]{:S(2)}) collective-permute-start(bf16[2,2,128,256]{3,2,1,0:T(8,128)(2,1)S(1)} %get-tuple-element.50), channel_id=1, source_target_pairs={{0,8},{4,12},{8,0},{12,4},{16,24},{20,28},{24,16},{28,20},{1,9},{5... | collective-permute-start | bytes 786440 | tf_op jit(solution)/shard_map/ppermute | solution.py:574
  14.1 1.5 %collective-permute-start.3 = (bf16[2,2,128,256]{3,2,1,0:T(8,128)(2,1)S(1)}, bf16[2,2,128,256]{3,2,1,0:T(8,128)(2,1)S(1)}, u32[]{:S(2)}, u32[]{:S(2)}) collective-permute-start(bf16[2,2,128,256]{3,2,1,0:T(8,128)(2,1)S(1)} %get-tuple-element.51), channel_id=1, source_target_pairs={{0,16},{4,20},{8,24},{12,28},{16,0},{20,4},{24,8},{28,12},{1,17},{... | collective-permute-start | bytes 786440 | tf_op jit(solution)/shard_map/ppermute | solution.py:574
  16.1 2.2 %collective-permute-start.7 = (bf16[128,2048]{1,0:T(8,128)(2,1)S(1)}, bf16[128,2048]{1,0:T(8,128)(2,1)S(1)}, u32[]{:S(2)}, u32[]{:S(2)}) collective-permute-start(bf16[128,2048]{1,0:T(8,128)(2,1)S(1)} %collective-permute-done.6.refs_1_), channel_id=1, source_target_pairs={{0,1},{1,0},{2,3},{3,2},{4,5},{5,4},{6,7},{7,6},{8,9},{9,8},{10,11... | collective-permute-start | bytes 1572872 | tf_op jit(solution)/shard_map/ppermute | solution.py:591
  18.3 6.0 %load_weight.1 = (bf16[4,256,8192]{2,1,0:T(8,128)(2,1)S(1)}, f32[8,128]{1,0:T(8,128)S(1)}) custom-call(bf16[2048,8192]{1,0:T(8,128)(2,1)} %refs_0_.7, f32[8,128]{1,0:T(8,128)S(1)} %get-tuple-element.53.refs_1_), custom_call_target="tpu_custom_call" | custom-call | tf_op jit(solution)/shard_map/load_weight/pallas_call | solution.py:179
  24.4 2.0 %mix.3 = (f32[4,256,256]{2,1,0:T(8,128)S(1)}, f32[8,128]{1,0:T(8,128)S(1)}) custom-call(bf16[128,2048]{1,0:T(8,128)(2,1)S(1)} %copy-done.2, bf16[128,2048]{1,0:T(8,128)(2,1)S(1)} %collective-permute-done.5.refs_1_, bf16[4,256,8192]{2,1,0:T(8,128)(2,1)S(1)} %get-tuple-element.54.refs_2_.refs_4_, f32[8,128]{1,0:T(8,128)S(1)} %get-tuple-element.55.refs_3_), custom_call_target="tpu_custom_call" | custom-call | tf_op jit(solution)/shard_map/mix/pallas_call | solution.py:179
  26.9 0.8 %collective-permute-done.3.refs_3_ = bf16[2,2,128,256]{3,2,1,0:T(8,128)(2,1)S(1)} collective-permute-done((bf16[2,2,128,256]{3,2,1,0:T(8,128)(2,1)S(1)}, bf16[2,2,128,256]{3,2,1,0:T(8,128)(2,1)S(1)}, u32[]{:S(2)}, u32[]{:S(2)}) %collective-permute-start.3) | collective-permute-done | bytes 262176 | tf_op jit(solution)/shard_map/ppermute | solution.py:574
  27.7 1.5 %kernels.1 = (bf16[2,4,512,256]{3,2,1,0:T(8,128)(2,1)S(1)}, f32[8,128]{1,0:T(8,128)S(1)}) custom-call(bf16[512,256]{1,0:T(8,128)(2,1)S(1)} %copy-done.3, bf16[2,2,128,256]{3,2,1,0:T(8,128)(2,1)S(1)} %get-tuple-element.49.refs_1_, bf16[2,2,128,256]{3,2,1,0:T(8,128)(2,1)S(1)} %collective-permute-done.2.refs_2_, ...), custom_call_target="tpu_custom_call" | custom-call | flops 3221225472 | tf_op jit(solution)/shard_map/kernels/pallas_call | solution.py:179
  29.2 0.8 %collective-permute-done.7.refs_0_ = bf16[128,2048]{1,0:T(8,128)(2,1)S(1)} collective-permute-done((bf16[128,2048]{1,0:T(8,128)(2,1)S(1)}, bf16[128,2048]{1,0:T(8,128)(2,1)S(1)}, u32[]{:S(2)}, u32[]{:S(2)}) %collective-permute-start.7) | collective-permute-done | bytes 524320 | tf_op jit(solution)/shard_map/ppermute | solution.py:591
  30.0 2.7 %collective-permute-start.10 = (bf16[128,2048]{1,0:T(8,128)(2,1)S(1)}, bf16[128,2048]{1,0:T(8,128)(2,1)S(1)}, u32[]{:S(2)}, u32[]{:S(2)}) collective-permute-start(bf16[128,2048]{1,0:T(8,128)(2,1)S(1)} %get-tuple-element.59.refs_1_), channel_id=1, source_target_pairs={{0,1},{1,0},{2,3},{3,2},{4,5},{5,4},{6,7},{7,6},{8,9},{9,8},{10,11... | collective-permute-start | bytes 1572872 | tf_op jit(solution)/shard_map/ppermute | solution.py:591
  32.8 2.0 %mix.4 = (f32[4,256,256]{2,1,0:T(8,128)S(1)}, bf16[128,2048]{1,0:T(8,128)(2,1)S(1)}, f32[8,128]{1,0:T(8,128)S(1)}) custom-call(bf16[128,2048]{1,0:T(8,128)(2,1)S(1)} %collective-permute-done.8.refs_0_, bf16[128,2048]{1,0:T(8,128)(2,1)S(1)} %collective-permute-done.13.refs_1_, ...), custom_call_target="tpu_custom_call", output_to_operand_aliasing={{1}: (4, {})} | custom-call | tf_op jit(solution)/shard_map/mix/pallas_call | solution.py:179
  35.4 7.8 %collective-permute-done.10.refs_0_ = bf16[128,2048]{1,0:T(8,128)(2,1)S(1)} collective-permute-done((bf16[128,2048]{1,0:T(8,128)(2,1)S(1)}, bf16[128,2048]{1,0:T(8,128)(2,1)S(1)}, u32[]{:S(2)}, u32[]{:S(2)}) %collective-permute-start.10) | collective-permute-done | bytes 524320 | tf_op jit(solution)/shard_map/ppermute | solution.py:591
  43.3 2.1 %mix.5 = (f32[4,256,256]{2,1,0:T(8,128)S(1)}, f32[8,128]{1,0:T(8,128)}) custom-call(bf16[128,2048]{1,0:T(8,128)(2,1)S(1)} %get-tuple-element.63.refs_0_, bf16[128,2048]{1,0:T(8,128)(2,1)S(1)} %collective-permute-done.6.refs_1_, bf16[128,2048]{1,0:T(8,128)(2,1)S(1)} %collective-permute-done.14.refs_2_, bf16[128,2048]{1,0:T(8,128)(2,1)S(1)} %collective-permute-done.15.refs_3_, ...), custom_call_target="tpu_custom_call" | custom-call | tf_op jit(solution)/shard_map/mix/pallas_call | solution.py:179
  45.4 1.4 %mix_gate.1 = (bf16[2,128,256]{2,1,0:T(8,128)(2,1)S(1)}, bf16[2,128,256]{2,1,0:T(8,128)(2,1)S(1)}, bf16[2,128,256]{2,1,0:T(8,128)(2,1)S(1)}, bf16[2,128,256]{2,1,0:T(8,128)(2,1)S(1)}, f32[8,128]{1,0:T(8,128)}) custom-call(bf16[128,2048]{1,0:T(8,128)(2,1)S(1)} %collective-permute-done.10.refs_0_, bf16[128,2048]{1,0:T(8,128)(2,1)S(1)} %get-tuple-element.59.refs_1_, ...), custom_call_target="tpu_custom_call" | custom-call | tf_op jit(solution)/shard_map/mix_gate/pallas_call | solution.py:179
  46.9 2.5 %collective-permute-start.16 = (bf16[2,128,256]{2,1,0:T(8,128)(2,1)S(1)}, bf16[2,128,256]{2,1,0:T(8,128)(2,1)S(1)}, u32[]{:S(2)}, u32[]{:S(2)}) collective-permute-start(bf16[2,128,256]{2,1,0:T(8,128)(2,1)S(1)} %get-tuple-element.69), channel_id=1, source_target_pairs={{0,24},{4,28},{8,16},{12,20},{16,8},{20,12},{24,0},{28,4},{1,25},{... | collective-permute-start | bytes 393224 | tf_op jit(solution)/shard_map/ppermute | solution.py:574
  50.4 3.6 %collective-permute-done.16.refs_4_ = bf16[2,128,256]{2,1,0:T(8,128)(2,1)S(1)} collective-permute-done((bf16[2,128,256]{2,1,0:T(8,128)(2,1)S(1)}, bf16[2,128,256]{2,1,0:T(8,128)(2,1)S(1)}, u32[]{:S(2)}, u32[]{:S(2)}) %collective-permute-start.16) | collective-permute-done | bytes 131104 | tf_op jit(solution)/shard_map/ppermute | solution.py:574
  54.0 2.5 %collective-permute-done.17.refs_5_ = bf16[2,128,256]{2,1,0:T(8,128)(2,1)S(1)} collective-permute-done((bf16[2,128,256]{2,1,0:T(8,128)(2,1)S(1)}, bf16[2,128,256]{2,1,0:T(8,128)(2,1)S(1)}, u32[]{:S(2)}, u32[]{:S(2)}) %collective-permute-start.17) | collective-permute-done | bytes 131104 | tf_op jit(solution)/shard_map/ppermute | solution.py:574
  56.7 3.4 %correlate.1 = (bf16[2,128,256]{2,1,0:T(8,128)(2,1)S(1)}, bf16[2,128,256]{2,1,0:T(8,128)(2,1)S(1)}, bf16[2,128,256]{2,1,0:T(8,128)(2,1)S(1)}, bf16[2,128,256]{2,...) custom-call(bf16[512,256]{1,0:T(8,128)(2,1)S(1)} %copy-done.3, ...), custom_call_target="tpu_custom_call" | custom-call | tf_op jit(solution)/shard_map/correlate/pallas_call | solution.py:179
  60.0 1.5 %collective-permute-start.20 = (bf16[2,128,256]{2,1,0:T(8,128)(2,1)S(1)}, bf16[2,128,256]{2,1,0:T(8,128)(2,1)S(1)}, u32[]{:S(2)}, u32[]{:S(2)}) collective-permute-start(bf16[2,128,256]{2,1,0:T(8,128)(2,1)S(1)} %get-tuple-element.74), channel_id=1, source_target_pairs={{0,8},{4,12},{8,0},{12,4},{16,24},{20,28},{24,16},{28,20},{1,9},{5... | collective-permute-start | bytes 393224 | tf_op jit(solution)/shard_map/ppermute | solution.py:574
  61.5 0.7 collective-permute-start.21
  62.2 0.8 %collective-permute-start.22 = (bf16[2,128,256]{2,1,0:T(8,128)(2,1)S(1)}, bf16[2,128,256]{2,1,0:T(8,128)(2,1)S(1)}, u32[]{:S(2)}, u32[]{:S(2)}) collective-permute-start(bf16[2,128,256]{2,1,0:T(8,128)(2,1)S(1)} %get-tuple-element.77), channel_id=1, source_target_pairs={{0,12},{4,8},{8,4},{12,0},{16,28},{20,24},{24,20},{28,16},{1,13},{... | collective-permute-start | bytes 393224 | tf_op jit(solution)/shard_map/ppermute | solution.py:574
  63.0 0.8 %collective-permute-start.23 = (bf16[2,128,256]{2,1,0:T(8,128)(2,1)S(1)}, bf16[2,128,256]{2,1,0:T(8,128)(2,1)S(1)}, u32[]{:S(2)}, u32[]{:S(2)}) collective-permute-start(bf16[2,128,256]{2,1,0:T(8,128)(2,1)S(1)} %get-tuple-element.78), channel_id=1, source_target_pairs={{0,20},{4,16},{8,28},{12,24},{16,4},{20,0},{24,12},{28,8},{1,21},{... | collective-permute-start | bytes 393224 | tf_op jit(solution)/shard_map/ppermute | solution.py:574
  63.8 1.6 %collective-permute-start.24 = (bf16[2,128,256]{2,1,0:T(8,128)(2,1)S(1)}, bf16[2,128,256]{2,1,0:T(8,128)(2,1)S(1)}, u32[]{:S(2)}, u32[]{:S(2)}) collective-permute-start(bf16[2,128,256]{2,1,0:T(8,128)(2,1)S(1)} %get-tuple-element.79), channel_id=1, source_target_pairs={{0,24},{4,28},{8,16},{12,20},{16,8},{20,12},{24,0},{28,4},{1,25},{... | collective-permute-start | bytes 393224 | tf_op jit(solution)/shard_map/ppermute | solution.py:574
  65.5 0.9 %collective-permute-done.20.refs_4_ = bf16[2,128,256]{2,1,0:T(8,128)(2,1)S(1)} collective-permute-done((bf16[2,128,256]{2,1,0:T(8,128)(2,1)S(1)}, bf16[2,128,256]{2,1,0:T(8,128)(2,1)S(1)}, u32[]{:S(2)}, u32[]{:S(2)}) %collective-permute-start.20) | collective-permute-done | bytes 131104 | tf_op jit(solution)/shard_map/ppermute | solution.py:574
  66.9 0.9 %collective-permute-done.21.refs_5_ = bf16[2,128,256]{2,1,0:T(8,128)(2,1)S(1)} collective-permute-done((bf16[2,128,256]{2,1,0:T(8,128)(2,1)S(1)}, bf16[2,128,256]{2,1,0:T(8,128)(2,1)S(1)}, u32[]{:S(2)}, u32[]{:S(2)}) %collective-permute-start.21) | collective-permute-done | bytes 131104 | tf_op jit(solution)/shard_map/ppermute | solution.py:574
  67.9 1.8 %finish.2 = (bf16[2,128,2048]{2,1,0:T(8,128)(2,1)S(1)}, bf16[128,2048]{1,0:T(8,128)(2,1)}, bf16[128,2048]{1,0:T(8,128)(2,1)}, f32[128,2048]{1,0:T(8,128)}, f32[8,128]{1,0:T(8,128)}) custom-call(bf16[128,2048]{1,0:T(8,128)(2,1)S(1)} %copy-done, bf16[128,2048]{1,0:T(8,128)(2,1)S(1)} %copy-done.1, bf16[2,128,256]{2,1,0:T(8,128)(2,1)S(1)} %get-tuple-element.72.refs_2_, ...), custom_call_target="tpu_custom_call" | custom-call | tf_op jit(solution)/shard_map/finish/pallas_call | solution.py:179
  69.7 4.2 %collective-permute-done.23.refs_2_ = bf16[2,128,256]{2,1,0:T(8,128)(2,1)S(1)} collective-permute-done((bf16[2,128,256]{2,1,0:T(8,128)(2,1)S(1)}, bf16[2,128,256]{2,1,0:T(8,128)(2,1)S(1)}, u32[]{:S(2)}, u32[]{:S(2)}) %collective-permute-start.23) | collective-permute-done | bytes 131104 | tf_op jit(solution)/shard_map/ppermute | solution.py:574
  73.9 1.0 %collective-permute-done.25.refs_4_ = bf16[2,128,256]{2,1,0:T(8,128)(2,1)S(1)} collective-permute-done((bf16[2,128,256]{2,1,0:T(8,128)(2,1)S(1)}, bf16[2,128,256]{2,1,0:T(8,128)(2,1)S(1)}, u32[]{:S(2)}, u32[]{:S(2)}) %collective-permute-start.25) | collective-permute-done | bytes 131104 | tf_op jit(solution)/shard_map/ppermute | solution.py:574
  74.9 1.7 %finish.3 = (bf16[128,2048]{1,0:T(8,128)(2,1)}, bf16[128,2048]{1,0:T(8,128)(2,1)}, f32[128,2048]{1,0:T(8,128)}, f32[8,128]{1,0:T(8,128)}) custom-call(bf16[2,128,2048]{2,1,0:T(8,128)(2,1)S(1)} %get-tuple-element.76.refs_0_, bf16[2,128,256]{2,1,0:T(8,128)(2,1)S(1)} %collective-permute-done.22.refs_1_, ...), custom_call_target="tpu_custom_call", output_to_operand_aliasing={{0}: (5, {}), {1}: (6, {}), {2}: (7, {})} | custom-call | tf_op jit(solution)/shard_map/finish/pallas_call | solution.py:179
  (44 shorter events, 5.9 us)
Async XLA Ops:
  0.6 14.9 %collective-permute-start.5 = (bf16[128,2048]{1,0:T(8,128)(2,1)}, bf16[128,2048]{1,0:T(8,128)(2,1)S(1)}, u32[]{:S(2)}, u32[]{:S(2)}) collective-permute-start(bf16[128,2048]{1,0:T(8,128)(2,1)} %refs_0_.8), channel_id=1, source_target_pairs={{0,4},{4,0},{8,12},{12,8},{16,20},{20,16},{24,28},{28,24},{1,5},{5... | collective-permute-start | bytes 1572872 | tf_op jit(solution)/shard_map/ppermute | solution.py:574
  1.1 14.9 %collective-permute-start.6 = (bf16[128,2048]{1,0:T(8,128)(2,1)}, bf16[128,2048]{1,0:T(8,128)(2,1)S(1)}, u32[]{:S(2)}, u32[]{:S(2)}) collective-permute-start(bf16[128,2048]{1,0:T(8,128)(2,1)} %refs_0_.8), channel_id=1, source_target_pairs={{1,2},{2,1},{0,4},{3,7},{5,6},{6,5},{4,0},{7,3},{9,10},{10,9},{8,1... | collective-permute-start | bytes 1572872 | tf_op jit(solution)/shard_map/ppermute | solution.py:594
  1.2 17.1 %collective-permute-start.8 = (bf16[128,2048]{1,0:T(8,128)(2,1)}, bf16[128,2048]{1,0:T(8,128)(2,1)S(1)}, u32[]{:S(2)}, u32[]{:S(2)}) collective-permute-start(bf16[128,2048]{1,0:T(8,128)(2,1)} %refs_0_.8), channel_id=1, source_target_pairs={{0,1},{1,0},{2,3},{3,2},{4,5},{5,4},{6,7},{7,6},{8,9},{9,8},{10,11... | collective-permute-start | bytes 1572872 | tf_op jit(solution)/shard_map/ppermute | solution.py:591
  7.9 2.0 %collective-permute-start = (bf16[3,4,64,256]{3,2,1,0:T(8,128)(2,1)}, bf16[3,4,64,256]{3,2,1,0:T(8,128)(2,1)S(1)}, u32[]{:S(2)}, u32[]{:S(2)}) collective-permute-start(bf16[3,4,64,256]{3,2,1,0:T(8,128)(2,1)} %get-tuple-element.46), channel_id=1, source_target_pairs={{0,4},{4,0},{8,12},{12,8},{16,20},{20,16},{24,28},{28,24},{1,5},{5... | collective-permute-start | bytes 1179656 | tf_op jit(solution)/shard_map/ppermute | solution.py:574
  8.0 2.5 %collective-permute-start.1 = (bf16[3,4,64,256]{3,2,1,0:T(8,128)(2,1)}, bf16[3,4,64,256]{3,2,1,0:T(8,128)(2,1)S(1)}, u32[]{:S(2)}, u32[]{:S(2)}) collective-permute-start(bf16[3,4,64,256]{3,2,1,0:T(8,128)(2,1)} %get-tuple-element.47), channel_id=1, source_target_pairs={{0,4},{4,0},{8,12},{12,8},{16,20},{20,16},{24,28},{28,24},{1,5},{5... | collective-permute-start | bytes 1179656 | tf_op jit(solution)/shard_map/ppermute | solution.py:574
  10.5 0.7 copy-start.5
  12.5 13.9 %collective-permute-start.2 = (bf16[2,2,128,256]{3,2,1,0:T(8,128)(2,1)S(1)}, bf16[2,2,128,256]{3,2,1,0:T(8,128)(2,1)S(1)}, u32[]{:S(2)}, u32[]{:S(2)}) collective-permute-start(bf16[2,2,128,256]{3,2,1,0:T(8,128)(2,1)S(1)} %get-tuple-element.50), channel_id=1, source_target_pairs={{0,8},{4,12},{8,0},{12,4},{16,24},{20,28},{24,16},{28,20},{1,9},{5... | collective-permute-start | bytes 786440 | tf_op jit(solution)/shard_map/ppermute | solution.py:574
  14.1 13.7 %collective-permute-start.3 = (bf16[2,2,128,256]{3,2,1,0:T(8,128)(2,1)S(1)}, bf16[2,2,128,256]{3,2,1,0:T(8,128)(2,1)S(1)}, u32[]{:S(2)}, u32[]{:S(2)}) collective-permute-start(bf16[2,2,128,256]{3,2,1,0:T(8,128)(2,1)S(1)} %get-tuple-element.51), channel_id=1, source_target_pairs={{0,16},{4,20},{8,24},{12,28},{16,0},{20,4},{24,8},{28,12},{1,17},{... | collective-permute-start | bytes 786440 | tf_op jit(solution)/shard_map/ppermute | solution.py:574
  15.6 12.2 %collective-permute-start.4 = (bf16[2,2,128,256]{3,2,1,0:T(8,128)(2,1)S(1)}, bf16[2,2,128,256]{3,2,1,0:T(8,128)(2,1)S(1)}, u32[]{:S(2)}, u32[]{:S(2)}) collective-permute-start(bf16[2,2,128,256]{3,2,1,0:T(8,128)(2,1)S(1)} %get-tuple-element.52), channel_id=1, source_target_pairs={{0,24},{4,28},{8,16},{12,20},{16,8},{20,12},{24,0},{28,4},{1,25},{... | collective-permute-start | bytes 786440 | tf_op jit(solution)/shard_map/ppermute | solution.py:574
  16.1 14.0 %collective-permute-start.7 = (bf16[128,2048]{1,0:T(8,128)(2,1)S(1)}, bf16[128,2048]{1,0:T(8,128)(2,1)S(1)}, u32[]{:S(2)}, u32[]{:S(2)}) collective-permute-start(bf16[128,2048]{1,0:T(8,128)(2,1)S(1)} %collective-permute-done.6.refs_1_), channel_id=1, source_target_pairs={{0,1},{1,0},{2,3},{3,2},{4,5},{5,4},{6,7},{7,6},{8,9},{9,8},{10,11... | collective-permute-start | bytes 1572872 | tf_op jit(solution)/shard_map/ppermute | solution.py:591
  18.3 11.7 %collective-permute-start.9 = (bf16[128,2048]{1,0:T(8,128)(2,1)S(1)}, bf16[128,2048]{1,0:T(8,128)(2,1)S(1)}, u32[]{:S(2)}, u32[]{:S(2)}) collective-permute-start(bf16[128,2048]{1,0:T(8,128)(2,1)S(1)} %collective-permute-done.8.refs_0_), channel_id=1, source_target_pairs={{1,2},{2,1},{0,4},{3,7},{5,6},{6,5},{4,0},{7,3},{9,10},{10,9},{8,1... | collective-permute-start | bytes 1572872 | tf_op jit(solution)/shard_map/ppermute | solution.py:594
  18.3 6.1 %copy-start.2 = (bf16[128,2048]{1,0:T(8,128)(2,1)S(1)}, bf16[128,2048]{1,0:T(8,128)(2,1)}, u32[]{:S(2)}) copy-start(bf16[128,2048]{1,0:T(8,128)(2,1)} %refs_0_.8) | copy-start | bytes 1572868
  24.3 3.4 %copy-start.3 = (bf16[512,256]{1,0:T(8,128)(2,1)S(1)}, bf16[512,256]{1,0:T(8,128)(2,1)}, u32[]{:S(2)}) copy-start(bf16[512,256]{1,0:T(8,128)(2,1)} %constant.4.clone.refs_0_) | copy-start | bytes 786436
  26.4 6.4 %collective-permute-start.13 = (bf16[128,2048]{1,0:T(8,128)(2,1)S(1)}, bf16[128,2048]{1,0:T(8,128)(2,1)S(1)}, u32[]{:S(2)}, u32[]{:S(2)}) collective-permute-start(bf16[128,2048]{1,0:T(8,128)(2,1)S(1)} %collective-permute-done.8.refs_0_), channel_id=1, source_target_pairs={{0,4},{4,0},{8,12},{12,8},{16,20},{20,16},{24,28},{28,24},{1,5},{5... | collective-permute-start | bytes 1572872 | tf_op jit(solution)/shard_map/ppermute | solution.py:574
  30.0 13.2 %collective-permute-start.10 = (bf16[128,2048]{1,0:T(8,128)(2,1)S(1)}, bf16[128,2048]{1,0:T(8,128)(2,1)S(1)}, u32[]{:S(2)}, u32[]{:S(2)}) collective-permute-start(bf16[128,2048]{1,0:T(8,128)(2,1)S(1)} %get-tuple-element.59.refs_1_), channel_id=1, source_target_pairs={{0,1},{1,0},{2,3},{3,2},{4,5},{5,4},{6,7},{7,6},{8,9},{9,8},{10,11... | collective-permute-start | bytes 1572872 | tf_op jit(solution)/shard_map/ppermute | solution.py:591
  32.7 10.5 %collective-permute-start.15 = (bf16[128,2048]{1,0:T(8,128)(2,1)S(1)}, bf16[128,2048]{1,0:T(8,128)(2,1)S(1)}, u32[]{:S(2)}, u32[]{:S(2)}) collective-permute-start(bf16[128,2048]{1,0:T(8,128)(2,1)S(1)} %collective-permute-done.6.refs_1_), channel_id=1, source_target_pairs={{0,4},{4,0},{8,12},{12,8},{16,20},{20,16},{24,28},{28,24},{1,5},{5... | collective-permute-start | bytes 1572872 | tf_op jit(solution)/shard_map/ppermute | solution.py:574
  34.7 8.5 %collective-permute-start.14 = (bf16[128,2048]{1,0:T(8,128)(2,1)S(1)}, bf16[128,2048]{1,0:T(8,128)(2,1)S(1)}, u32[]{:S(2)}, u32[]{:S(2)}) collective-permute-start(bf16[128,2048]{1,0:T(8,128)(2,1)S(1)} %get-tuple-element.63.refs_0_), channel_id=1, source_target_pairs={{0,4},{4,0},{8,12},{12,8},{16,20},{20,16},{24,28},{28,24},{1,5},{5... | collective-permute-start | bytes 1572872 | tf_op jit(solution)/shard_map/ppermute | solution.py:574
  35.3 10.1 %collective-permute-start.12 = (bf16[128,2048]{1,0:T(8,128)(2,1)S(1)}, bf16[128,2048]{1,0:T(8,128)(2,1)S(1)}, u32[]{:S(2)}, u32[]{:S(2)}) collective-permute-start(bf16[128,2048]{1,0:T(8,128)(2,1)S(1)} %get-tuple-element.59.refs_1_), channel_id=1, source_target_pairs={{0,4},{4,0},{8,12},{12,8},{16,20},{20,16},{24,28},{28,24},{1,5},{5... | collective-permute-start | bytes 1572872 | tf_op jit(solution)/shard_map/ppermute | solution.py:574
  43.2 2.2 %collective-permute-start.11 = (bf16[128,2048]{1,0:T(8,128)(2,1)S(1)}, bf16[128,2048]{1,0:T(8,128)(2,1)S(1)}, u32[]{:S(2)}, u32[]{:S(2)}) collective-permute-start(bf16[128,2048]{1,0:T(8,128)(2,1)S(1)} %collective-permute-done.10.refs_0_), channel_id=1, source_target_pairs={{0,4},{4,0},{8,12},{12,8},{16,20},{20,16},{24,28},{28,24},{1,5},{5... | collective-permute-start | bytes 1572872 | tf_op jit(solution)/shard_map/ppermute | solution.py:574
  43.3 13.4 %copy-start.4 = (bf16[256,512]{1,0:T(8,128)(2,1)S(1)}, bf16[256,512]{1,0:T(8,128)(2,1)}, u32[]{:S(2)}) copy-start(bf16[256,512]{1,0:T(8,128)(2,1)} %constant.5.clone.refs_1_) | copy-start | bytes 786436
  45.4 22.5 %copy-start = (bf16[128,2048]{1,0:T(8,128)(2,1)S(1)}, bf16[128,2048]{1,0:T(8,128)(2,1)}, u32[]{:S(2)}) copy-start(bf16[128,2048]{1,0:T(8,128)(2,1)} %refs_0_.9) | copy-start | bytes 1572868
  45.4 22.4 %copy-start.1 = (bf16[128,2048]{1,0:T(8,128)(2,1)S(1)}, bf16[128,2048]{1,0:T(8,128)(2,1)}, u32[]{:S(2)}) copy-start(bf16[128,2048]{1,0:T(8,128)(2,1)} %refs_1_.4) | copy-start | bytes 1572868
  46.9 7.1 %collective-permute-start.16 = (bf16[2,128,256]{2,1,0:T(8,128)(2,1)S(1)}, bf16[2,128,256]{2,1,0:T(8,128)(2,1)S(1)}, u32[]{:S(2)}, u32[]{:S(2)}) collective-permute-start(bf16[2,128,256]{2,1,0:T(8,128)(2,1)S(1)} %get-tuple-element.69), channel_id=1, source_target_pairs={{0,24},{4,28},{8,16},{12,20},{16,8},{20,12},{24,0},{28,4},{1,25},{... | collective-permute-start | bytes 393224 | tf_op jit(solution)/shard_map/ppermute | solution.py:574
  49.4 7.2 %collective-permute-start.17 = (bf16[2,128,256]{2,1,0:T(8,128)(2,1)S(1)}, bf16[2,128,256]{2,1,0:T(8,128)(2,1)S(1)}, u32[]{:S(2)}, u32[]{:S(2)}) collective-permute-start(bf16[2,128,256]{2,1,0:T(8,128)(2,1)S(1)} %get-tuple-element.70), channel_id=1, source_target_pairs={{0,16},{4,20},{8,24},{12,28},{16,0},{20,4},{24,8},{28,12},{1,17},{... | collective-permute-start | bytes 393224 | tf_op jit(solution)/shard_map/ppermute | solution.py:574
  49.9 6.8 %collective-permute-start.18 = (bf16[2,128,256]{2,1,0:T(8,128)(2,1)S(1)}, bf16[2,128,256]{2,1,0:T(8,128)(2,1)S(1)}, u32[]{:S(2)}, u32[]{:S(2)}) collective-permute-start(bf16[2,128,256]{2,1,0:T(8,128)(2,1)S(1)} %get-tuple-element.71), channel_id=1, source_target_pairs={{0,8},{4,12},{8,0},{12,4},{16,24},{20,28},{24,16},{28,20},{1,9},{5... | collective-permute-start | bytes 393224 | tf_op jit(solution)/shard_map/ppermute | solution.py:574
  60.0 3.8 %collective-permute-start.19 = (bf16[2,128,256]{2,1,0:T(8,128)(2,1)S(1)}, bf16[2,128,256]{2,1,0:T(8,128)(2,1)S(1)}, u32[]{:S(2)}, u32[]{:S(2)}) collective-permute-start(bf16[2,128,256]{2,1,0:T(8,128)(2,1)S(1)} %get-tuple-element.73), channel_id=1, source_target_pairs={{0,4},{4,0},{8,12},{12,8},{16,20},{20,16},{24,28},{28,24},{1,5},{5... | collective-permute-start | bytes 393224 | tf_op jit(solution)/shard_map/ppermute | solution.py:574
  60.0 6.3 %collective-permute-start.20 = (bf16[2,128,256]{2,1,0:T(8,128)(2,1)S(1)}, bf16[2,128,256]{2,1,0:T(8,128)(2,1)S(1)}, u32[]{:S(2)}, u32[]{:S(2)}) collective-permute-start(bf16[2,128,256]{2,1,0:T(8,128)(2,1)S(1)} %get-tuple-element.74), channel_id=1, source_target_pairs={{0,8},{4,12},{8,0},{12,4},{16,24},{20,28},{24,16},{28,20},{1,9},{5... | collective-permute-start | bytes 393224 | tf_op jit(solution)/shard_map/ppermute | solution.py:574
  61.5 6.3 %collective-permute-start.21 = (bf16[2,128,256]{2,1,0:T(8,128)(2,1)S(1)}, bf16[2,128,256]{2,1,0:T(8,128)(2,1)S(1)}, u32[]{:S(2)}, u32[]{:S(2)}) collective-permute-start(bf16[2,128,256]{2,1,0:T(8,128)(2,1)S(1)} %get-tuple-element.75), channel_id=1, source_target_pairs={{0,16},{4,20},{8,24},{12,28},{16,0},{20,4},{24,8},{28,12},{1,17},{... | collective-permute-start | bytes 393224 | tf_op jit(solution)/shard_map/ppermute | solution.py:574
  62.2 7.4 %collective-permute-start.22 = (bf16[2,128,256]{2,1,0:T(8,128)(2,1)S(1)}, bf16[2,128,256]{2,1,0:T(8,128)(2,1)S(1)}, u32[]{:S(2)}, u32[]{:S(2)}) collective-permute-start(bf16[2,128,256]{2,1,0:T(8,128)(2,1)S(1)} %get-tuple-element.77), channel_id=1, source_target_pairs={{0,12},{4,8},{8,4},{12,0},{16,28},{20,24},{24,20},{28,16},{1,13},{... | collective-permute-start | bytes 393224 | tf_op jit(solution)/shard_map/ppermute | solution.py:574
  63.0 10.8 %collective-permute-start.23 = (bf16[2,128,256]{2,1,0:T(8,128)(2,1)S(1)}, bf16[2,128,256]{2,1,0:T(8,128)(2,1)S(1)}, u32[]{:S(2)}, u32[]{:S(2)}) collective-permute-start(bf16[2,128,256]{2,1,0:T(8,128)(2,1)S(1)} %get-tuple-element.78), channel_id=1, source_target_pairs={{0,20},{4,16},{8,28},{12,24},{16,4},{20,0},{24,12},{28,8},{1,21},{... | collective-permute-start | bytes 393224 | tf_op jit(solution)/shard_map/ppermute | solution.py:574
  63.8 10.0 %collective-permute-start.24 = (bf16[2,128,256]{2,1,0:T(8,128)(2,1)S(1)}, bf16[2,128,256]{2,1,0:T(8,128)(2,1)S(1)}, u32[]{:S(2)}, u32[]{:S(2)}) collective-permute-start(bf16[2,128,256]{2,1,0:T(8,128)(2,1)S(1)} %get-tuple-element.79), channel_id=1, source_target_pairs={{0,24},{4,28},{8,16},{12,20},{16,8},{20,12},{24,0},{28,4},{1,25},{... | collective-permute-start | bytes 393224 | tf_op jit(solution)/shard_map/ppermute | solution.py:574
  66.3 8.6 %collective-permute-start.25 = (bf16[2,128,256]{2,1,0:T(8,128)(2,1)S(1)}, bf16[2,128,256]{2,1,0:T(8,128)(2,1)S(1)}, u32[]{:S(2)}, u32[]{:S(2)}) collective-permute-start(bf16[2,128,256]{2,1,0:T(8,128)(2,1)S(1)} %get-tuple-element.80), channel_id=1, source_target_pairs={{0,28},{4,24},{8,20},{12,16},{16,12},{20,8},{24,4},{28,0},{1,29},{... | collective-permute-start | bytes 393224 | tf_op jit(solution)/shard_map/ppermute | solution.py:574

commit v6 on v5

--- a/solution.py
+++ b/solution.py
@@ -602,11 +602,11 @@
     taps_input = [swap(x, 2 * k, n) for k, x in enumerate(taps_input)]
     outer_1, inner_1 = send_outer(inner_0), send_inner(outer_0)
     held, loaded = load(out_weight, chips, after=[merged])
-    total, first = mix(0, [[grad_out], [others]], held, None, after=[loaded])
-    kern, tapped = tap_kernels(forward, taps_input, after=[first])
+    kern, tapped = tap_kernels(forward, taps_input, after=[loaded])
     outer_1, inner_1, gone = hold([outer_1, inner_1], after=[tapped])
     outer_2 = send_outer(inner_1)
-    total, outer_1, second = mix(1, [[outer_0], [other(outer_0)]], held, total, carry=[outer_1], after=[gone])
+    total, first = mix(0, [[grad_out], [others]], held, None, after=[gone])
+    total, outer_1, second = mix(1, [[outer_0], [other(outer_0)]], held, total, carry=[outer_1], after=[first])
     blocks = [[outer_1, inner_0], [other(outer_1), other(inner_0)]]
     total, _ = mix(2, blocks, held, total, after=[second])
     gated = mix_gate([[outer_2, inner_1], [other(outer_2), other(inner_1)]], held, total, gates)[:chips]

time: 76.9 us -> 76.3 us (level)
  starting transfers between devices: 24.6 us -> 22.8 us
  waiting for transfers between devices: 24.7 us -> 26 us
    ppermute x21, waiting for transfers between devices: 16.1 us -> 18.4 us  [swap(): return lax.ppermute(x, 'seq', [(i, i ^ k) for i in range(n)]) if k else x]
    ppermute x3, starting transfers between devices: 9.09 us -> 7.95 us  [send_outer(): return lax.ppermute(x, 'ch', outer)]
    ppermute x3, waiting for transfers between devices: 8.65 us -> 7.56 us  [send_outer(): return lax.ppermute(x, 'ch', outer)]
    ppermute x21, starting transfers between devices: 15.4 us -> 14.4 us  [swap(): return lax.ppermute(x, 'seq', [(i, i ^ k) for i in range(n)]) if k else x]
  transfers between devices with their start and end apart: 26 -> 26, of which waited for: 12 -> 11; matrix products, arithmetic and copies ran while one was open for 0% -> 0% of each run, Pallas kernels for 25% -> 25%
where the time goes in v6:
time: 76.3 us; the launch traced here: 76.2 us
  waiting for transfers between devices  26 us (34%)
  Pallas kernels  25.8 us (34%)
  starting transfers between devices  22.8 us (30%)
  between operations  0.85 us (1%)
    pallas_call x12, Pallas kernels, call(): pl.pallas_call(body, input_output_aliases={count + i: results + i for i i...  25.8 us
    ppermute x21, waiting for transfers between devices, swap(): return lax.ppermute(x, 'seq', [(i, i ^ k) for i in range(n)]) if k else x  18.4 us
    ppermute x21, starting transfers between devices, swap(): return lax.ppermute(x, 'seq', [(i, i ^ k) for i in range(n)]) if k else x  14.4 us
    ppermute x3, starting transfers between devices, send_outer(): return lax.ppermute(x, 'ch', outer)  7.95 us
    ppermute x3, waiting for transfers between devices, send_outer(): return lax.ppermute(x, 'ch', outer)  7.56 us
  transfers between devices with their start and end apart: 26, of which 11 were waited for; matrix products, arithmetic and copies ran while one was open for 0% of the time, Pallas kernels for 25%

profile of v6, /device:TPU:0, one launch (start us, length us, event | category | flops | bytes accessed | tf_op | source)
XLA Modules:
  0.0 76.2 jit_solution(15192435052586688)
XLA Ops:
  1.1 4.1 %collective-permute-start.7 = (bf16[128,2048]{1,0:T(8,128)(2,1)}, bf16[128,2048]{1,0:T(8,128)(2,1)S(1)}, u32[]{:S(2)}, u32[]{:S(2)}) collective-permute-start(bf16[128,2048]{1,0:T(8,128)(2,1)} %refs_0_.8), channel_id=1, source_target_pairs={{0,1},{1,0},{2,3},{3,2},{4,5},{5,4},{6,7},{7,6},{8,9},{9,8},{10,11... | collective-permute-start | bytes 1572872 | tf_op jit(solution)/shard_map/ppermute | solution.py:591
  5.3 2.5 %pack_core.1 = (bf16[3,4,128,256]{3,2,1,0:T(8,128)(2,1)S(1)}, bf16[3,4,64,256]{3,2,1,0:T(8,128)(2,1)}, bf16[3,4,64,256]{3,2,1,0:T(8,128)(2,1)}, f32[8,128]{1,0:T(8,128)}) custom-call(bf16[128,2048]{1,0:T(8,128)(2,1)} %refs_0_.6, bf16[128,2048]{1,0:T(8,128)(2,1)} %refs_0_.9, bf16[128,2048]{1,0:T(8,128)(2,1)} %refs_1_.4, bf16[128,2048]{1,0:T(8,128)(2,1)} %refs_3_.1), custom_call_target="tpu_custom_call" | custom-call | tf_op jit(solution)/shard_map/pack_core/pallas_call | solution.py:179
  8.4 1.4 %collective-permute-done.refs_1_ = bf16[3,4,64,256]{3,2,1,0:T(8,128)(2,1)S(1)} collective-permute-done((bf16[3,4,64,256]{3,2,1,0:T(8,128)(2,1)}, bf16[3,4,64,256]{3,2,1,0:T(8,128)(2,1)S(1)}, u32[]{:S(2)}, u32[]{:S(2)}) %collective-permute-start) | collective-permute-done | bytes 393248 | tf_op jit(solution)/shard_map/ppermute | solution.py:574
  9.9 0.6 collective-permute-done.1.refs_2_
  10.4 0.7 copy-done.5
  11.1 1.3 %merge_cores.1 = (bf16[4,2,128,256]{3,2,1,0:T(8,128)(2,1)S(1)}, bf16[2,2,128,256]{3,2,1,0:T(8,128)(2,1)S(1)}, bf16[2,2,128,256]{3,2,1,0:T(8,128)(2,1)S(1)}, bf16...) custom-call(bf16[3,4,128,256]{3,2,1,0:T(8,128)(2,1)S(1)} %get-tuple-element.45.refs_0_, ...), custom_call_target="tpu_custom_call" | custom-call | tf_op jit(solution)/shard_map/merge_cores/pallas_call | solution.py:179
  12.4 1.6 %collective-permute-start.2 = (bf16[2,2,128,256]{3,2,1,0:T(8,128)(2,1)S(1)}, bf16[2,2,128,256]{3,2,1,0:T(8,128)(2,1)S(1)}, u32[]{:S(2)}, u32[]{:S(2)}) collective-permute-start(bf16[2,2,128,256]{3,2,1,0:T(8,128)(2,1)S(1)} %get-tuple-element.50), channel_id=1, source_target_pairs={{0,8},{4,12},{8,0},{12,4},{16,24},{20,28},{24,16},{28,20},{1,9},{5... | collective-permute-start | bytes 786440 | tf_op jit(solution)/shard_map/ppermute | solution.py:574
  14.0 1.5 %collective-permute-start.3 = (bf16[2,2,128,256]{3,2,1,0:T(8,128)(2,1)S(1)}, bf16[2,2,128,256]{3,2,1,0:T(8,128)(2,1)S(1)}, u32[]{:S(2)}, u32[]{:S(2)}) collective-permute-start(bf16[2,2,128,256]{3,2,1,0:T(8,128)(2,1)S(1)} %get-tuple-element.51), channel_id=1, source_target_pairs={{0,16},{4,20},{8,24},{12,28},{16,0},{20,4},{24,8},{28,12},{1,17},{... | collective-permute-start | bytes 786440 | tf_op jit(solution)/shard_map/ppermute | solution.py:574
  16.0 1.6 %collective-permute-start.6 = (bf16[128,2048]{1,0:T(8,128)(2,1)S(1)}, bf16[128,2048]{1,0:T(8,128)(2,1)S(1)}, u32[]{:S(2)}, u32[]{:S(2)}) collective-permute-start(bf16[128,2048]{1,0:T(8,128)(2,1)S(1)} %collective-permute-done.5.refs_1_), channel_id=1, source_target_pairs={{0,1},{1,0},{2,3},{3,2},{4,5},{5,4},{6,7},{7,6},{8,9},{9,8},{10,11... | collective-permute-start | bytes 1572872 | tf_op jit(solution)/shard_map/ppermute | solution.py:591
  17.6 6.0 %load_weight.1 = (bf16[4,256,8192]{2,1,0:T(8,128)(2,1)S(1)}, f32[8,128]{1,0:T(8,128)S(1)}) custom-call(bf16[2048,8192]{1,0:T(8,128)(2,1)} %refs_0_.7, f32[8,128]{1,0:T(8,128)S(1)} %get-tuple-element.53.refs_1_), custom_call_target="tpu_custom_call" | custom-call | tf_op jit(solution)/shard_map/load_weight/pallas_call | solution.py:179
  24.2 3.4 %collective-permute-done.3.refs_3_ = bf16[2,2,128,256]{3,2,1,0:T(8,128)(2,1)S(1)} collective-permute-done((bf16[2,2,128,256]{3,2,1,0:T(8,128)(2,1)S(1)}, bf16[2,2,128,256]{3,2,1,0:T(8,128)(2,1)S(1)}, u32[]{:S(2)}, u32[]{:S(2)}) %collective-permute-start.3) | collective-permute-done | bytes 262176 | tf_op jit(solution)/shard_map/ppermute | solution.py:574
  27.7 1.5 %kernels.1 = (bf16[2,4,512,256]{3,2,1,0:T(8,128)(2,1)S(1)}, f32[8,128]{1,0:T(8,128)S(1)}) custom-call(bf16[512,256]{1,0:T(8,128)(2,1)S(1)} %copy-done.3, bf16[2,2,128,256]{3,2,1,0:T(8,128)(2,1)S(1)} %get-tuple-element.49.refs_1_, bf16[2,2,128,256]{3,2,1,0:T(8,128)(2,1)S(1)} %collective-permute-done.2.refs_2_, ...), custom_call_target="tpu_custom_call" | custom-call | flops 3221225472 | tf_op jit(solution)/shard_map/kernels/pallas_call | solution.py:179
  29.2 2.2 %collective-permute-start.9 = (bf16[128,2048]{1,0:T(8,128)(2,1)S(1)}, bf16[128,2048]{1,0:T(8,128)(2,1)S(1)}, u32[]{:S(2)}, u32[]{:S(2)}) collective-permute-start(bf16[128,2048]{1,0:T(8,128)(2,1)S(1)} %get-tuple-element.57.refs_1_), channel_id=1, source_target_pairs={{0,1},{1,0},{2,3},{3,2},{4,5},{5,4},{6,7},{7,6},{8,9},{9,8},{10,11... | collective-permute-start | bytes 1572872 | tf_op jit(solution)/shard_map/ppermute | solution.py:591
  31.4 2.0 %mix.3 = (f32[4,256,256]{2,1,0:T(8,128)S(1)}, f32[8,128]{1,0:T(8,128)S(1)}) custom-call(bf16[128,2048]{1,0:T(8,128)(2,1)S(1)} %copy-done.2, bf16[128,2048]{1,0:T(8,128)(2,1)S(1)} %collective-permute-done.13.refs_1_, bf16[4,256,8192]{2,1,0:T(8,128)(2,1)S(1)} %get-tuple-element.58.refs_2_.refs_4_, f32[8,128]{1,0:T(8,128)S(1)} %get-tuple-element.59.refs_3_), custom_call_target="tpu_custom_call" | custom-call | tf_op jit(solution)/shard_map/mix/pallas_call | solution.py:179
  33.4 2.0 %mix.4 = (f32[4,256,256]{2,1,0:T(8,128)S(1)}, bf16[128,2048]{1,0:T(8,128)(2,1)S(1)}, f32[8,128]{1,0:T(8,128)S(1)}) custom-call(bf16[128,2048]{1,0:T(8,128)(2,1)S(1)} %collective-permute-done.7.refs_0_, bf16[128,2048]{1,0:T(8,128)(2,1)S(1)} %collective-permute-done.12.refs_1_, ...), custom_call_target="tpu_custom_call", output_to_operand_aliasing={{1}: (4, {})} | custom-call | tf_op jit(solution)/shard_map/mix/pallas_call | solution.py:179
  35.4 0.6 collective-permute-start.14
  36.0 7.6 %collective-permute-done.9.refs_0_ = bf16[128,2048]{1,0:T(8,128)(2,1)S(1)} collective-permute-done((bf16[128,2048]{1,0:T(8,128)(2,1)S(1)}, bf16[128,2048]{1,0:T(8,128)(2,1)S(1)}, u32[]{:S(2)}, u32[]{:S(2)}) %collective-permute-start.9) | collective-permute-done | bytes 524320 | tf_op jit(solution)/shard_map/ppermute | solution.py:591
  43.6 2.1 %mix.5 = (f32[4,256,256]{2,1,0:T(8,128)S(1)}, f32[8,128]{1,0:T(8,128)}) custom-call(bf16[128,2048]{1,0:T(8,128)(2,1)S(1)} %get-tuple-element.63.refs_0_, bf16[128,2048]{1,0:T(8,128)(2,1)S(1)} %collective-permute-done.5.refs_1_, bf16[128,2048]{1,0:T(8,128)(2,1)S(1)} %collective-permute-done.14.refs_2_, bf16[128,2048]{1,0:T(8,128)(2,1)S(1)} %collective-permute-done.15.refs_3_, ...), custom_call_target="tpu_custom_call" | custom-call | tf_op jit(solution)/shard_map/mix/pallas_call | solution.py:179
  45.8 1.4 %mix_gate.1 = (bf16[2,128,256]{2,1,0:T(8,128)(2,1)S(1)}, bf16[2,128,256]{2,1,0:T(8,128)(2,1)S(1)}, bf16[2,128,256]{2,1,0:T(8,128)(2,1)S(1)}, bf16[2,128,256]{2,1,0:T(8,128)(2,1)S(1)}, f32[8,128]{1,0:T(8,128)}) custom-call(bf16[128,2048]{1,0:T(8,128)(2,1)S(1)} %collective-permute-done.9.refs_0_, bf16[128,2048]{1,0:T(8,128)(2,1)S(1)} %get-tuple-element.57.refs_1_, ...), custom_call_target="tpu_custom_call" | custom-call | tf_op jit(solution)/shard_map/mix_gate/pallas_call | solution.py:179
  47.2 1.6 %collective-permute-start.16 = (bf16[2,128,256]{2,1,0:T(8,128)(2,1)S(1)}, bf16[2,128,256]{2,1,0:T(8,128)(2,1)S(1)}, u32[]{:S(2)}, u32[]{:S(2)}) collective-permute-start(bf16[2,128,256]{2,1,0:T(8,128)(2,1)S(1)} %get-tuple-element.69), channel_id=1, source_target_pairs={{0,24},{4,28},{8,16},{12,20},{16,8},{20,12},{24,0},{28,4},{1,25},{... | collective-permute-start | bytes 393224 | tf_op jit(solution)/shard_map/ppermute | solution.py:574
  48.9 1.9 %collective-permute-start.18 = (bf16[2,128,256]{2,1,0:T(8,128)(2,1)S(1)}, bf16[2,128,256]{2,1,0:T(8,128)(2,1)S(1)}, u32[]{:S(2)}, u32[]{:S(2)}) collective-permute-start(bf16[2,128,256]{2,1,0:T(8,128)(2,1)S(1)} %get-tuple-element.71), channel_id=1, source_target_pairs={{0,8},{4,12},{8,0},{12,4},{16,24},{20,28},{24,16},{28,20},{1,9},{5... | collective-permute-start | bytes 393224 | tf_op jit(solution)/shard_map/ppermute | solution.py:574
  50.8 3.7 %collective-permute-done.16.refs_4_ = bf16[2,128,256]{2,1,0:T(8,128)(2,1)S(1)} collective-permute-done((bf16[2,128,256]{2,1,0:T(8,128)(2,1)S(1)}, bf16[2,128,256]{2,1,0:T(8,128)(2,1)S(1)}, u32[]{:S(2)}, u32[]{:S(2)}) %collective-permute-start.16) | collective-permute-done | bytes 131104 | tf_op jit(solution)/shard_map/ppermute | solution.py:574
  54.5 2.4 %collective-permute-done.17.refs_5_ = bf16[2,128,256]{2,1,0:T(8,128)(2,1)S(1)} collective-permute-done((bf16[2,128,256]{2,1,0:T(8,128)(2,1)S(1)}, bf16[2,128,256]{2,1,0:T(8,128)(2,1)S(1)}, u32[]{:S(2)}, u32[]{:S(2)}) %collective-permute-start.17) | collective-permute-done | bytes 131104 | tf_op jit(solution)/shard_map/ppermute | solution.py:574
  57.0 3.3 %correlate.1 = (bf16[2,128,256]{2,1,0:T(8,128)(2,1)S(1)}, bf16[2,128,256]{2,1,0:T(8,128)(2,1)S(1)}, bf16[2,128,256]{2,1,0:T(8,128)(2,1)S(1)}, bf16[2,128,256]{2,...) custom-call(bf16[512,256]{1,0:T(8,128)(2,1)S(1)} %copy-done.3, ...), custom_call_target="tpu_custom_call" | custom-call | tf_op jit(solution)/shard_map/correlate/pallas_call | solution.py:179
  60.9 1.5 %collective-permute-start.21 = (bf16[2,128,256]{2,1,0:T(8,128)(2,1)S(1)}, bf16[2,128,256]{2,1,0:T(8,128)(2,1)S(1)}, u32[]{:S(2)}, u32[]{:S(2)}) collective-permute-start(bf16[2,128,256]{2,1,0:T(8,128)(2,1)S(1)} %get-tuple-element.75), channel_id=1, source_target_pairs={{0,16},{4,20},{8,24},{12,28},{16,0},{20,4},{24,8},{28,12},{1,17},{... | collective-permute-start | bytes 393224 | tf_op jit(solution)/shard_map/ppermute | solution.py:574
  62.5 1.6 %collective-permute-start.23 = (bf16[2,128,256]{2,1,0:T(8,128)(2,1)S(1)}, bf16[2,128,256]{2,1,0:T(8,128)(2,1)S(1)}, u32[]{:S(2)}, u32[]{:S(2)}) collective-permute-start(bf16[2,128,256]{2,1,0:T(8,128)(2,1)S(1)} %get-tuple-element.78), channel_id=1, source_target_pairs={{0,20},{4,16},{8,28},{12,24},{16,4},{20,0},{24,12},{28,8},{1,21},{... | collective-permute-start | bytes 393224 | tf_op jit(solution)/shard_map/ppermute | solution.py:574
  64.1 1.4 %collective-permute-start.24 = (bf16[2,128,256]{2,1,0:T(8,128)(2,1)S(1)}, bf16[2,128,256]{2,1,0:T(8,128)(2,1)S(1)}, u32[]{:S(2)}, u32[]{:S(2)}) collective-permute-start(bf16[2,128,256]{2,1,0:T(8,128)(2,1)S(1)} %get-tuple-element.79), channel_id=1, source_target_pairs={{0,24},{4,28},{8,16},{12,20},{16,8},{20,12},{24,0},{28,4},{1,25},{... | collective-permute-start | bytes 393224 | tf_op jit(solution)/shard_map/ppermute | solution.py:574
  65.5 1.1 %collective-permute-done.20.refs_4_ = bf16[2,128,256]{2,1,0:T(8,128)(2,1)S(1)} collective-permute-done((bf16[2,128,256]{2,1,0:T(8,128)(2,1)S(1)}, bf16[2,128,256]{2,1,0:T(8,128)(2,1)S(1)}, u32[]{:S(2)}, u32[]{:S(2)}) %collective-permute-start.20) | collective-permute-done | bytes 131104 | tf_op jit(solution)/shard_map/ppermute | solution.py:574
  67.2 1.8 %finish.2 = (bf16[2,128,2048]{2,1,0:T(8,128)(2,1)S(1)}, bf16[128,2048]{1,0:T(8,128)(2,1)}, bf16[128,2048]{1,0:T(8,128)(2,1)}, f32[128,2048]{1,0:T(8,128)}, f32[8,128]{1,0:T(8,128)}) custom-call(bf16[128,2048]{1,0:T(8,128)(2,1)S(1)} %copy-done, bf16[128,2048]{1,0:T(8,128)(2,1)S(1)} %copy-done.1, bf16[2,128,256]{2,1,0:T(8,128)(2,1)S(1)} %get-tuple-element.72.refs_2_, ...), custom_call_target="tpu_custom_call" | custom-call | tf_op jit(solution)/shard_map/finish/pallas_call | solution.py:179
  69.0 3.4 %collective-permute-done.24.refs_3_ = bf16[2,128,256]{2,1,0:T(8,128)(2,1)S(1)} collective-permute-done((bf16[2,128,256]{2,1,0:T(8,128)(2,1)S(1)}, bf16[2,128,256]{2,1,0:T(8,128)(2,1)S(1)}, u32[]{:S(2)}, u32[]{:S(2)}) %collective-permute-start.24) | collective-permute-done | bytes 131104 | tf_op jit(solution)/shard_map/ppermute | solution.py:574
  72.4 2.0 %collective-permute-done.25.refs_4_ = bf16[2,128,256]{2,1,0:T(8,128)(2,1)S(1)} collective-permute-done((bf16[2,128,256]{2,1,0:T(8,128)(2,1)S(1)}, bf16[2,128,256]{2,1,0:T(8,128)(2,1)S(1)}, u32[]{:S(2)}, u32[]{:S(2)}) %collective-permute-start.25) | collective-permute-done | bytes 131104 | tf_op jit(solution)/shard_map/ppermute | solution.py:574
  74.4 1.7 %finish.3 = (bf16[128,2048]{1,0:T(8,128)(2,1)}, bf16[128,2048]{1,0:T(8,128)(2,1)}, f32[128,2048]{1,0:T(8,128)}, f32[8,128]{1,0:T(8,128)}) custom-call(bf16[2,128,2048]{2,1,0:T(8,128)(2,1)S(1)} %get-tuple-element.76.refs_0_, bf16[2,128,256]{2,1,0:T(8,128)(2,1)S(1)} %collective-permute-done.22.refs_1_, ...), custom_call_target="tpu_custom_call", output_to_operand_aliasing={{0}: (5, {}), {1}: (6, {}), {2}: (7, {})} | custom-call | tf_op jit(solution)/shard_map/finish/pallas_call | solution.py:179
  (44 shorter events, 3.8 us)
Async XLA Ops:
  0.6 15.3 %collective-permute-start.5 = (bf16[128,2048]{1,0:T(8,128)(2,1)}, bf16[128,2048]{1,0:T(8,128)(2,1)S(1)}, u32[]{:S(2)}, u32[]{:S(2)}) collective-permute-start(bf16[128,2048]{1,0:T(8,128)(2,1)} %refs_0_.8), channel_id=1, source_target_pairs={{1,2},{2,1},{0,4},{3,7},{5,6},{6,5},{4,0},{7,3},{9,10},{10,9},{8,1... | collective-permute-start | bytes 1572872 | tf_op jit(solution)/shard_map/ppermute | solution.py:594
  1.1 16.4 %collective-permute-start.7 = (bf16[128,2048]{1,0:T(8,128)(2,1)}, bf16[128,2048]{1,0:T(8,128)(2,1)S(1)}, u32[]{:S(2)}, u32[]{:S(2)}) collective-permute-start(bf16[128,2048]{1,0:T(8,128)(2,1)} %refs_0_.8), channel_id=1, source_target_pairs={{0,1},{1,0},{2,3},{3,2},{4,5},{5,4},{6,7},{7,6},{8,9},{9,8},{10,11... | collective-permute-start | bytes 1572872 | tf_op jit(solution)/shard_map/ppermute | solution.py:591
  7.9 2.0 %collective-permute-start = (bf16[3,4,64,256]{3,2,1,0:T(8,128)(2,1)}, bf16[3,4,64,256]{3,2,1,0:T(8,128)(2,1)S(1)}, u32[]{:S(2)}, u32[]{:S(2)}) collective-permute-start(bf16[3,4,64,256]{3,2,1,0:T(8,128)(2,1)} %get-tuple-element.46), channel_id=1, source_target_pairs={{0,4},{4,0},{8,12},{12,8},{16,20},{20,16},{24,28},{28,24},{1,5},{5... | collective-permute-start | bytes 1179656 | tf_op jit(solution)/shard_map/ppermute | solution.py:574
  7.9 2.5 %collective-permute-start.1 = (bf16[3,4,64,256]{3,2,1,0:T(8,128)(2,1)}, bf16[3,4,64,256]{3,2,1,0:T(8,128)(2,1)S(1)}, u32[]{:S(2)}, u32[]{:S(2)}) collective-permute-start(bf16[3,4,64,256]{3,2,1,0:T(8,128)(2,1)} %get-tuple-element.47), channel_id=1, source_target_pairs={{0,4},{4,0},{8,12},{12,8},{16,20},{20,16},{24,28},{28,24},{1,5},{5... | collective-permute-start | bytes 1179656 | tf_op jit(solution)/shard_map/ppermute | solution.py:574
  10.4 0.7 copy-start.5
  12.4 11.3 %collective-permute-start.2 = (bf16[2,2,128,256]{3,2,1,0:T(8,128)(2,1)S(1)}, bf16[2,2,128,256]{3,2,1,0:T(8,128)(2,1)S(1)}, u32[]{:S(2)}, u32[]{:S(2)}) collective-permute-start(bf16[2,2,128,256]{3,2,1,0:T(8,128)(2,1)S(1)} %get-tuple-element.50), channel_id=1, source_target_pairs={{0,8},{4,12},{8,0},{12,4},{16,24},{20,28},{24,16},{28,20},{1,9},{5... | collective-permute-start | bytes 786440 | tf_op jit(solution)/shard_map/ppermute | solution.py:574
  14.0 13.7 %collective-permute-start.3 = (bf16[2,2,128,256]{3,2,1,0:T(8,128)(2,1)S(1)}, bf16[2,2,128,256]{3,2,1,0:T(8,128)(2,1)S(1)}, u32[]{:S(2)}, u32[]{:S(2)}) collective-permute-start(bf16[2,2,128,256]{3,2,1,0:T(8,128)(2,1)S(1)} %get-tuple-element.51), channel_id=1, source_target_pairs={{0,16},{4,20},{8,24},{12,28},{16,0},{20,4},{24,8},{28,12},{1,17},{... | collective-permute-start | bytes 786440 | tf_op jit(solution)/shard_map/ppermute | solution.py:574
  15.5 12.2 %collective-permute-start.4 = (bf16[2,2,128,256]{3,2,1,0:T(8,128)(2,1)S(1)}, bf16[2,2,128,256]{3,2,1,0:T(8,128)(2,1)S(1)}, u32[]{:S(2)}, u32[]{:S(2)}) collective-permute-start(bf16[2,2,128,256]{3,2,1,0:T(8,128)(2,1)S(1)} %get-tuple-element.52), channel_id=1, source_target_pairs={{0,24},{4,28},{8,16},{12,20},{16,8},{20,12},{24,0},{28,4},{1,25},{... | collective-permute-start | bytes 786440 | tf_op jit(solution)/shard_map/ppermute | solution.py:574
  16.0 13.2 %collective-permute-start.6 = (bf16[128,2048]{1,0:T(8,128)(2,1)S(1)}, bf16[128,2048]{1,0:T(8,128)(2,1)S(1)}, u32[]{:S(2)}, u32[]{:S(2)}) collective-permute-start(bf16[128,2048]{1,0:T(8,128)(2,1)S(1)} %collective-permute-done.5.refs_1_), channel_id=1, source_target_pairs={{0,1},{1,0},{2,3},{3,2},{4,5},{5,4},{6,7},{7,6},{8,9},{9,8},{10,11... | collective-permute-start | bytes 1572872 | tf_op jit(solution)/shard_map/ppermute | solution.py:591
  17.6 11.6 %collective-permute-start.8 = (bf16[128,2048]{1,0:T(8,128)(2,1)S(1)}, bf16[128,2048]{1,0:T(8,128)(2,1)S(1)}, u32[]{:S(2)}, u32[]{:S(2)}) collective-permute-start(bf16[128,2048]{1,0:T(8,128)(2,1)S(1)} %collective-permute-done.7.refs_0_), channel_id=1, source_target_pairs={{1,2},{2,1},{0,4},{3,7},{5,6},{6,5},{4,0},{7,3},{9,10},{10,9},{8,1... | collective-permute-start | bytes 1572872 | tf_op jit(solution)/shard_map/ppermute | solution.py:594
  17.6 6.1 %copy-start.2 = (bf16[128,2048]{1,0:T(8,128)(2,1)S(1)}, bf16[128,2048]{1,0:T(8,128)(2,1)}, u32[]{:S(2)}) copy-start(bf16[128,2048]{1,0:T(8,128)(2,1)} %refs_0_.8) | copy-start | bytes 1572868
  17.6 10.1 %copy-start.3 = (bf16[512,256]{1,0:T(8,128)(2,1)S(1)}, bf16[512,256]{1,0:T(8,128)(2,1)}, u32[]{:S(2)}) copy-start(bf16[512,256]{1,0:T(8,128)(2,1)} %constant.4.clone.refs_0_) | copy-start | bytes 786436
  23.7 7.7 %collective-permute-start.13 = (bf16[128,2048]{1,0:T(8,128)(2,1)S(1)}, bf16[128,2048]{1,0:T(8,128)(2,1)S(1)}, u32[]{:S(2)}, u32[]{:S(2)}) collective-permute-start(bf16[128,2048]{1,0:T(8,128)(2,1)S(1)} %copy-done.2), channel_id=1, source_target_pairs={{0,4},{4,0},{8,12},{12,8},{16,20},{20,16},{24,28},{28,24},{1,5},{5... | collective-permute-start | bytes 1572872 | tf_op jit(solution)/shard_map/ppermute | solution.py:574
  27.7 5.7 %collective-permute-start.12 = (bf16[128,2048]{1,0:T(8,128)(2,1)S(1)}, bf16[128,2048]{1,0:T(8,128)(2,1)S(1)}, u32[]{:S(2)}, u32[]{:S(2)}) collective-permute-start(bf16[128,2048]{1,0:T(8,128)(2,1)S(1)} %collective-permute-done.7.refs_0_), channel_id=1, source_target_pairs={{0,4},{4,0},{8,12},{12,8},{16,20},{20,16},{24,28},{28,24},{1,5},{5... | collective-permute-start | bytes 1572872 | tf_op jit(solution)/shard_map/ppermute | solution.py:574
  29.2 14.4 %collective-permute-start.9 = (bf16[128,2048]{1,0:T(8,128)(2,1)S(1)}, bf16[128,2048]{1,0:T(8,128)(2,1)S(1)}, u32[]{:S(2)}, u32[]{:S(2)}) collective-permute-start(bf16[128,2048]{1,0:T(8,128)(2,1)S(1)} %get-tuple-element.57.refs_1_), channel_id=1, source_target_pairs={{0,1},{1,0},{2,3},{3,2},{4,5},{5,4},{6,7},{7,6},{8,9},{9,8},{10,11... | collective-permute-start | bytes 1572872 | tf_op jit(solution)/shard_map/ppermute | solution.py:591
  31.4 12.2 %collective-permute-start.15 = (bf16[128,2048]{1,0:T(8,128)(2,1)S(1)}, bf16[128,2048]{1,0:T(8,128)(2,1)S(1)}, u32[]{:S(2)}, u32[]{:S(2)}) collective-permute-start(bf16[128,2048]{1,0:T(8,128)(2,1)S(1)} %collective-permute-done.5.refs_1_), channel_id=1, source_target_pairs={{0,4},{4,0},{8,12},{12,8},{16,20},{20,16},{24,28},{28,24},{1,5},{5... | collective-permute-start | bytes 1572872 | tf_op jit(solution)/shard_map/ppermute | solution.py:574
  35.4 8.2 %collective-permute-start.14 = (bf16[128,2048]{1,0:T(8,128)(2,1)S(1)}, bf16[128,2048]{1,0:T(8,128)(2,1)S(1)}, u32[]{:S(2)}, u32[]{:S(2)}) collective-permute-start(bf16[128,2048]{1,0:T(8,128)(2,1)S(1)} %get-tuple-element.63.refs_0_), channel_id=1, source_target_pairs={{0,4},{4,0},{8,12},{12,8},{16,20},{20,16},{24,28},{28,24},{1,5},{5... | collective-permute-start | bytes 1572872 | tf_op jit(solution)/shard_map/ppermute | solution.py:574
  35.9 9.8 %collective-permute-start.11 = (bf16[128,2048]{1,0:T(8,128)(2,1)S(1)}, bf16[128,2048]{1,0:T(8,128)(2,1)S(1)}, u32[]{:S(2)}, u32[]{:S(2)}) collective-permute-start(bf16[128,2048]{1,0:T(8,128)(2,1)S(1)} %get-tuple-element.57.refs_1_), channel_id=1, source_target_pairs={{0,4},{4,0},{8,12},{12,8},{16,20},{20,16},{24,28},{28,24},{1,5},{5... | collective-permute-start | bytes 1572872 | tf_op jit(solution)/shard_map/ppermute | solution.py:574
  43.6 2.2 %collective-permute-start.10 = (bf16[128,2048]{1,0:T(8,128)(2,1)S(1)}, bf16[128,2048]{1,0:T(8,128)(2,1)S(1)}, u32[]{:S(2)}, u32[]{:S(2)}) collective-permute-start(bf16[128,2048]{1,0:T(8,128)(2,1)S(1)} %collective-permute-done.9.refs_0_), channel_id=1, source_target_pairs={{0,4},{4,0},{8,12},{12,8},{16,20},{20,16},{24,28},{28,24},{1,5},{5... | collective-permute-start | bytes 1572872 | tf_op jit(solution)/shard_map/ppermute | solution.py:574
  43.6 13.4 %copy-start.4 = (bf16[256,512]{1,0:T(8,128)(2,1)S(1)}, bf16[256,512]{1,0:T(8,128)(2,1)}, u32[]{:S(2)}) copy-start(bf16[256,512]{1,0:T(8,128)(2,1)} %constant.5.clone.refs_1_) | copy-start | bytes 786436
  45.7 21.5 %copy-start = (bf16[128,2048]{1,0:T(8,128)(2,1)S(1)}, bf16[128,2048]{1,0:T(8,128)(2,1)}, u32[]{:S(2)}) copy-start(bf16[128,2048]{1,0:T(8,128)(2,1)} %refs_0_.9) | copy-start | bytes 1572868
  45.8 21.4 %copy-start.1 = (bf16[128,2048]{1,0:T(8,128)(2,1)S(1)}, bf16[128,2048]{1,0:T(8,128)(2,1)}, u32[]{:S(2)}) copy-start(bf16[128,2048]{1,0:T(8,128)(2,1)} %refs_1_.4) | copy-start | bytes 1572868
  47.2 7.3 %collective-permute-start.16 = (bf16[2,128,256]{2,1,0:T(8,128)(2,1)S(1)}, bf16[2,128,256]{2,1,0:T(8,128)(2,1)S(1)}, u32[]{:S(2)}, u32[]{:S(2)}) collective-permute-start(bf16[2,128,256]{2,1,0:T(8,128)(2,1)S(1)} %get-tuple-element.69), channel_id=1, source_target_pairs={{0,24},{4,28},{8,16},{12,20},{16,8},{20,12},{24,0},{28,4},{1,25},{... | collective-permute-start | bytes 393224 | tf_op jit(solution)/shard_map/ppermute | solution.py:574
  48.8 8.1 %collective-permute-start.17 = (bf16[2,128,256]{2,1,0:T(8,128)(2,1)S(1)}, bf16[2,128,256]{2,1,0:T(8,128)(2,1)S(1)}, u32[]{:S(2)}, u32[]{:S(2)}) collective-permute-start(bf16[2,128,256]{2,1,0:T(8,128)(2,1)S(1)} %get-tuple-element.70), channel_id=1, source_target_pairs={{0,16},{4,20},{8,24},{12,28},{16,0},{20,4},{24,8},{28,12},{1,17},{... | collective-permute-start | bytes 393224 | tf_op jit(solution)/shard_map/ppermute | solution.py:574
  48.9 8.1 %collective-permute-start.18 = (bf16[2,128,256]{2,1,0:T(8,128)(2,1)S(1)}, bf16[2,128,256]{2,1,0:T(8,128)(2,1)S(1)}, u32[]{:S(2)}, u32[]{:S(2)}) collective-permute-start(bf16[2,128,256]{2,1,0:T(8,128)(2,1)S(1)} %get-tuple-element.71), channel_id=1, source_target_pairs={{0,8},{4,12},{8,0},{12,4},{16,24},{20,28},{24,16},{28,20},{1,9},{5... | collective-permute-start | bytes 393224 | tf_op jit(solution)/shard_map/ppermute | solution.py:574
  60.3 3.8 %collective-permute-start.19 = (bf16[2,128,256]{2,1,0:T(8,128)(2,1)S(1)}, bf16[2,128,256]{2,1,0:T(8,128)(2,1)S(1)}, u32[]{:S(2)}, u32[]{:S(2)}) collective-permute-start(bf16[2,128,256]{2,1,0:T(8,128)(2,1)S(1)} %get-tuple-element.73), channel_id=1, source_target_pairs={{0,4},{4,0},{8,12},{12,8},{16,20},{20,16},{24,28},{28,24},{1,5},{5... | collective-permute-start | bytes 393224 | tf_op jit(solution)/shard_map/ppermute | solution.py:574
  60.3 6.3 %collective-permute-start.20 = (bf16[2,128,256]{2,1,0:T(8,128)(2,1)S(1)}, bf16[2,128,256]{2,1,0:T(8,128)(2,1)S(1)}, u32[]{:S(2)}, u32[]{:S(2)}) collective-permute-start(bf16[2,128,256]{2,1,0:T(8,128)(2,1)S(1)} %get-tuple-element.74), channel_id=1, source_target_pairs={{0,8},{4,12},{8,0},{12,4},{16,24},{20,28},{24,16},{28,20},{1,9},{5... | collective-permute-start | bytes 393224 | tf_op jit(solution)/shard_map/ppermute | solution.py:574
  60.9 6.3 %collective-permute-start.21 = (bf16[2,128,256]{2,1,0:T(8,128)(2,1)S(1)}, bf16[2,128,256]{2,1,0:T(8,128)(2,1)S(1)}, u32[]{:S(2)}, u32[]{:S(2)}) collective-permute-start(bf16[2,128,256]{2,1,0:T(8,128)(2,1)S(1)} %get-tuple-element.75), channel_id=1, source_target_pairs={{0,16},{4,20},{8,24},{12,28},{16,0},{20,4},{24,8},{28,12},{1,17},{... | collective-permute-start | bytes 393224 | tf_op jit(solution)/shard_map/ppermute | solution.py:574
  62.3 6.7 %collective-permute-start.22 = (bf16[2,128,256]{2,1,0:T(8,128)(2,1)S(1)}, bf16[2,128,256]{2,1,0:T(8,128)(2,1)S(1)}, u32[]{:S(2)}, u32[]{:S(2)}) collective-permute-start(bf16[2,128,256]{2,1,0:T(8,128)(2,1)S(1)} %get-tuple-element.77), channel_id=1, source_target_pairs={{0,12},{4,8},{8,4},{12,0},{16,28},{20,24},{24,20},{28,16},{1,13},{... | collective-permute-start | bytes 393224 | tf_op jit(solution)/shard_map/ppermute | solution.py:574
  62.5 6.5 %collective-permute-start.23 = (bf16[2,128,256]{2,1,0:T(8,128)(2,1)S(1)}, bf16[2,128,256]{2,1,0:T(8,128)(2,1)S(1)}, u32[]{:S(2)}, u32[]{:S(2)}) collective-permute-start(bf16[2,128,256]{2,1,0:T(8,128)(2,1)S(1)} %get-tuple-element.78), channel_id=1, source_target_pairs={{0,20},{4,16},{8,28},{12,24},{16,4},{20,0},{24,12},{28,8},{1,21},{... | collective-permute-start | bytes 393224 | tf_op jit(solution)/shard_map/ppermute | solution.py:574
  64.1 8.3 %collective-permute-start.24 = (bf16[2,128,256]{2,1,0:T(8,128)(2,1)S(1)}, bf16[2,128,256]{2,1,0:T(8,128)(2,1)S(1)}, u32[]{:S(2)}, u32[]{:S(2)}) collective-permute-start(bf16[2,128,256]{2,1,0:T(8,128)(2,1)S(1)} %get-tuple-element.79), channel_id=1, source_target_pairs={{0,24},{4,28},{8,16},{12,20},{16,8},{20,12},{24,0},{28,4},{1,25},{... | collective-permute-start | bytes 393224 | tf_op jit(solution)/shard_map/ppermute | solution.py:574
  66.6 7.8 %collective-permute-start.25 = (bf16[2,128,256]{2,1,0:T(8,128)(2,1)S(1)}, bf16[2,128,256]{2,1,0:T(8,128)(2,1)S(1)}, u32[]{:S(2)}, u32[]{:S(2)}) collective-permute-start(bf16[2,128,256]{2,1,0:T(8,128)(2,1)S(1)} %get-tuple-element.80), channel_id=1, source_target_pairs={{0,28},{4,24},{8,20},{12,16},{16,12},{20,8},{24,4},{28,0},{1,29},{... | collective-permute-start | bytes 393224 | tf_op jit(solution)/shard_map/ppermute | solution.py:574

commit v7 on v6

--- a/solution.py
+++ b/solution.py
@@ -11,6 +11,7 @@
 from jax.sharding import PartitionSpec as P
 
 LANES = 128
+PIECES = 4
 
 
 def build_tables(seg_len):
@@ -317,17 +318,21 @@
 
 
 def fetch(spot, groups, x, sem):
-    rows = groups[0][0].shape[0]
+    rows = groups[0][0].shape[0] // PIECES
+    waits = []
     for i, group in enumerate(groups):
-        to = x.at[pl.ds(i * rows, rows)]
-        for j, ref in enumerate(group):
-            copy = pltpu.make_async_copy(ref, to, sem.at[i])
+        for p in range(PIECES):
+            at = i * PIECES + p
+            to = x.at[pl.ds(at * rows, rows)]
+            copies = [pltpu.make_async_copy(ref.at[pl.ds(p * rows, rows)], to, sem.at[at]) for ref in group]
             if len(group) == 1:
-                copy.start()
+                copies[0].start()
             else:
-                pl.when(spot.outer if j == 0 else ~spot.outer)(copy.start)
-    for i, group in enumerate(groups):
-        pltpu.make_async_copy(group[0], x.at[pl.ds(i * rows, rows)], sem.at[i]).wait()
+                pl.when(spot.outer)(copies[0].start)
+                pl.when(~spot.outer)(copies[1].start)
+            waits.append(copies[0])
+    for copy in waits:
+        copy.wait()
 
 
 def grouped(refs, sizes):
@@ -363,7 +368,7 @@
         [pltpu.VMEM(out, jnp.float32)],
         [VMEM],
         "mix",
-        [pltpu.VMEM((rows, depth), jnp.bfloat16), pltpu.SemaphoreType.DMA((len(groups),))],
+        [pltpu.VMEM((rows, depth), jnp.bfloat16), pltpu.SemaphoreType.DMA((PIECES * len(groups),))],
         **order,
     )
 
@@ -396,7 +401,7 @@
         [piece] * chips,
         [whole(piece)] * chips,
         "mix_gate",
-        [pltpu.VMEM((2 * rows, depth), jnp.bfloat16), pltpu.SemaphoreType.DMA((len(groups),))],
+        [pltpu.VMEM((2 * rows, depth), jnp.bfloat16), pltpu.SemaphoreType.DMA((PIECES * len(groups),))],
     )
 
 

time: 76.3 us -> 79 us (1.035)
  Pallas kernels: 25.8 us -> 31.1 us
  waiting for transfers between devices: 26 us -> 23.3 us
    pallas_call x12, Pallas kernels: 25.8 us -> 31.1 us  [call(): pl.pallas_call(body, input_output_aliases={count + i: results + i for i i...]
    ppermute x3, waiting for transfers between devices: 7.56 us -> 4.91 us  [send_outer(): return lax.ppermute(x, 'ch', outer)]
  transfers between devices with their start and end apart: 26 -> 26, of which waited for: 11 -> 11; matrix products, arithmetic and copies ran while one was open for 0% -> 0% of each run, Pallas kernels for 25% -> 30%
where the time goes in v7:
time: 79 us; the launch traced here: 78.8 us
  Pallas kernels  31.1 us (39%)
  waiting for transfers between devices  23.3 us (29%)
  starting transfers between devices  22.8 us (29%)
  between operations  0.85 us (1%)
    pallas_call x12, Pallas kernels, call(): pl.pallas_call(body, input_output_aliases={count + i: results + i for i i...  31.1 us
    ppermute x21, waiting for transfers between devices, swap(): return lax.ppermute(x, 'seq', [(i, i ^ k) for i in range(n)]) if k else x  18.4 us
    ppermute x21, starting transfers between devices, swap(): return lax.ppermute(x, 'seq', [(i, i ^ k) for i in range(n)]) if k else x  14.4 us
    ppermute x3, starting transfers between devices, send_outer(): return lax.ppermute(x, 'ch', outer)  7.95 us
    ppermute x3, waiting for transfers between devices, send_outer(): return lax.ppermute(x, 'ch', outer)  4.91 us
  transfers between devices with their start and end apart: 26, of which 11 were waited for; matrix products, arithmetic and copies ran while one was open for 0% of the time, Pallas kernels for 30%

profile of v7, /device:TPU:0, one launch (start us, length us, event | category | flops | bytes accessed | tf_op | source)
XLA Modules:
  0.0 78.8 jit_solution(5291600128125623091)
XLA Ops:
  1.1 4.1 %collective-permute-start.7 = (bf16[128,2048]{1,0:T(8,128)(2,1)}, bf16[128,2048]{1,0:T(8,128)(2,1)S(1)}, u32[]{:S(2)}, u32[]{:S(2)}) collective-permute-start(bf16[128,2048]{1,0:T(8,128)(2,1)} %refs_0_.8), channel_id=1, source_target_pairs={{0,1},{1,0},{2,3},{3,2},{4,5},{5,4},{6,7},{7,6},{8,9},{9,8},{10,11... | collective-permute-start | bytes 1572872 | tf_op jit(solution)/shard_map/ppermute | solution.py:596
  5.3 2.5 %pack_core.1 = (bf16[3,4,128,256]{3,2,1,0:T(8,128)(2,1)S(1)}, bf16[3,4,64,256]{3,2,1,0:T(8,128)(2,1)}, bf16[3,4,64,256]{3,2,1,0:T(8,128)(2,1)}, f32[8,128]{1,0:T(8,128)}) custom-call(bf16[128,2048]{1,0:T(8,128)(2,1)} %refs_0_.6, bf16[128,2048]{1,0:T(8,128)(2,1)} %refs_0_.9, bf16[128,2048]{1,0:T(8,128)(2,1)} %refs_1_.4, bf16[128,2048]{1,0:T(8,128)(2,1)} %refs_3_.1), custom_call_target="tpu_custom_call" | custom-call | tf_op jit(solution)/shard_map/pack_core/pallas_call | solution.py:180
  8.4 1.4 %collective-permute-done.refs_1_ = bf16[3,4,64,256]{3,2,1,0:T(8,128)(2,1)S(1)} collective-permute-done((bf16[3,4,64,256]{3,2,1,0:T(8,128)(2,1)}, bf16[3,4,64,256]{3,2,1,0:T(8,128)(2,1)S(1)}, u32[]{:S(2)}, u32[]{:S(2)}) %collective-permute-start) | collective-permute-done | bytes 393248 | tf_op jit(solution)/shard_map/ppermute | solution.py:579
  9.9 0.6 collective-permute-done.1.refs_2_
  10.4 0.7 copy-done.5
  11.1 1.3 %merge_cores.1 = (bf16[4,2,128,256]{3,2,1,0:T(8,128)(2,1)S(1)}, bf16[2,2,128,256]{3,2,1,0:T(8,128)(2,1)S(1)}, bf16[2,2,128,256]{3,2,1,0:T(8,128)(2,1)S(1)}, bf16...) custom-call(bf16[3,4,128,256]{3,2,1,0:T(8,128)(2,1)S(1)} %get-tuple-element.45.refs_0_, ...), custom_call_target="tpu_custom_call" | custom-call | tf_op jit(solution)/shard_map/merge_cores/pallas_call | solution.py:180
  12.4 1.6 %collective-permute-start.2 = (bf16[2,2,128,256]{3,2,1,0:T(8,128)(2,1)S(1)}, bf16[2,2,128,256]{3,2,1,0:T(8,128)(2,1)S(1)}, u32[]{:S(2)}, u32[]{:S(2)}) collective-permute-start(bf16[2,2,128,256]{3,2,1,0:T(8,128)(2,1)S(1)} %get-tuple-element.50), channel_id=1, source_target_pairs={{0,8},{4,12},{8,0},{12,4},{16,24},{20,28},{24,16},{28,20},{1,9},{5... | collective-permute-start | bytes 786440 | tf_op jit(solution)/shard_map/ppermute | solution.py:579
  14.0 1.5 %collective-permute-start.3 = (bf16[2,2,128,256]{3,2,1,0:T(8,128)(2,1)S(1)}, bf16[2,2,128,256]{3,2,1,0:T(8,128)(2,1)S(1)}, u32[]{:S(2)}, u32[]{:S(2)}) collective-permute-start(bf16[2,2,128,256]{3,2,1,0:T(8,128)(2,1)S(1)} %get-tuple-element.51), channel_id=1, source_target_pairs={{0,16},{4,20},{8,24},{12,28},{16,0},{20,4},{24,8},{28,12},{1,17},{... | collective-permute-start | bytes 786440 | tf_op jit(solution)/shard_map/ppermute | solution.py:579
  16.0 1.6 %collective-permute-start.6 = (bf16[128,2048]{1,0:T(8,128)(2,1)S(1)}, bf16[128,2048]{1,0:T(8,128)(2,1)S(1)}, u32[]{:S(2)}, u32[]{:S(2)}) collective-permute-start(bf16[128,2048]{1,0:T(8,128)(2,1)S(1)} %collective-permute-done.5.refs_1_), channel_id=1, source_target_pairs={{0,1},{1,0},{2,3},{3,2},{4,5},{5,4},{6,7},{7,6},{8,9},{9,8},{10,11... | collective-permute-start | bytes 1572872 | tf_op jit(solution)/shard_map/ppermute | solution.py:596
  17.6 6.0 %load_weight.1 = (bf16[4,256,8192]{2,1,0:T(8,128)(2,1)S(1)}, f32[8,128]{1,0:T(8,128)S(1)}) custom-call(bf16[2048,8192]{1,0:T(8,128)(2,1)} %refs_0_.7, f32[8,128]{1,0:T(8,128)S(1)} %get-tuple-element.53.refs_1_), custom_call_target="tpu_custom_call" | custom-call | tf_op jit(solution)/shard_map/load_weight/pallas_call | solution.py:180
  24.2 3.4 %collective-permute-done.3.refs_3_ = bf16[2,2,128,256]{3,2,1,0:T(8,128)(2,1)S(1)} collective-permute-done((bf16[2,2,128,256]{3,2,1,0:T(8,128)(2,1)S(1)}, bf16[2,2,128,256]{3,2,1,0:T(8,128)(2,1)S(1)}, u32[]{:S(2)}, u32[]{:S(2)}) %collective-permute-start.3) | collective-permute-done | bytes 262176 | tf_op jit(solution)/shard_map/ppermute | solution.py:579
  27.7 1.5 %kernels.1 = (bf16[2,4,512,256]{3,2,1,0:T(8,128)(2,1)S(1)}, f32[8,128]{1,0:T(8,128)S(1)}) custom-call(bf16[512,256]{1,0:T(8,128)(2,1)S(1)} %copy-done.3, bf16[2,2,128,256]{3,2,1,0:T(8,128)(2,1)S(1)} %get-tuple-element.49.refs_1_, bf16[2,2,128,256]{3,2,1,0:T(8,128)(2,1)S(1)} %collective-permute-done.2.refs_2_, ...), custom_call_target="tpu_custom_call" | custom-call | flops 3221225472 | tf_op jit(solution)/shard_map/kernels/pallas_call | solution.py:180
  29.2 2.2 %collective-permute-start.9 = (bf16[128,2048]{1,0:T(8,128)(2,1)S(1)}, bf16[128,2048]{1,0:T(8,128)(2,1)S(1)}, u32[]{:S(2)}, u32[]{:S(2)}) collective-permute-start(bf16[128,2048]{1,0:T(8,128)(2,1)S(1)} %get-tuple-element.57.refs_1_), channel_id=1, source_target_pairs={{0,1},{1,0},{2,3},{3,2},{4,5},{5,4},{6,7},{7,6},{8,9},{9,8},{10,11... | collective-permute-start | bytes 1572872 | tf_op jit(solution)/shard_map/ppermute | solution.py:596
  31.4 3.3 %mix.3 = (f32[4,256,256]{2,1,0:T(8,128)S(1)}, f32[8,128]{1,0:T(8,128)S(1)}) custom-call(bf16[128,2048]{1,0:T(8,128)(2,1)S(1)} %copy-done.2, bf16[128,2048]{1,0:T(8,128)(2,1)S(1)} %collective-permute-done.13.refs_1_, bf16[4,256,8192]{2,1,0:T(8,128)(2,1)S(1)} %get-tuple-element.58.refs_2_.refs_4_, f32[8,128]{1,0:T(8,128)S(1)} %get-tuple-element.59.refs_3_), custom_call_target="tpu_custom_call" | custom-call | tf_op jit(solution)/shard_map/mix/pallas_call | solution.py:180
  34.7 3.3 %mix.4 = (f32[4,256,256]{2,1,0:T(8,128)S(1)}, bf16[128,2048]{1,0:T(8,128)(2,1)S(1)}, f32[8,128]{1,0:T(8,128)S(1)}) custom-call(bf16[128,2048]{1,0:T(8,128)(2,1)S(1)} %collective-permute-done.7.refs_0_, bf16[128,2048]{1,0:T(8,128)(2,1)S(1)} %collective-permute-done.12.refs_1_, ...), custom_call_target="tpu_custom_call", output_to_operand_aliasing={{1}: (4, {})} | custom-call | tf_op jit(solution)/shard_map/mix/pallas_call | solution.py:180
  38.0 0.6 collective-permute-start.14
  38.7 4.9 %collective-permute-done.9.refs_0_ = bf16[128,2048]{1,0:T(8,128)(2,1)S(1)} collective-permute-done((bf16[128,2048]{1,0:T(8,128)(2,1)S(1)}, bf16[128,2048]{1,0:T(8,128)(2,1)S(1)}, u32[]{:S(2)}, u32[]{:S(2)}) %collective-permute-start.9) | collective-permute-done | bytes 524320 | tf_op jit(solution)/shard_map/ppermute | solution.py:596
  43.6 3.5 %mix.5 = (f32[4,256,256]{2,1,0:T(8,128)S(1)}, f32[8,128]{1,0:T(8,128)}) custom-call(bf16[128,2048]{1,0:T(8,128)(2,1)S(1)} %get-tuple-element.63.refs_0_, bf16[128,2048]{1,0:T(8,128)(2,1)S(1)} %collective-permute-done.5.refs_1_, bf16[128,2048]{1,0:T(8,128)(2,1)S(1)} %collective-permute-done.14.refs_2_, bf16[128,2048]{1,0:T(8,128)(2,1)S(1)} %collective-permute-done.15.refs_3_, ...), custom_call_target="tpu_custom_call" | custom-call | tf_op jit(solution)/shard_map/mix/pallas_call | solution.py:180
  47.1 2.8 %mix_gate.1 = (bf16[2,128,256]{2,1,0:T(8,128)(2,1)S(1)}, bf16[2,128,256]{2,1,0:T(8,128)(2,1)S(1)}, bf16[2,128,256]{2,1,0:T(8,128)(2,1)S(1)}, bf16[2,128,256]{2,1,0:T(8,128)(2,1)S(1)}, f32[8,128]{1,0:T(8,128)}) custom-call(bf16[128,2048]{1,0:T(8,128)(2,1)S(1)} %collective-permute-done.9.refs_0_, bf16[128,2048]{1,0:T(8,128)(2,1)S(1)} %get-tuple-element.57.refs_1_, ...), custom_call_target="tpu_custom_call" | custom-call | tf_op jit(solution)/shard_map/mix_gate/pallas_call | solution.py:180
  49.9 1.6 %collective-permute-start.16 = (bf16[2,128,256]{2,1,0:T(8,128)(2,1)S(1)}, bf16[2,128,256]{2,1,0:T(8,128)(2,1)S(1)}, u32[]{:S(2)}, u32[]{:S(2)}) collective-permute-start(bf16[2,128,256]{2,1,0:T(8,128)(2,1)S(1)} %get-tuple-element.69), channel_id=1, source_target_pairs={{0,24},{4,28},{8,16},{12,20},{16,8},{20,12},{24,0},{28,4},{1,25},{... | collective-permute-start | bytes 393224 | tf_op jit(solution)/shard_map/ppermute | solution.py:579
  51.6 1.9 %collective-permute-start.18 = (bf16[2,128,256]{2,1,0:T(8,128)(2,1)S(1)}, bf16[2,128,256]{2,1,0:T(8,128)(2,1)S(1)}, u32[]{:S(2)}, u32[]{:S(2)}) collective-permute-start(bf16[2,128,256]{2,1,0:T(8,128)(2,1)S(1)} %get-tuple-element.71), channel_id=1, source_target_pairs={{0,8},{4,12},{8,0},{12,4},{16,24},{20,28},{24,16},{28,20},{1,9},{5... | collective-permute-start | bytes 393224 | tf_op jit(solution)/shard_map/ppermute | solution.py:579
  53.5 3.7 %collective-permute-done.16.refs_4_ = bf16[2,128,256]{2,1,0:T(8,128)(2,1)S(1)} collective-permute-done((bf16[2,128,256]{2,1,0:T(8,128)(2,1)S(1)}, bf16[2,128,256]{2,1,0:T(8,128)(2,1)S(1)}, u32[]{:S(2)}, u32[]{:S(2)}) %collective-permute-start.16) | collective-permute-done | bytes 131104 | tf_op jit(solution)/shard_map/ppermute | solution.py:579
  57.2 2.4 %collective-permute-done.17.refs_5_ = bf16[2,128,256]{2,1,0:T(8,128)(2,1)S(1)} collective-permute-done((bf16[2,128,256]{2,1,0:T(8,128)(2,1)S(1)}, bf16[2,128,256]{2,1,0:T(8,128)(2,1)S(1)}, u32[]{:S(2)}, u32[]{:S(2)}) %collective-permute-start.17) | collective-permute-done | bytes 131104 | tf_op jit(solution)/shard_map/ppermute | solution.py:579
  59.7 3.3 %correlate.1 = (bf16[2,128,256]{2,1,0:T(8,128)(2,1)S(1)}, bf16[2,128,256]{2,1,0:T(8,128)(2,1)S(1)}, bf16[2,128,256]{2,1,0:T(8,128)(2,1)S(1)}, bf16[2,128,256]{2,...) custom-call(bf16[512,256]{1,0:T(8,128)(2,1)S(1)} %copy-done.3, ...), custom_call_target="tpu_custom_call" | custom-call | tf_op jit(solution)/shard_map/correlate/pallas_call | solution.py:180
  63.5 1.5 %collective-permute-start.21 = (bf16[2,128,256]{2,1,0:T(8,128)(2,1)S(1)}, bf16[2,128,256]{2,1,0:T(8,128)(2,1)S(1)}, u32[]{:S(2)}, u32[]{:S(2)}) collective-permute-start(bf16[2,128,256]{2,1,0:T(8,128)(2,1)S(1)} %get-tuple-element.75), channel_id=1, source_target_pairs={{0,16},{4,20},{8,24},{12,28},{16,0},{20,4},{24,8},{28,12},{1,17},{... | collective-permute-start | bytes 393224 | tf_op jit(solution)/shard_map/ppermute | solution.py:579
  65.2 1.6 %collective-permute-start.23 = (bf16[2,128,256]{2,1,0:T(8,128)(2,1)S(1)}, bf16[2,128,256]{2,1,0:T(8,128)(2,1)S(1)}, u32[]{:S(2)}, u32[]{:S(2)}) collective-permute-start(bf16[2,128,256]{2,1,0:T(8,128)(2,1)S(1)} %get-tuple-element.78), channel_id=1, source_target_pairs={{0,20},{4,16},{8,28},{12,24},{16,4},{20,0},{24,12},{28,8},{1,21},{... | collective-permute-start | bytes 393224 | tf_op jit(solution)/shard_map/ppermute | solution.py:579
  66.8 1.4 %collective-permute-start.24 = (bf16[2,128,256]{2,1,0:T(8,128)(2,1)S(1)}, bf16[2,128,256]{2,1,0:T(8,128)(2,1)S(1)}, u32[]{:S(2)}, u32[]{:S(2)}) collective-permute-start(bf16[2,128,256]{2,1,0:T(8,128)(2,1)S(1)} %get-tuple-element.79), channel_id=1, source_target_pairs={{0,24},{4,28},{8,16},{12,20},{16,8},{20,12},{24,0},{28,4},{1,25},{... | collective-permute-start | bytes 393224 | tf_op jit(solution)/shard_map/ppermute | solution.py:579
  68.2 1.1 %collective-permute-done.20.refs_4_ = bf16[2,128,256]{2,1,0:T(8,128)(2,1)S(1)} collective-permute-done((bf16[2,128,256]{2,1,0:T(8,128)(2,1)S(1)}, bf16[2,128,256]{2,1,0:T(8,128)(2,1)S(1)}, u32[]{:S(2)}, u32[]{:S(2)}) %collective-permute-start.20) | collective-permute-done | bytes 131104 | tf_op jit(solution)/shard_map/ppermute | solution.py:579
  69.9 1.8 %finish.2 = (bf16[2,128,2048]{2,1,0:T(8,128)(2,1)S(1)}, bf16[128,2048]{1,0:T(8,128)(2,1)}, bf16[128,2048]{1,0:T(8,128)(2,1)}, f32[128,2048]{1,0:T(8,128)}, f32[8,128]{1,0:T(8,128)}) custom-call(bf16[128,2048]{1,0:T(8,128)(2,1)S(1)} %copy-done, bf16[128,2048]{1,0:T(8,128)(2,1)S(1)} %copy-done.1, bf16[2,128,256]{2,1,0:T(8,128)(2,1)S(1)} %get-tuple-element.72.refs_2_, ...), custom_call_target="tpu_custom_call" | custom-call | tf_op jit(solution)/shard_map/finish/pallas_call | solution.py:180
  71.7 3.4 %collective-permute-done.24.refs_3_ = bf16[2,128,256]{2,1,0:T(8,128)(2,1)S(1)} collective-permute-done((bf16[2,128,256]{2,1,0:T(8,128)(2,1)S(1)}, bf16[2,128,256]{2,1,0:T(8,128)(2,1)S(1)}, u32[]{:S(2)}, u32[]{:S(2)}) %collective-permute-start.24) | collective-permute-done | bytes 131104 | tf_op jit(solution)/shard_map/ppermute | solution.py:579
  75.1 2.0 %collective-permute-done.25.refs_4_ = bf16[2,128,256]{2,1,0:T(8,128)(2,1)S(1)} collective-permute-done((bf16[2,128,256]{2,1,0:T(8,128)(2,1)S(1)}, bf16[2,128,256]{2,1,0:T(8,128)(2,1)S(1)}, u32[]{:S(2)}, u32[]{:S(2)}) %collective-permute-start.25) | collective-permute-done | bytes 131104 | tf_op jit(solution)/shard_map/ppermute | solution.py:579
  77.1 1.7 %finish.3 = (bf16[128,2048]{1,0:T(8,128)(2,1)}, bf16[128,2048]{1,0:T(8,128)(2,1)}, f32[128,2048]{1,0:T(8,128)}, f32[8,128]{1,0:T(8,128)}) custom-call(bf16[2,128,2048]{2,1,0:T(8,128)(2,1)S(1)} %get-tuple-element.76.refs_0_, bf16[2,128,256]{2,1,0:T(8,128)(2,1)S(1)} %collective-permute-done.22.refs_1_, ...), custom_call_target="tpu_custom_call", output_to_operand_aliasing={{0}: (5, {}), {1}: (6, {}), {2}: (7, {})} | custom-call | tf_op jit(solution)/shard_map/finish/pallas_call | solution.py:180
  (44 shorter events, 3.8 us)
Async XLA Ops:
  0.6 15.3 %collective-permute-start.5 = (bf16[128,2048]{1,0:T(8,128)(2,1)}, bf16[128,2048]{1,0:T(8,128)(2,1)S(1)}, u32[]{:S(2)}, u32[]{:S(2)}) collective-permute-start(bf16[128,2048]{1,0:T(8,128)(2,1)} %refs_0_.8), channel_id=1, source_target_pairs={{1,2},{2,1},{0,4},{3,7},{5,6},{6,5},{4,0},{7,3},{9,10},{10,9},{8,1... | collective-permute-start | bytes 1572872 | tf_op jit(solution)/shard_map/ppermute | solution.py:599
  1.1 16.4 %collective-permute-start.7 = (bf16[128,2048]{1,0:T(8,128)(2,1)}, bf16[128,2048]{1,0:T(8,128)(2,1)S(1)}, u32[]{:S(2)}, u32[]{:S(2)}) collective-permute-start(bf16[128,2048]{1,0:T(8,128)(2,1)} %refs_0_.8), channel_id=1, source_target_pairs={{0,1},{1,0},{2,3},{3,2},{4,5},{5,4},{6,7},{7,6},{8,9},{9,8},{10,11... | collective-permute-start | bytes 1572872 | tf_op jit(solution)/shard_map/ppermute | solution.py:596
  7.9 2.0 %collective-permute-start = (bf16[3,4,64,256]{3,2,1,0:T(8,128)(2,1)}, bf16[3,4,64,256]{3,2,1,0:T(8,128)(2,1)S(1)}, u32[]{:S(2)}, u32[]{:S(2)}) collective-permute-start(bf16[3,4,64,256]{3,2,1,0:T(8,128)(2,1)} %get-tuple-element.46), channel_id=1, source_target_pairs={{0,4},{4,0},{8,12},{12,8},{16,20},{20,16},{24,28},{28,24},{1,5},{5... | collective-permute-start | bytes 1179656 | tf_op jit(solution)/shard_map/ppermute | solution.py:579
  7.9 2.5 %collective-permute-start.1 = (bf16[3,4,64,256]{3,2,1,0:T(8,128)(2,1)}, bf16[3,4,64,256]{3,2,1,0:T(8,128)(2,1)S(1)}, u32[]{:S(2)}, u32[]{:S(2)}) collective-permute-start(bf16[3,4,64,256]{3,2,1,0:T(8,128)(2,1)} %get-tuple-element.47), channel_id=1, source_target_pairs={{0,4},{4,0},{8,12},{12,8},{16,20},{20,16},{24,28},{28,24},{1,5},{5... | collective-permute-start | bytes 1179656 | tf_op jit(solution)/shard_map/ppermute | solution.py:579
  10.4 0.7 copy-start.5
  12.4 11.3 %collective-permute-start.2 = (bf16[2,2,128,256]{3,2,1,0:T(8,128)(2,1)S(1)}, bf16[2,2,128,256]{3,2,1,0:T(8,128)(2,1)S(1)}, u32[]{:S(2)}, u32[]{:S(2)}) collective-permute-start(bf16[2,2,128,256]{3,2,1,0:T(8,128)(2,1)S(1)} %get-tuple-element.50), channel_id=1, source_target_pairs={{0,8},{4,12},{8,0},{12,4},{16,24},{20,28},{24,16},{28,20},{1,9},{5... | collective-permute-start | bytes 786440 | tf_op jit(solution)/shard_map/ppermute | solution.py:579
  14.0 13.7 %collective-permute-start.3 = (bf16[2,2,128,256]{3,2,1,0:T(8,128)(2,1)S(1)}, bf16[2,2,128,256]{3,2,1,0:T(8,128)(2,1)S(1)}, u32[]{:S(2)}, u32[]{:S(2)}) collective-permute-start(bf16[2,2,128,256]{3,2,1,0:T(8,128)(2,1)S(1)} %get-tuple-element.51), channel_id=1, source_target_pairs={{0,16},{4,20},{8,24},{12,28},{16,0},{20,4},{24,8},{28,12},{1,17},{... | collective-permute-start | bytes 786440 | tf_op jit(solution)/shard_map/ppermute | solution.py:579
  15.5 12.2 %collective-permute-start.4 = (bf16[2,2,128,256]{3,2,1,0:T(8,128)(2,1)S(1)}, bf16[2,2,128,256]{3,2,1,0:T(8,128)(2,1)S(1)}, u32[]{:S(2)}, u32[]{:S(2)}) collective-permute-start(bf16[2,2,128,256]{3,2,1,0:T(8,128)(2,1)S(1)} %get-tuple-element.52), channel_id=1, source_target_pairs={{0,24},{4,28},{8,16},{12,20},{16,8},{20,12},{24,0},{28,4},{1,25},{... | collective-permute-start | bytes 786440 | tf_op jit(solution)/shard_map/ppermute | solution.py:579
  16.0 13.2 %collective-permute-start.6 = (bf16[128,2048]{1,0:T(8,128)(2,1)S(1)}, bf16[128,2048]{1,0:T(8,128)(2,1)S(1)}, u32[]{:S(2)}, u32[]{:S(2)}) collective-permute-start(bf16[128,2048]{1,0:T(8,128)(2,1)S(1)} %collective-permute-done.5.refs_1_), channel_id=1, source_target_pairs={{0,1},{1,0},{2,3},{3,2},{4,5},{5,4},{6,7},{7,6},{8,9},{9,8},{10,11... | collective-permute-start | bytes 1572872 | tf_op jit(solution)/shard_map/ppermute | solution.py:596
  17.6 11.6 %collective-permute-start.8 = (bf16[128,2048]{1,0:T(8,128)(2,1)S(1)}, bf16[128,2048]{1,0:T(8,128)(2,1)S(1)}, u32[]{:S(2)}, u32[]{:S(2)}) collective-permute-start(bf16[128,2048]{1,0:T(8,128)(2,1)S(1)} %collective-permute-done.7.refs_0_), channel_id=1, source_target_pairs={{1,2},{2,1},{0,4},{3,7},{5,6},{6,5},{4,0},{7,3},{9,10},{10,9},{8,1... | collective-permute-start | bytes 1572872 | tf_op jit(solution)/shard_map/ppermute | solution.py:599
  17.6 6.1 %copy-start.2 = (bf16[128,2048]{1,0:T(8,128)(2,1)S(1)}, bf16[128,2048]{1,0:T(8,128)(2,1)}, u32[]{:S(2)}) copy-start(bf16[128,2048]{1,0:T(8,128)(2,1)} %refs_0_.8) | copy-start | bytes 1572868
  17.6 10.1 %copy-start.3 = (bf16[512,256]{1,0:T(8,128)(2,1)S(1)}, bf16[512,256]{1,0:T(8,128)(2,1)}, u32[]{:S(2)}) copy-start(bf16[512,256]{1,0:T(8,128)(2,1)} %constant.4.clone.refs_0_) | copy-start | bytes 786436
  23.7 7.7 %collective-permute-start.13 = (bf16[128,2048]{1,0:T(8,128)(2,1)S(1)}, bf16[128,2048]{1,0:T(8,128)(2,1)S(1)}, u32[]{:S(2)}, u32[]{:S(2)}) collective-permute-start(bf16[128,2048]{1,0:T(8,128)(2,1)S(1)} %copy-done.2), channel_id=1, source_target_pairs={{0,4},{4,0},{8,12},{12,8},{16,20},{20,16},{24,28},{28,24},{1,5},{5... | collective-permute-start | bytes 1572872 | tf_op jit(solution)/shard_map/ppermute | solution.py:579
  27.7 7.0 %collective-permute-start.12 = (bf16[128,2048]{1,0:T(8,128)(2,1)S(1)}, bf16[128,2048]{1,0:T(8,128)(2,1)S(1)}, u32[]{:S(2)}, u32[]{:S(2)}) collective-permute-start(bf16[128,2048]{1,0:T(8,128)(2,1)S(1)} %collective-permute-done.7.refs_0_), channel_id=1, source_target_pairs={{0,4},{4,0},{8,12},{12,8},{16,20},{20,16},{24,28},{28,24},{1,5},{5... | collective-permute-start | bytes 1572872 | tf_op jit(solution)/shard_map/ppermute | solution.py:579
  29.2 14.4 %collective-permute-start.9 = (bf16[128,2048]{1,0:T(8,128)(2,1)S(1)}, bf16[128,2048]{1,0:T(8,128)(2,1)S(1)}, u32[]{:S(2)}, u32[]{:S(2)}) collective-permute-start(bf16[128,2048]{1,0:T(8,128)(2,1)S(1)} %get-tuple-element.57.refs_1_), channel_id=1, source_target_pairs={{0,1},{1,0},{2,3},{3,2},{4,5},{5,4},{6,7},{7,6},{8,9},{9,8},{10,11... | collective-permute-start | bytes 1572872 | tf_op jit(solution)/shard_map/ppermute | solution.py:596
  31.4 12.2 %collective-permute-start.15 = (bf16[128,2048]{1,0:T(8,128)(2,1)S(1)}, bf16[128,2048]{1,0:T(8,128)(2,1)S(1)}, u32[]{:S(2)}, u32[]{:S(2)}) collective-permute-start(bf16[128,2048]{1,0:T(8,128)(2,1)S(1)} %collective-permute-done.5.refs_1_), channel_id=1, source_target_pairs={{0,4},{4,0},{8,12},{12,8},{16,20},{20,16},{24,28},{28,24},{1,5},{5... | collective-permute-start | bytes 1572872 | tf_op jit(solution)/shard_map/ppermute | solution.py:579
  38.0 5.6 %collective-permute-start.14 = (bf16[128,2048]{1,0:T(8,128)(2,1)S(1)}, bf16[128,2048]{1,0:T(8,128)(2,1)S(1)}, u32[]{:S(2)}, u32[]{:S(2)}) collective-permute-start(bf16[128,2048]{1,0:T(8,128)(2,1)S(1)} %get-tuple-element.63.refs_0_), channel_id=1, source_target_pairs={{0,4},{4,0},{8,12},{12,8},{16,20},{20,16},{24,28},{28,24},{1,5},{5... | collective-permute-start | bytes 1572872 | tf_op jit(solution)/shard_map/ppermute | solution.py:579
  38.6 8.5 %collective-permute-start.11 = (bf16[128,2048]{1,0:T(8,128)(2,1)S(1)}, bf16[128,2048]{1,0:T(8,128)(2,1)S(1)}, u32[]{:S(2)}, u32[]{:S(2)}) collective-permute-start(bf16[128,2048]{1,0:T(8,128)(2,1)S(1)} %get-tuple-element.57.refs_1_), channel_id=1, source_target_pairs={{0,4},{4,0},{8,12},{12,8},{16,20},{20,16},{24,28},{28,24},{1,5},{5... | collective-permute-start | bytes 1572872 | tf_op jit(solution)/shard_map/ppermute | solution.py:579
  43.6 3.5 %collective-permute-start.10 = (bf16[128,2048]{1,0:T(8,128)(2,1)S(1)}, bf16[128,2048]{1,0:T(8,128)(2,1)S(1)}, u32[]{:S(2)}, u32[]{:S(2)}) collective-permute-start(bf16[128,2048]{1,0:T(8,128)(2,1)S(1)} %collective-permute-done.9.refs_0_), channel_id=1, source_target_pairs={{0,4},{4,0},{8,12},{12,8},{16,20},{20,16},{24,28},{28,24},{1,5},{5... | collective-permute-start | bytes 1572872 | tf_op jit(solution)/shard_map/ppermute | solution.py:579
  43.6 16.1 %copy-start.4 = (bf16[256,512]{1,0:T(8,128)(2,1)S(1)}, bf16[256,512]{1,0:T(8,128)(2,1)}, u32[]{:S(2)}) copy-start(bf16[256,512]{1,0:T(8,128)(2,1)} %constant.5.clone.refs_1_) | copy-start | bytes 786436
  47.1 22.8 %copy-start = (bf16[128,2048]{1,0:T(8,128)(2,1)S(1)}, bf16[128,2048]{1,0:T(8,128)(2,1)}, u32[]{:S(2)}) copy-start(bf16[128,2048]{1,0:T(8,128)(2,1)} %refs_0_.9) | copy-start | bytes 1572868
  47.1 22.8 %copy-start.1 = (bf16[128,2048]{1,0:T(8,128)(2,1)S(1)}, bf16[128,2048]{1,0:T(8,128)(2,1)}, u32[]{:S(2)}) copy-start(bf16[128,2048]{1,0:T(8,128)(2,1)} %refs_1_.4) | copy-start | bytes 1572868
  49.9 7.3 %collective-permute-start.16 = (bf16[2,128,256]{2,1,0:T(8,128)(2,1)S(1)}, bf16[2,128,256]{2,1,0:T(8,128)(2,1)S(1)}, u32[]{:S(2)}, u32[]{:S(2)}) collective-permute-start(bf16[2,128,256]{2,1,0:T(8,128)(2,1)S(1)} %get-tuple-element.69), channel_id=1, source_target_pairs={{0,24},{4,28},{8,16},{12,20},{16,8},{20,12},{24,0},{28,4},{1,25},{... | collective-permute-start | bytes 393224 | tf_op jit(solution)/shard_map/ppermute | solution.py:579
  51.5 8.1 %collective-permute-start.17 = (bf16[2,128,256]{2,1,0:T(8,128)(2,1)S(1)}, bf16[2,128,256]{2,1,0:T(8,128)(2,1)S(1)}, u32[]{:S(2)}, u32[]{:S(2)}) collective-permute-start(bf16[2,128,256]{2,1,0:T(8,128)(2,1)S(1)} %get-tuple-element.70), channel_id=1, source_target_pairs={{0,16},{4,20},{8,24},{12,28},{16,0},{20,4},{24,8},{28,12},{1,17},{... | collective-permute-start | bytes 393224 | tf_op jit(solution)/shard_map/ppermute | solution.py:579
  51.6 8.1 %collective-permute-start.18 = (bf16[2,128,256]{2,1,0:T(8,128)(2,1)S(1)}, bf16[2,128,256]{2,1,0:T(8,128)(2,1)S(1)}, u32[]{:S(2)}, u32[]{:S(2)}) collective-permute-start(bf16[2,128,256]{2,1,0:T(8,128)(2,1)S(1)} %get-tuple-element.71), channel_id=1, source_target_pairs={{0,8},{4,12},{8,0},{12,4},{16,24},{20,28},{24,16},{28,20},{1,9},{5... | collective-permute-start | bytes 393224 | tf_op jit(solution)/shard_map/ppermute | solution.py:579
  63.0 3.8 %collective-permute-start.19 = (bf16[2,128,256]{2,1,0:T(8,128)(2,1)S(1)}, bf16[2,128,256]{2,1,0:T(8,128)(2,1)S(1)}, u32[]{:S(2)}, u32[]{:S(2)}) collective-permute-start(bf16[2,128,256]{2,1,0:T(8,128)(2,1)S(1)} %get-tuple-element.73), channel_id=1, source_target_pairs={{0,4},{4,0},{8,12},{12,8},{16,20},{20,16},{24,28},{28,24},{1,5},{5... | collective-permute-start | bytes 393224 | tf_op jit(solution)/shard_map/ppermute | solution.py:579
  63.0 6.3 %collective-permute-start.20 = (bf16[2,128,256]{2,1,0:T(8,128)(2,1)S(1)}, bf16[2,128,256]{2,1,0:T(8,128)(2,1)S(1)}, u32[]{:S(2)}, u32[]{:S(2)}) collective-permute-start(bf16[2,128,256]{2,1,0:T(8,128)(2,1)S(1)} %get-tuple-element.74), channel_id=1, source_target_pairs={{0,8},{4,12},{8,0},{12,4},{16,24},{20,28},{24,16},{28,20},{1,9},{5... | collective-permute-start | bytes 393224 | tf_op jit(solution)/shard_map/ppermute | solution.py:579
  63.5 6.3 %collective-permute-start.21 = (bf16[2,128,256]{2,1,0:T(8,128)(2,1)S(1)}, bf16[2,128,256]{2,1,0:T(8,128)(2,1)S(1)}, u32[]{:S(2)}, u32[]{:S(2)}) collective-permute-start(bf16[2,128,256]{2,1,0:T(8,128)(2,1)S(1)} %get-tuple-element.75), channel_id=1, source_target_pairs={{0,16},{4,20},{8,24},{12,28},{16,0},{20,4},{24,8},{28,12},{1,17},{... | collective-permute-start | bytes 393224 | tf_op jit(solution)/shard_map/ppermute | solution.py:579
  65.0 6.7 %collective-permute-start.22 = (bf16[2,128,256]{2,1,0:T(8,128)(2,1)S(1)}, bf16[2,128,256]{2,1,0:T(8,128)(2,1)S(1)}, u32[]{:S(2)}, u32[]{:S(2)}) collective-permute-start(bf16[2,128,256]{2,1,0:T(8,128)(2,1)S(1)} %get-tuple-element.77), channel_id=1, source_target_pairs={{0,12},{4,8},{8,4},{12,0},{16,28},{20,24},{24,20},{28,16},{1,13},{... | collective-permute-start | bytes 393224 | tf_op jit(solution)/shard_map/ppermute | solution.py:579
  65.2 6.5 %collective-permute-start.23 = (bf16[2,128,256]{2,1,0:T(8,128)(2,1)S(1)}, bf16[2,128,256]{2,1,0:T(8,128)(2,1)S(1)}, u32[]{:S(2)}, u32[]{:S(2)}) collective-permute-start(bf16[2,128,256]{2,1,0:T(8,128)(2,1)S(1)} %get-tuple-element.78), channel_id=1, source_target_pairs={{0,20},{4,16},{8,28},{12,24},{16,4},{20,0},{24,12},{28,8},{1,21},{... | collective-permute-start | bytes 393224 | tf_op jit(solution)/shard_map/ppermute | solution.py:579
  66.8 8.3 %collective-permute-start.24 = (bf16[2,128,256]{2,1,0:T(8,128)(2,1)S(1)}, bf16[2,128,256]{2,1,0:T(8,128)(2,1)S(1)}, u32[]{:S(2)}, u32[]{:S(2)}) collective-permute-start(bf16[2,128,256]{2,1,0:T(8,128)(2,1)S(1)} %get-tuple-element.79), channel_id=1, source_target_pairs={{0,24},{4,28},{8,16},{12,20},{16,8},{20,12},{24,0},{28,4},{1,25},{... | collective-permute-start | bytes 393224 | tf_op jit(solution)/shard_map/ppermute | solution.py:579
  69.3 7.8 %collective-permute-start.25 = (bf16[2,128,256]{2,1,0:T(8,128)(2,1)S(1)}, bf16[2,128,256]{2,1,0:T(8,128)(2,1)S(1)}, u32[]{:S(2)}, u32[]{:S(2)}) collective-permute-start(bf16[2,128,256]{2,1,0:T(8,128)(2,1)S(1)} %get-tuple-element.80), channel_id=1, source_target_pairs={{0,28},{4,24},{8,20},{12,16},{16,12},{20,8},{24,4},{28,0},{1,29},{... | collective-permute-start | bytes 393224 | tf_op jit(solution)/shard_map/ppermute | solution.py:579
